TPU v7x, 128 devices: a whole 4x4x4 slice. The times are simulated.
128 devices in a mesh: azim: 16 (over x, y_hi, core), axial: 8 (over z, y_lo).
Axes of the slice: x: 4, y: 4 (y_hi: 2, y_lo: 2; y = y_hi * 2 + y_lo), z: 4, core: 2. Of those that a mesh axis runs over, the one named last changes fastest.
Arguments:
- populations: float32 [19, 128, 128, 256], P(None, 'azim', 'axial'), may hold values from 0.03 to 0.09
- fluid_flags: int32 [128, 128, 256], P('azim', 'axial'), may hold values 0 or 1
- wall_cell: int32 [65536], P(('azim', 'axial')), may hold values from 0 to 32767
- wall_drive: float32 [65536], P(('azim', 'axial')), may hold values from -6 to 6
- wall_owner: int32 [65536], P(('azim', 'axial')), may hold values from 0 to 127, as said below
- wall_slot: int32 [65536], P(('azim', 'axial')), may hold values from 0 to 7
- receive_cell: int32 [131072], P(('azim', 'axial')), may hold values from 0 to 65536, as said below
- materials: int32 [256, 128, 256], P('azim', 'axial'), may hold values from 0 to 3
- solid_temp: float32 [256, 128, 256], P('azim', 'axial'), may hold values from -6 to 6
Outputs:
- fluid_out: float32 [19, 128, 128, 256], P(None, 'azim', 'axial')
- solid_out: float32 [256, 128, 256], P('azim', 'axial')
Inputs may be any that keep to these rules, and one draw needn't show every extreme that they name: `wall_cell`: index into the sending device's own fluid block, flattened with azimuth slowest and radius fastest. `wall_owner`: device index azim index * 8 + axial index. Rows of one device never share an (owner, slot) pair; some owner receives all 8 slots from every device. `receive_cell`: ordered by owner, then sender, then slot; equals 65536 exactly where the sender has no row for that owner and slot.
All inputs are finite; a program needn't handle non-finite values. No bound on the sum of `fluid_flags` on one device may be relied on, other than what follows from the above.
Results may differ from a plain program's by a relative error of at most 0.0003.
Values sent between devices are 32-bit elements; how exact they have to be, the bound alone decides.
No kernel may reach another device: no remote copies, remote signals or barrier semaphores. Data moves between devices by JAX's collectives and lax.ppermute only.
A program may use at most 128 MiB of HBM per device.

v0:
```python
import functools
import itertools

import jax
import jax.numpy as jnp
from jax import lax
from jax.experimental import pallas as pl
from jax.experimental.pallas import tpu as pltpu
from jax.sharding import PartitionSpec as P

CAP = 8
STEP_A = [0, 1, -1, 0, 0, 0, 0, 1, -1, 1, -1, 1, -1, 1, -1, 0, 0, 0, 0]
STEP_Z = [0, 0, 0, 1, -1, 0, 0, 1, -1, -1, 1, 0, 0, 0, 0, 1, -1, 1, -1]
STEP_R = [0, 0, 0, 0, 0, 1, -1, 0, 0, 0, 0, 1, -1, -1, 1, 1, -1, -1, 1]
OPPOSITE = [0, 2, 1, 4, 3, 6, 5, 8, 7, 10, 9, 12, 11, 14, 13, 16, 15, 18, 17]
AZIM_UP = [i for i in range(19) if STEP_A[i] == 1]
AZIM_DOWN = [i for i in range(19) if STEP_A[i] == -1]
AXIAL_UP = [i for i in range(19) if STEP_Z[i] == 1]
AXIAL_DOWN = [i for i in range(19) if STEP_Z[i] == -1]
RELAXATION = 1.25
SPEED_REF = 0.05
HEAT_CAPACITY = 6.5

Q = 19
CA, CZ, NR = 8, 16, 256
SA, SZ = 16, 16
HALVES = (0, 1)
ROWS = 32

FLAG_PLANE = 24
TEMP_PLANE = 26
COND_PLANE = 29
CELL_ROW = 512
AZIM_ROWS = 520
PER_PLACE = 26
TEMP_ROW = 312
COND_ROW = 378
TAIL_ROW = 448
AXIAL_ROWS = 464

VMEM = pltpu.VMEM
f32 = jnp.float32
bf16 = jnp.bfloat16


def lanes(half):
    return pl.ds(128 * half, 128)


def moments(f):
    rho = f[0]
    for i in range(1, Q):
        rho = rho + f[i]
    d = [f[i] - f[i + 1] for i in range(1, Q, 2)]
    mom_a = d[0] + d[3] + d[4] + d[5] + d[6]
    mom_z = d[1] + d[3] - d[4] + d[7] + d[8]
    mom_r = d[2] + d[5] - d[6] + d[7] - d[8]
    return rho, mom_a, mom_z, mom_r


def collide(f, flag):
    rho, mom_a, mom_z, mom_r = moments(f)
    open_cell = flag > 0
    inv = 1.0 / jnp.where(open_cell, rho, 1.0)
    omega = jnp.where(open_cell, RELAXATION, 0.0)
    keep = 1.0 - omega
    ua, uz, ur = mom_a * inv, mom_z * inv, mom_r * inv
    base = 1.0 - 1.5 * (ua * ua + uz * uz + ur * ur)
    scale = omega * rho
    face, edge = scale * (1.0 / 18.0), scale * (1.0 / 36.0)
    post = [keep * f[0] + scale * (1.0 / 3.0) * base]
    for n, proj in enumerate(
        (ua, uz, ur, ua + uz, ua - uz, ua + ur, ua - ur, uz + ur, uz - ur)
    ):
        weight = face if n < 3 else edge
        even = weight * (base + 4.5 * proj * proj)
        odd = weight * (3.0 * proj)
        post.append(keep * f[2 * n + 1] + (even + odd))
        post.append(keep * f[2 * n + 2] + (even - odd))
    return post


def conductivity(material):
    return jnp.where(
        material == 0,
        1.0,
        jnp.where(material == 1, 0.55, jnp.where(material == 2, 0.2, 0.8)),
    ).astype(f32)


def by_parity(axis, body, near, far):
    odd = lax.rem(lax.axis_index(axis), 2) == 1

    @pl.when(odd)
    def _():
        body(near, far)

    @pl.when(jnp.logical_not(odd))
    def _():
        body(far, near)


def first_kernel(f, flags, temp, mat, cells, post, near, far, low, high):
    def layer(a, carry):
        for half in HALVES:
            for part in (0, 1):
                rows = pl.ds(8 * part, 8)
                flag = flags[a, rows, lanes(half)].astype(f32)
                out = collide([f[i, a, rows, lanes(half)] for i in range(Q)], flag)
                for i in range(Q):
                    post[i, a, rows, lanes(half)] = out[i]
                place = (a + 2) * PER_PLACE
                target, inner, edge, near_edge = (
                    (low, AXIAL_DOWN, 0, 1) if part == 0 else (high, AXIAL_UP, 7, 6)
                )
                for i in range(Q):
                    target[half, pl.ds(place + i, 1), :] = out[i][edge : edge + 1]
                for n, i in enumerate(inner):
                    target[half, pl.ds(place + Q + n, 1), :] = out[i][
                        near_edge : near_edge + 1
                    ]
                target[half, pl.ds(place + 24, 1), :] = flag[edge : edge + 1]
                target[half, pl.ds(place + 25, 1), :] = flag[
                    near_edge : near_edge + 1
                ]
        return carry

    lax.fori_loop(0, CA, layer, 0)

    def solid_layer(a, carry):
        for half in HALVES:
            for part, target in ((0, low), (1, high)):
                rows = pl.ds(8 * part, 8)
                t = temp[a, rows, lanes(half)]
                c = conductivity(mat[a, rows, lanes(half)])
                for depth in range(3):
                    at = depth if part == 0 else 7 - depth
                    target[half, pl.ds(TEMP_ROW + depth * 22 + 3 + a, 1), :] = t[
                        at : at + 1
                    ]
                    target[half, pl.ds(COND_ROW + depth * 22 + 3 + a, 1), :] = c[
                        at : at + 1
                    ]
        return carry

    lax.fori_loop(0, SA, solid_layer, 0)
    rc = cells[...].astype(f32)
    low[0, pl.ds(TAIL_ROW, 8), :] = rc
    high[0, pl.ds(TAIL_ROW, 8), :] = rc

    def fill(down, up):
        for target, outer, second, moving, solid in (
            (down, 0, 1, AZIM_DOWN, (0, 1, 2)),
            (up, 7, 6, AZIM_UP, (15, 14, 13)),
        ):
            for half in HALVES:
                for i in range(Q):
                    target[half, pl.ds(16 * i, 16), :] = post[i, outer, :, lanes(half)]
                for n, i in enumerate(moving):
                    target[half, pl.ds(16 * (Q + n), 16), :] = post[
                        i, second, :, lanes(half)
                    ]
                for n, a in enumerate((outer, second)):
                    target[half, pl.ds(16 * (FLAG_PLANE + n), 16), :] = flags[
                        a, :, lanes(half)
                    ].astype(f32)
                for depth, a in enumerate(solid):
                    target[half, pl.ds(16 * (TEMP_PLANE + depth), 16), :] = temp[
                        a, :, lanes(half)
                    ]
                    target[half, pl.ds(16 * (COND_PLANE + depth), 16), :] = (
                        conductivity(mat[a, :, lanes(half)])
                    )
            target[0, pl.ds(CELL_ROW, 8), :] = rc

    by_parity("azim", fill, near, far)


def axial_kernel(near_in, far_in, low_in, high_in, near, far):
    def pass_on(lower, upper):
        def fill(down, up):
            down[...] = low_in[...]
            up[...] = high_in[...]
            for half, (target, edge, near_edge, inner, solid) in itertools.product(
                HALVES,
                (
                    (down, 0, 1, AXIAL_DOWN, (0, 1, 2)),
                    (up, 15, 14, AXIAL_UP, (15, 14, 13)),
                ),
            ):
                for source, moving, first, second, layers in (
                    (lower, AZIM_UP, -1, -2, (-1, -2, -3)),
                    (upper, AZIM_DOWN, 8, 9, (16, 17, 18)),
                ):

                    def put(row, plane, z):
                        target[half, pl.ds(row, 1), :] = source[
                            half, pl.ds(16 * plane + z, 1), :
                        ]

                    place = (first + 2) * PER_PLACE
                    for i in range(Q):
                        put(place + i, i, edge)
                    for n, i in enumerate(inner):
                        put(place + Q + n, i, near_edge)
                    put(place + 24, FLAG_PLANE, edge)
                    put(place + 25, FLAG_PLANE, near_edge)
                    place = (second + 2) * PER_PLACE
                    for n, i in enumerate(moving):
                        put(place + i, Q + n, edge)
                        if i in inner:
                            put(place + Q + inner.index(i), Q + n, near_edge)
                    put(place + 24, FLAG_PLANE + 1, edge)
                    put(place + 25, FLAG_PLANE + 1, near_edge)
                    for n, a in enumerate(layers):
                        for depth, z in enumerate(solid):
                            put(TEMP_ROW + depth * 22 + 3 + a, TEMP_PLANE + n, z)
                            put(COND_ROW + depth * 22 + 3 + a, COND_PLANE + n, z)
            for target in (down, up):
                target[1, pl.ds(TAIL_ROW, 8), :] = lower[0, pl.ds(CELL_ROW, 8), :]
                target[0, pl.ds(TAIL_ROW + 8, 8), :] = upper[0, pl.ds(CELL_ROW, 8), :]

        by_parity("axial", fill, near, far)

    by_parity("azim", pass_on, near_in, far_in)


def ends(n_axial):
    z = lax.axis_index("axial")
    return (
        jnp.where(z > 0, 1.0, 0.0).astype(f32),
        jnp.where(z < n_axial - 1, 1.0, 0.0).astype(f32),
    )


def shifted(pair, step, lane):
    if step == 0:
        return pair
    turn = 1 if step == 1 else 127
    at = 0 if step == 1 else 127
    a, b = (pltpu.roll(x, turn, 1) for x in pair)
    return [jnp.where(lane == at, b, a), jnp.where(lane == at, a, b)]


def split3(x):
    one = x.astype(bf16)
    rest = x - one.astype(f32)
    two = rest.astype(bf16)
    return one, two, (rest - two.astype(f32)).astype(bf16)


def stream(source, opened, at_a, flag_a, row, lane):
    rows = pl.ds(row, 8)
    out = [[], []]
    for i in range(Q):
        own = OPPOSITE[i]
        moved = shifted(
            [
                source[i, at_a - STEP_A[i], half, pl.ds(row - STEP_Z[i], 8), :]
                for half in HALVES
            ],
            STEP_R[i],
            lane,
        )
        for half in HALVES:
            if i == 0:
                out[half].append(moved[half])
                continue
            mask = opened[
                STEP_R[i] % 3,
                flag_a - STEP_A[i],
                half,
                pl.ds(row - STEP_Z[i], 8),
                :,
            ]
            out[half].append(
                jnp.where(mask > 0, moved[half], source[own, at_a, half, rows, :])
            )
    return out


def fluid_kernel(
    n_azim,
    n_axial,
    post,
    flags,
    near_a,
    far_a,
    near_z,
    far_z,
    cell,
    drive,
    owner,
    slot,
    fluid_out,
    message,
    ext,
    opened,
    second,
    speeds,
):
    lane = lax.broadcasted_iota(jnp.int32, (8, 128), 1)

    def own_layer(a, carry):
        for half in HALVES:
            for part in (0, 1):
                rows = pl.ds(8 * part, 8)
                to = pl.ds(8 + 8 * part, 8)
                for i in range(Q):
                    ext[i, a + 2, half, to, :] = post[i, a, rows, lanes(half)]
                opened[0, a + 2, half, to, :] = flags[a, rows, lanes(half)].astype(f32)
        return carry

    lax.fori_loop(0, CA, own_layer, 0)

    def azim_rim(lower, upper):
        for half in HALVES:
            for source, first, last, moving in (
                (lower, 1, 0, AZIM_UP),
                (upper, 10, 11, AZIM_DOWN),
            ):
                to = pl.ds(8, 16)
                for i in range(Q):
                    ext[i, first, half, to, :] = source[half, pl.ds(16 * i, 16), :]
                for n, i in enumerate(moving):
                    ext[i, last, half, to, :] = source[half, pl.ds(16 * (Q + n), 16), :]
                opened[0, first, half, to, :] = source[half, pl.ds(16 * FLAG_PLANE, 16), :]
                opened[0, last, half, to, :] = source[half, pl.ds(16 * (FLAG_PLANE + 1), 16), :]

    by_parity("azim", azim_rim, near_a, far_a)
    below, above = ends(n_axial)

    def axial_rim(lower, upper):
        def layer(a, carry):
            place = a * PER_PLACE
            for half in HALVES:
                for source, first, last, moving, there in (
                    (lower, 7, 6, AXIAL_UP, below),
                    (upper, 24, 25, AXIAL_DOWN, above),
                ):
                    for i in range(Q):
                        ext[i, a, half, pl.ds(first, 1), :] = source[half, pl.ds(place + i, 1), :]
                    for n, i in enumerate(moving):
                        ext[i, a, half, pl.ds(last, 1), :] = source[half, pl.ds(place + Q + n, 1), :]
                    opened[0, a, half, pl.ds(first, 1), :] = (
                        source[half, pl.ds(place + 24, 1), :] * there
                    )
                    opened[0, a, half, pl.ds(last, 1), :] = (
                        source[half, pl.ds(place + 25, 1), :] * there
                    )
            return carry

        lax.fori_loop(0, CA + 4, layer, 0)

    by_parity("axial", axial_rim, near_z, far_z)

    def turn(a, carry):
        for part in range(4):
            rows = pl.ds(8 * part, 8)
            pair = [opened[0, a, half, rows, :] for half in HALVES]
            up = shifted(pair, 1, lane)
            down = shifted(pair, -1, lane)
            opened[1, a, 0, rows, :] = jnp.where(lane == 0, 0.0, up[0])
            opened[1, a, 1, rows, :] = up[1]
            opened[2, a, 0, rows, :] = down[0]
            opened[2, a, 1, rows, :] = jnp.where(lane == 127, 0.0, down[1])
        return carry

    lax.fori_loop(0, CA + 4, turn, 0)

    def first_step(a, carry):
        for row in (7, 15, 23):
            moved = stream(ext, opened, a + 1, a + 1, row, lane)
            for half in HALVES:
                out = collide(moved[half], opened[0, a + 1, half, pl.ds(row, 8), :])
                for i in range(Q):
                    second[i, a, half, pl.ds(row, 8), :] = out[i]
        return carry

    lax.fori_loop(0, CA + 2, first_step, 0)

    def second_step(a, carry):
        for part in (0, 1):
            moved = stream(second, opened, a + 1, a + 2, 8 + 8 * part, lane)
            for half in HALVES:
                for i in range(Q):
                    fluid_out[i, a, pl.ds(8 * part, 8), lanes(half)] = moved[half][i]
                rho, mom_a, mom_z, mom_r = moments(moved[half])
                inv = 1.0 / rho
                ua, uz, ur = mom_a * inv, mom_z * inv, mom_r * inv
                speeds[pl.ds(a * CZ + 8 * part, 8), lanes(half)] = jnp.sqrt(
                    ua * ua + uz * uz + ur * ur + 1e-06
                )
        return carry

    lax.fori_loop(0, CA, second_step, 0)

    rows_here = cell.shape[1]
    place = cell[...]
    row_hot = (
        lax.broadcasted_iota(jnp.int32, (CA * CZ, rows_here), 0) == place // NR
    ).astype(f32).astype(bf16)
    turned = jnp.transpose(speeds[...])
    picked = jnp.zeros((NR, rows_here), f32)
    for term in split3(turned):
        picked = picked + jnp.dot(term, row_hot, preferred_element_type=f32)
    column = lax.broadcasted_iota(jnp.int32, (NR, rows_here), 0) == place % NR
    speed = jnp.sum(jnp.where(column, picked, 0.0), axis=0, keepdims=True)
    flux = drive[...] * (0.2 + speed / SPEED_REF)
    devices = n_azim * n_axial
    owner_hot = (
        lax.broadcasted_iota(jnp.int32, (devices, rows_here), 0) == owner[...]
    ).astype(f32).astype(bf16)
    slotted = jnp.where(
        lax.broadcasted_iota(jnp.int32, (128, rows_here), 0) == slot[...], flux, 0.0
    )
    sent = jnp.zeros((devices, 128), f32)
    for term in split3(slotted):
        sent = sent + lax.dot_general(
            owner_hot, term, (((1,), (1,)), ((), ())), preferred_element_type=f32
        )
    total = jnp.zeros((devices, 128), f32)
    for da in (-1, 0, 1):
        for dz in (-1, 0, 1):
            which = (da + 1) * 3 + dz + 1
            back = (-(da * n_axial + dz)) % devices
            moved = pltpu.roll(sent, back, 0) if back else sent
            total = total + (pltpu.roll(moved, CAP * which, 1) if which else moved)
    for o in range(devices):
        message[o, :, :] = total[o : o + 1]


def link(first, second):
    joined = first + second
    good = joined > 0
    return jnp.where(
        good,
        (2.0 / HEAT_CAPACITY) * first * second / jnp.where(good, joined, 1.0),
        0.0,
    )


def sweep(source, link_a, link_z, link_r, keep, a, row, lane):
    rows = pl.ds(row, 8)
    pair = [source[a, half, rows, :] for half in HALVES]
    lr = [link_r[a, half, rows, :] for half in HALVES]
    up = shifted(pair, -1, lane)
    down = shifted([x * y for x, y in zip(pair, lr)], 1, lane)
    out = []
    for half in HALVES:
        total = keep[a, half, rows, :] * pair[half]
        total = total + link_a[a, half, rows, :] * source[a + 1, half, rows, :]
        total = total + link_a[a - 1, half, rows, :] * source[a - 1, half, rows, :]
        total = (
            total + link_z[a, half, rows, :] * source[a, half, pl.ds(row + 1, 8), :]
        )
        total = (
            total
            + link_z[a, half, pl.ds(row - 1, 8), :]
            * source[a, half, pl.ds(row - 1, 8), :]
        )
        out.append(total + lr[half] * up[half] + down[half])
    return out


def solid_kernel(
    n_axial,
    temp,
    mat,
    near_a,
    far_a,
    near_z,
    far_z,
    swept,
    link_a,
    link_z,
    link_r,
    keep,
    ext,
    cond,
    other,
):
    lane = lax.broadcasted_iota(jnp.int32, (8, 128), 1)

    def own_layer(a, carry):
        for half in HALVES:
            for part in (0, 1):
                rows = pl.ds(8 * part, 8)
                to = pl.ds(8 + 8 * part, 8)
                ext[a + 3, half, to, :] = temp[a, rows, lanes(half)]
                cond[a + 3, half, to, :] = conductivity(mat[a, rows, lanes(half)])
        return carry

    lax.fori_loop(0, SA, own_layer, 0)

    def azim_rim(lower, upper):
        for half in HALVES:
            for depth in range(3):
                for source, a in ((lower, 2 - depth), (upper, 19 + depth)):
                    ext[a, half, pl.ds(8, 16), :] = source[half, pl.ds(16 * (TEMP_PLANE + depth), 16), :]
                    cond[a, half, pl.ds(8, 16), :] = source[half, pl.ds(16 * (COND_PLANE + depth), 16), :]

    by_parity("azim", azim_rim, near_a, far_a)
    below, above = ends(n_axial)

    def axial_rim(lower, upper):
        def layer(a, carry):
            for half in HALVES:
                for depth in range(3):
                    for source, row, there in (
                        (lower, 7 - depth, below),
                        (upper, 24 + depth, above),
                    ):
                        ext[a, half, pl.ds(row, 1), :] = source[half, pl.ds(TEMP_ROW + depth * 22 + a, 1), :]
                        cond[a, half, pl.ds(row, 1), :] = (
                            source[half, pl.ds(COND_ROW + depth * 22 + a, 1), :]
                            * there
                        )
            return carry

        lax.fori_loop(0, SA + 6, layer, 0)

    by_parity("axial", axial_rim, near_z, far_z)

    def links(a, carry):
        for row in (5, 13, 21):
            rows = pl.ds(row, 8)
            pair = [cond[a, half, rows, :] for half in HALVES]
            up = shifted(pair, -1, lane)
            up = [up[0], jnp.where(lane == 127, 0.0, up[1])]
            for half in HALVES:
                link_a[a, half, rows, :] = link(pair[half], cond[a + 1, half, rows, :])
                link_z[a, half, rows, :] = link(
                    pair[half], cond[a, half, pl.ds(row + 1, 8), :]
                )
                link_r[a, half, rows, :] = link(pair[half], up[half])
        return carry

    lax.fori_loop(0, SA + 5, links, 0)

    def keeps(a, carry):
        for row in (6, 14, 22):
            rows = pl.ds(row, 8)
            pair = [link_r[a, half, rows, :] for half in HALVES]
            down = shifted(pair, 1, lane)
            for half in HALVES:
                keep[a, half, rows, :] = 1.0 - (
                    link_a[a, half, rows, :]
                    + link_a[a - 1, half, rows, :]
                    + link_z[a, half, rows, :]
                    + link_z[a, half, pl.ds(row - 1, 8), :]
                    + pair[half]
                    + down[half]
                )
        return carry

    lax.fori_loop(1, SA + 5, keeps, 0)

    def once(source, target, first, last, at):
        def layer(a, carry):
            for row in at:
                out = sweep(source, link_a, link_z, link_r, keep, a, row, lane)
                for half in HALVES:
                    target[a, half, pl.ds(row, 8), :] = out[half]
            return carry

        lax.fori_loop(first, last, layer, 0)

    once(ext, other, 1, SA + 5, (6, 14, 22))
    once(other, ext, 2, SA + 4, (7, 15, 23))

    def final(a, carry):
        for part in (0, 1):
            out = sweep(ext, link_a, link_z, link_r, keep, a + 3, 8 + 8 * part, lane)
            for half in HALVES:
                swept[a, pl.ds(8 * part, 8), lanes(half)] = out[half]
        return carry

    lax.fori_loop(0, SA, final, 0)


def deposit_kernel(
    n_axial,
    arrived,
    cells,
    near_a,
    far_a,
    near_z,
    far_z,
    swept,
    link_a,
    link_z,
    link_r,
    keep,
    solid_out,
    heat,
    other,
    rim_cells,
    came,
):
    lane = lax.broadcasted_iota(jnp.int32, (8, 128), 1)
    senders = arrived.shape[0]
    for s in range(senders):
        came[pl.ds(s, 1), :] = arrived[s]

    def clear(a, carry):
        for half in HALVES:
            heat[a, half] = jnp.zeros((ROWS, 128), f32)
        return carry

    lax.fori_loop(0, SA + 6, clear, 0)

    rim_cells[4] = cells[...]

    def azim_cells(lower, upper):
        rim_cells[1] = lower[0, pl.ds(CELL_ROW, 8), :].astype(jnp.int32)
        rim_cells[7] = upper[0, pl.ds(CELL_ROW, 8), :].astype(jnp.int32)

    by_parity("azim", azim_cells, near_a, far_a)
    below, above = ends(n_axial)

    def axial_cells(lower, upper):
        for source, dz, there in ((lower, 0, below), (upper, 2, above)):
            for which, row, half in (
                (3, TAIL_ROW, 0),
                (0, TAIL_ROW, 1),
                (6, TAIL_ROW + 8, 0),
            ):
                got = source[half, pl.ds(row, 8), :].astype(jnp.int32)
                rim_cells[which + dz] = jnp.where(there > 0, got, SA * SZ * NR)

    by_parity("axial", axial_cells, near_z, far_z)

    values = jnp.transpose(came[...]) * (1.0 / HEAT_CAPACITY)

    def place(which, rows, row_of):
        cell = rim_cells[which]
        value = values[CAP * which : CAP * (which + 1)]
        one, two, three = split3(value)
        at_row = row_of(lax.broadcasted_iota(jnp.int32, (rows, senders), 0))
        at_col = lax.broadcasted_iota(jnp.int32, (NR, senders), 0)
        left, right = [[], [], []], []
        for c in range(CAP):
            hit = at_row == (cell[c : c + 1] // NR)
            for to, term in zip(left, (one, two, three)):
                to.append(
                    jnp.where(hit, term[c : c + 1].astype(f32), 0.0).astype(bf16)
                )
            right.append((at_col == cell[c : c + 1] % NR).astype(f32).astype(bf16))
        right = jnp.concatenate(right, axis=1)
        total = None
        for to in left:
            part = lax.dot_general(
                jnp.concatenate(to, axis=1),
                right,
                (((1,), (1,)), ((), ())),
                preferred_element_type=f32,
            )
            total = part if total is None else total + part
        return total

    own = place(4, SA * SZ, lambda j: j)
    for a in range(SA):
        for half in HALVES:
            heat[a + 3, half, pl.ds(8, 16), :] = own[
                16 * a : 16 * a + 16, 128 * half : 128 * half + 128
            ]
    low = place(1, 32, lambda j: j + 14 * SZ)
    high = place(7, 32, lambda j: j)
    for n in range(2):
        for half in HALVES:
            cut = slice(128 * half, 128 * half + 128)
            heat[1 + n, half, pl.ds(8, 16), :] = low[16 * n : 16 * n + 16, cut]
            heat[19 + n, half, pl.ds(8, 16), :] = high[16 * n : 16 * n + 16, cut]
    low = place(3, 32, lambda j: (j // 2) * SZ + 14 + j % 2)
    high = place(5, 32, lambda j: (j // 2) * SZ + j % 2)
    for a in range(SA):
        for half in HALVES:
            cut = slice(128 * half, 128 * half + 128)
            heat[a + 3, half, pl.ds(6, 2), :] = low[2 * a : 2 * a + 2, cut]
            heat[a + 3, half, pl.ds(24, 2), :] = high[2 * a : 2 * a + 2, cut]
    for which, cell_row, a, row in (
        (0, 255, 2, 7),
        (2, 240, 2, 24),
        (6, 15, 19, 7),
        (8, 0, 19, 24),
    ):
        one = place(which, 8, lambda j: jnp.where(j == 0, cell_row, -1))
        for half in HALVES:
            heat[a, half, pl.ds(row, 1), :] = one[0:1, 128 * half : 128 * half + 128]

    def middle(a, carry):
        for row in (7, 15, 23):
            out = sweep(heat, link_a, link_z, link_r, keep, a, row, lane)
            for half in HALVES:
                other[a, half, pl.ds(row, 8), :] = (
                    out[half] + heat[a, half, pl.ds(row, 8), :]
                )
        return carry

    lax.fori_loop(2, SA + 4, middle, 0)

    def final(a, carry):
        for part in (0, 1):
            rows = pl.ds(8 * part, 8)
            out = sweep(other, link_a, link_z, link_r, keep, a + 3, 8 + 8 * part, lane)
            for half in HALVES:
                solid_out[a, rows, lanes(half)] = (
                    out[half]
                    + heat[a + 3, half, pl.ds(8 + 8 * part, 8), :]
                    + swept[a, rows, lanes(half)]
                )
        return carry

    lax.fori_loop(0, SA, final, 0)


def call(kernel, ins, outs, scratch=(), limit=48, flops=0, moved=0):
    return pl.pallas_call(
        kernel,
        out_shape=[jax.ShapeDtypeStruct(s, f32) for s in outs],
        in_specs=[pl.BlockSpec(memory_space=VMEM)] * ins,
        out_specs=[pl.BlockSpec(memory_space=VMEM)] * len(outs),
        scratch_shapes=list(scratch),
        compiler_params=pltpu.CompilerParams(vmem_limit_bytes=limit * 1024 * 1024),
        cost_estimate=pl.CostEstimate(
            flops=flops, bytes_accessed=moved, transcendentals=0
        ),
    )


def swap(values, axis, far):
    count = lax.axis_size(axis)
    pairs = [(i, (((i + 1) ^ 1) - 1) % count if far else i ^ 1) for i in range(count)]
    return lax.ppermute(values, axis, pairs)


def per_device(
    n_azim,
    n_axial,
    populations,
    fluid_flags,
    wall_cell,
    wall_drive,
    wall_owner,
    wall_slot,
    receive_cell,
    materials,
    solid_temp,
):
    devices = n_azim * n_axial
    cells = receive_cell.reshape(devices, CAP).T
    azim_msg = (2, AZIM_ROWS, 128)
    axial_msg = (2, AXIAL_ROWS, 128)
    post, near, far, low, high = call(
        first_kernel,
        5,
        [(Q, CA, CZ, NR), azim_msg, azim_msg, axial_msg, axial_msg],
        moved=8 << 20,
    )(populations, fluid_flags, solid_temp, materials, cells)
    far_a = swap(far, "azim", True)
    near_a = swap(near, "azim", False)
    near, far = call(axial_kernel, 4, [axial_msg, axial_msg], moved=4 << 20)(
        near_a, far_a, low, high
    )
    far_z = swap(far, "axial", True)
    near_z = swap(near, "axial", False)
    rows = wall_cell.shape[0]
    fluid_out, message = call(
        functools.partial(fluid_kernel, n_azim, n_axial),
        10,
        [(Q, CA, CZ, NR), (devices, 1, 128)],
        [
            VMEM((Q, CA + 4, 2, ROWS, 128), f32),
            VMEM((3, CA + 4, 2, ROWS, 128), f32),
            VMEM((Q, CA + 2, 2, ROWS, 128), f32),
            VMEM((CA * CZ, NR), f32),
        ],
        moved=16 << 20,
    )(
        post,
        fluid_flags,
        near_a,
        far_a,
        near_z,
        far_z,
        wall_cell.reshape(1, rows),
        wall_drive.reshape(1, rows),
        wall_owner.reshape(1, rows),
        wall_slot.reshape(1, rows),
    )
    arrived = lax.all_to_all(
        message, ("azim", "axial"), split_axis=0, concat_axis=0, tiled=True
    )
    solid_ext = (SA + 6, 2, ROWS, 128)
    swept, *links = call(
        functools.partial(solid_kernel, n_axial),
        6,
        [(SA, SZ, NR)] + [solid_ext] * 4,
        [VMEM(solid_ext, f32)] * 3,
        moved=8 << 20,
    )(solid_temp, materials, near_a, far_a, near_z, far_z)
    (solid_out,) = call(
        functools.partial(deposit_kernel, n_axial),
        11,
        [(SA, SZ, NR)],
        [
            VMEM(solid_ext, f32),
            VMEM(solid_ext, f32),
            VMEM((9, CAP, devices), jnp.int32),
            VMEM((devices, 128), f32),
        ],
        moved=8 << 20,
    )(arrived, cells, near_a, far_a, near_z, far_z, swept, *links)
    return fluid_out, solid_out


def solution(mesh):
    both = ("azim", "axial")
    in_specs = (
        P(None, "azim", "axial", None),
        P("azim", "axial", None),
        P(both),
        P(both),
        P(both),
        P(both),
        P(both),
        P("azim", "axial", None),
        P("azim", "axial", None),
    )
    out_specs = (P(None, "azim", "axial", None), P("azim", "axial", None))
    return jax.shard_map(
        functools.partial(per_device, mesh.shape["azim"], mesh.shape["axial"]),
        mesh=mesh,
        in_specs=in_specs,
        out_specs=out_specs,
        check_vma=False,
    )
```

profile of v0, /device:TPU:1, one launch (start us, length us, event | category | flops | bytes accessed | tf_op | source)
XLA Modules:
  0.0 86.7 jit_solution(7229087734068145759)
XLA Ops:
  0.6 0.8 reshape.19
  1.5 1.0 %copy-done = f32[16,16,256]{2,1,0:T(8,128)S(1)} copy-done((f32[16,16,256]{2,1,0:T(8,128)S(1)}, f32[16,16,256]{2,1,0:T(8,128)}, u32[]{:S(2)}) %copy-start) | copy-done | bytes 262168
  2.4 0.9 %copy-done.2 = s32[16,16,256]{2,1,0:T(8,128)S(1)} copy-done((s32[16,16,256]{2,1,0:T(8,128)S(1)}, s32[16,16,256]{2,1,0:T(8,128)}, u32[]{:S(2)}) %copy-start.2) | copy-done | bytes 262168
  3.4 0.9 %copy-done.10 = s32[8,16,256]{2,1,0:T(8,128)S(1)} copy-done((s32[8,16,256]{2,1,0:T(8,128)S(1)}, s32[8,16,256]{2,1,0:T(8,128)}, u32[]{:S(2)}) %copy-start.10) | copy-done | bytes 131096
  4.3 0.0 copy-start.17
  4.3 3.1 %shard_map.104 = (f32[19,8,16,256]{3,2,1,0:T(8,128)S(1)}, f32[2,520,128]{2,1,0:T(8,128)S(1)}, f32[2,520,128]{2,1,0:T(8,128)S(1)}, f32[2,464,128]{2,1,0:T(8,128)S(1)}, f32[2,464,128]{2,1,0:T(8,128)S(1)}) custom-call(f32[19,8,16,256]{3,2,1,0:T(8,128)} %f.1, s32[8,16,256]{2,1,0:T(8,128)S(1)} %copy-done.10, f32[16,16,256]{2,1,0:T(8,128)S(1)} %copy-done, ...), custom_call_target="tpu_custom_call" | custom-call | bytes 8388608 | tf_op jit(solution)/shard_map/pallas_call | solution.py:755
  7.4 1.5 %collective-permute-start = (f32[2,520,128]{2,1,0:T(8,128)S(1)}, f32[2,520,128]{2,1,0:T(8,128)S(1)}, u32[]{:S(2)}, u32[]{:S(2)}) collective-permute-start(f32[2,520,128]{2,1,0:T(8,128)S(1)} %get-tuple-element.17), channel_id=1, source_target_pairs={{0,8},{8,0},{16,24},{24,16},{32,40},{40,32},{48,56},{56,48},{64,72... | collective-permute-start | bytes 1597448 | tf_op jit(solution)/shard_map/ppermute | solution.py:735
  8.9 3.0 %collective-permute-start.1 = (f32[2,520,128]{2,1,0:T(8,128)S(1)}, f32[2,520,128]{2,1,0:T(8,128)S(1)}, u32[]{:S(2)}, u32[]{:S(2)}) collective-permute-start(f32[2,520,128]{2,1,0:T(8,128)S(1)} %get-tuple-element.18), channel_id=1, source_target_pairs={{0,120},{8,16},{16,8},{24,32},{32,24},{40,48},{48,40},{56,64},{64,... | collective-permute-start | bytes 1597448 | tf_op jit(solution)/shard_map/ppermute | solution.py:735
  11.9 0.0 collective-permute-done.near_in.near_a
  11.9 12.9 %collective-permute-done.1.far_in.far_a = f32[2,520,128]{2,1,0:T(8,128)S(1)} collective-permute-done((f32[2,520,128]{2,1,0:T(8,128)S(1)}, f32[2,520,128]{2,1,0:T(8,128)S(1)}, u32[]{:S(2)}, u32[]{:S(2)}) %collective-permute-start.1) | collective-permute-done | bytes 532512 | tf_op jit(solution)/shard_map/ppermute | solution.py:735
  24.8 0.2 shard_map.105
  25.0 0.0 copy-start.1
  25.0 0.0 copy-start.3
  25.0 2.4 %collective-permute-start.2 = (f32[2,464,128]{2,1,0:T(8,128)S(1)}, f32[2,464,128]{2,1,0:T(8,128)S(1)}, u32[]{:S(2)}, u32[]{:S(2)}) collective-permute-start(f32[2,464,128]{2,1,0:T(8,128)S(1)} %get-tuple-element.21), channel_id=1, source_target_pairs={{0,1},{1,0},{2,3},{3,2},{4,5},{5,4},{6,7},{7,6},{8,9},{9,8},{10,11... | collective-permute-start | bytes 1425416 | tf_op jit(solution)/shard_map/ppermute | solution.py:735
  27.4 3.6 %collective-permute-start.3 = (f32[2,464,128]{2,1,0:T(8,128)S(1)}, f32[2,464,128]{2,1,0:T(8,128)S(1)}, u32[]{:S(2)}, u32[]{:S(2)}) collective-permute-start(f32[2,464,128]{2,1,0:T(8,128)S(1)} %get-tuple-element.22), channel_id=1, source_target_pairs={{0,7},{1,2},{2,1},{3,4},{4,3},{5,6},{6,5},{7,0},{8,15},{9,10},{10,... | collective-permute-start | bytes 1425416 | tf_op jit(solution)/shard_map/ppermute | solution.py:735
  31.0 7.9 %collective-permute-done.2.near_z = f32[2,464,128]{2,1,0:T(8,128)S(1)} collective-permute-done((f32[2,464,128]{2,1,0:T(8,128)S(1)}, f32[2,464,128]{2,1,0:T(8,128)S(1)}, u32[]{:S(2)}, u32[]{:S(2)}) %collective-permute-start.2) | collective-permute-done | bytes 475168 | tf_op jit(solution)/shard_map/ppermute | solution.py:735
  38.9 9.7 %collective-permute-done.3.far_z = f32[2,464,128]{2,1,0:T(8,128)S(1)} collective-permute-done((f32[2,464,128]{2,1,0:T(8,128)S(1)}, f32[2,464,128]{2,1,0:T(8,128)S(1)}, u32[]{:S(2)}, u32[]{:S(2)}) %collective-permute-start.3) | collective-permute-done | bytes 475168 | tf_op jit(solution)/shard_map/ppermute | solution.py:735
  48.6 7.4 %shard_map.106 = (f32[19,8,16,256]{3,2,1,0:T(8,128)}, f32[128,1,128]{2,1,0:T(1,128)}) custom-call(f32[19,8,16,256]{3,2,1,0:T(8,128)S(1)} %get-tuple-element.16.post, s32[8,16,256]{2,1,0:T(8,128)S(1)} %copy-done.11, f32[2,520,128]{2,1,0:T(8,128)S(1)} %collective-permute-done.near_in.near_a, f32[2,520,128]{2,1,0:T(8,128)S(1)} %collective-permute-done.1.far_in.far_a, ...), custom_call_target="tpu_custom_call" | custom-call | bytes 16777216 | tf_op jit(solution)/shard_map/pallas_call | solution.py:769
  56.0 7.1 %all-to-all-start = ((f32[128,1,128]{2,1,0:T(1,128)}), f32[128,1,128]{2,1,0:T(1,128)S(1)}, u32[]{:S(2)}, u32[]{:S(2)}) async-start(f32[128,1,128]{2,1,0:T(1,128)} %get-tuple-element.24), calls=%async_computation | async-start | bytes 131072 | tf_op jit(solution)/shard_map/all_to_all | solution.py:792
  63.1 0.0 copy-done.1
  63.1 0.0 copy-done.3
  63.1 8.2 %shard_map.107 = (f32[16,16,256]{2,1,0:T(8,128)S(1)}, f32[22,2,32,128]{3,2,1,0:T(8,128)S(1)}, f32[22,2,32,128]{3,2,1,0:T(8,128)S(1)}, f32[22,2,32,128]{3,2,1,0:T(8,128)S(1)}, f32[22,2,32,128]{3,2,1,0:T(8,128)S(1)}) custom-call(f32[16,16,256]{2,1,0:T(8,128)S(1)} %copy-done.1, s32[16,16,256]{2,1,0:T(8,128)S(1)} %copy-done.3, ...), custom_call_target="tpu_custom_call" | custom-call | bytes 8388608 | tf_op jit(solution)/shard_map/pallas_call | solution.py:796
  71.3 0.9 %copy-done.4 = f32[22,2,32,128]{3,2,1,0:T(8,128)} copy-done((f32[22,2,32,128]{3,2,1,0:T(8,128)}, f32[22,2,32,128]{3,2,1,0:T(8,128)S(1)}, u32[]{:S(2)}) %copy-start.4) | copy-done | bytes 720920
  72.1 0.9 %copy-done.6 = f32[22,2,32,128]{3,2,1,0:T(8,128)} copy-done((f32[22,2,32,128]{3,2,1,0:T(8,128)}, f32[22,2,32,128]{3,2,1,0:T(8,128)S(1)}, u32[]{:S(2)}) %copy-start.6) | copy-done | bytes 720920
  73.0 0.9 copy-done.8
  73.9 0.7 copy-done.12
  74.6 0.0 all-to-all-done.arrived
  74.6 1.1 %copy-done.5 = f32[22,2,32,128]{3,2,1,0:T(8,128)S(1)} copy-done((f32[22,2,32,128]{3,2,1,0:T(8,128)S(1)}, f32[22,2,32,128]{3,2,1,0:T(8,128)}, u32[]{:S(2)}) %copy-start.5) | copy-done | bytes 720920
  75.7 1.1 %copy-done.7 = f32[22,2,32,128]{3,2,1,0:T(8,128)S(1)} copy-done((f32[22,2,32,128]{3,2,1,0:T(8,128)S(1)}, f32[22,2,32,128]{3,2,1,0:T(8,128)}, u32[]{:S(2)}) %copy-start.7) | copy-done | bytes 720920
  76.8 1.1 %copy-done.9 = f32[22,2,32,128]{3,2,1,0:T(8,128)S(1)} copy-done((f32[22,2,32,128]{3,2,1,0:T(8,128)S(1)}, f32[22,2,32,128]{3,2,1,0:T(8,128)}, u32[]{:S(2)}) %copy-start.9) | copy-done | bytes 720920
  77.9 0.9 %copy-done.13 = f32[16,16,256]{2,1,0:T(8,128)S(1)} copy-done((f32[16,16,256]{2,1,0:T(8,128)S(1)}, f32[16,16,256]{2,1,0:T(8,128)}, u32[]{:S(2)}) %copy-start.13) | copy-done | bytes 262168
  78.9 7.8 %shard_map.108 = f32[16,16,256]{2,1,0:T(8,128)} custom-call(f32[128,1,128]{2,1,0:T(1,128)S(1)} %all-to-all-done.arrived, s32[8,128]{1,0:T(8,128)S(1)} %bitcast.6, f32[2,520,128]{2,1,0:T(8,128)S(1)} %collective-permute-done.near_in.near_a, f32[2,520,128]{2,1,0:T(8,128)S(1)} %collective-permute-done.1.far_in.far_a, ...), custom_call_target="tpu_custom_call" | custom-call | bytes 8388608 | tf_op jit(solution)/shard_map/pallas_call | solution.py:803
  (21 shorter events, 0.1 us)
Async XLA Ops:
  1.5 1.0 %copy-start = (f32[16,16,256]{2,1,0:T(8,128)S(1)}, f32[16,16,256]{2,1,0:T(8,128)}, u32[]{:S(2)}) copy-start(f32[16,16,256]{2,1,0:T(8,128)} %temp.3) | copy-start | bytes 786436
  2.4 0.9 %copy-start.2 = (s32[16,16,256]{2,1,0:T(8,128)S(1)}, s32[16,16,256]{2,1,0:T(8,128)}, u32[]{:S(2)}) copy-start(s32[16,16,256]{2,1,0:T(8,128)} %mat.3) | copy-start | bytes 786436
  3.4 0.9 %copy-start.10 = (s32[8,16,256]{2,1,0:T(8,128)S(1)}, s32[8,16,256]{2,1,0:T(8,128)}, u32[]{:S(2)}) copy-start(s32[8,16,256]{2,1,0:T(8,128)} %flags.3) | copy-start | bytes 393220
  4.3 44.3 %copy-start.11 = (s32[8,16,256]{2,1,0:T(8,128)S(1)}, s32[8,16,256]{2,1,0:T(8,128)}, u32[]{:S(2)}) copy-start(s32[8,16,256]{2,1,0:T(8,128)} %flags.3) | copy-start | bytes 393220
  4.3 44.3 %copy-start.14 = (s32[512]{0:T(512)S(1)}, s32[512]{0:T(512)}, u32[]{:S(2)}) copy-start(s32[512]{0:T(512)} %param.11) | copy-start | bytes 6148
  4.3 44.3 %copy-start.15 = (f32[512]{0:T(512)S(1)}, f32[512]{0:T(512)}, u32[]{:S(2)}) copy-start(f32[512]{0:T(512)} %param.12) | copy-start | bytes 6148
  4.3 44.3 %copy-start.16 = (s32[512]{0:T(512)S(1)}, s32[512]{0:T(512)}, u32[]{:S(2)}) copy-start(s32[512]{0:T(512)} %param.13) | copy-start | bytes 6148
  4.3 44.3 %copy-start.17 = (s32[512]{0:T(512)S(1)}, s32[512]{0:T(512)}, u32[]{:S(2)}) copy-start(s32[512]{0:T(512)} %param.14) | copy-start | bytes 6148
  7.4 4.5 %collective-permute-start = (f32[2,520,128]{2,1,0:T(8,128)S(1)}, f32[2,520,128]{2,1,0:T(8,128)S(1)}, u32[]{:S(2)}, u32[]{:S(2)}) collective-permute-start(f32[2,520,128]{2,1,0:T(8,128)S(1)} %get-tuple-element.17), channel_id=1, source_target_pairs={{0,8},{8,0},{16,24},{24,16},{32,40},{40,32},{48,56},{56,48},{64,72... | collective-permute-start | bytes 1597448 | tf_op jit(solution)/shard_map/ppermute | solution.py:735
  8.9 15.9 %collective-permute-start.1 = (f32[2,520,128]{2,1,0:T(8,128)S(1)}, f32[2,520,128]{2,1,0:T(8,128)S(1)}, u32[]{:S(2)}, u32[]{:S(2)}) collective-permute-start(f32[2,520,128]{2,1,0:T(8,128)S(1)} %get-tuple-element.18), channel_id=1, source_target_pairs={{0,120},{8,16},{16,8},{24,32},{32,24},{40,48},{48,40},{56,64},{64,... | collective-permute-start | bytes 1597448 | tf_op jit(solution)/shard_map/ppermute | solution.py:735
  25.0 38.0 %copy-start.1 = (f32[16,16,256]{2,1,0:T(8,128)S(1)}, f32[16,16,256]{2,1,0:T(8,128)}, u32[]{:S(2)}) copy-start(f32[16,16,256]{2,1,0:T(8,128)} %temp.3) | copy-start | bytes 786436
  25.0 38.0 %copy-start.3 = (s32[16,16,256]{2,1,0:T(8,128)S(1)}, s32[16,16,256]{2,1,0:T(8,128)}, u32[]{:S(2)}) copy-start(s32[16,16,256]{2,1,0:T(8,128)} %mat.3) | copy-start | bytes 786436
  25.0 13.8 %collective-permute-start.2 = (f32[2,464,128]{2,1,0:T(8,128)S(1)}, f32[2,464,128]{2,1,0:T(8,128)S(1)}, u32[]{:S(2)}, u32[]{:S(2)}) collective-permute-start(f32[2,464,128]{2,1,0:T(8,128)S(1)} %get-tuple-element.21), channel_id=1, source_target_pairs={{0,1},{1,0},{2,3},{3,2},{4,5},{5,4},{6,7},{7,6},{8,9},{9,8},{10,11... | collective-permute-start | bytes 1425416 | tf_op jit(solution)/shard_map/ppermute | solution.py:735
  27.4 21.2 %collective-permute-start.3 = (f32[2,464,128]{2,1,0:T(8,128)S(1)}, f32[2,464,128]{2,1,0:T(8,128)S(1)}, u32[]{:S(2)}, u32[]{:S(2)}) collective-permute-start(f32[2,464,128]{2,1,0:T(8,128)S(1)} %get-tuple-element.22), channel_id=1, source_target_pairs={{0,7},{1,2},{2,1},{3,4},{4,3},{5,6},{6,5},{7,0},{8,15},{9,10},{10,... | collective-permute-start | bytes 1425416 | tf_op jit(solution)/shard_map/ppermute | solution.py:735
  56.0 18.6 %all-to-all-start = ((f32[128,1,128]{2,1,0:T(1,128)}), f32[128,1,128]{2,1,0:T(1,128)S(1)}, u32[]{:S(2)}, u32[]{:S(2)}) async-start(f32[128,1,128]{2,1,0:T(1,128)} %get-tuple-element.24), calls=%async_computation | async-start | bytes 131072 | tf_op jit(solution)/shard_map/all_to_all | solution.py:792
  71.3 0.9 %copy-start.4 = (f32[22,2,32,128]{3,2,1,0:T(8,128)}, f32[22,2,32,128]{3,2,1,0:T(8,128)S(1)}, u32[]{:S(2)}) copy-start(f32[22,2,32,128]{3,2,1,0:T(8,128)S(1)} %get-tuple-element.27.link_z) | copy-start | bytes 2162692
  72.1 0.9 %copy-start.6 = (f32[22,2,32,128]{3,2,1,0:T(8,128)}, f32[22,2,32,128]{3,2,1,0:T(8,128)S(1)}, u32[]{:S(2)}) copy-start(f32[22,2,32,128]{3,2,1,0:T(8,128)S(1)} %get-tuple-element.28.link_r) | copy-start | bytes 2162692
  73.0 0.9 copy-start.8
  73.9 0.7 copy-start.12
  74.6 1.1 %copy-start.5 = (f32[22,2,32,128]{3,2,1,0:T(8,128)S(1)}, f32[22,2,32,128]{3,2,1,0:T(8,128)}, u32[]{:S(2)}) copy-start(f32[22,2,32,128]{3,2,1,0:T(8,128)} %copy-done.4) | copy-start | bytes 2162692
  75.7 1.1 %copy-start.7 = (f32[22,2,32,128]{3,2,1,0:T(8,128)S(1)}, f32[22,2,32,128]{3,2,1,0:T(8,128)}, u32[]{:S(2)}) copy-start(f32[22,2,32,128]{3,2,1,0:T(8,128)} %copy-done.6) | copy-start | bytes 2162692
  76.8 1.1 %copy-start.9 = (f32[22,2,32,128]{3,2,1,0:T(8,128)S(1)}, f32[22,2,32,128]{3,2,1,0:T(8,128)}, u32[]{:S(2)}) copy-start(f32[22,2,32,128]{3,2,1,0:T(8,128)} %copy-done.8) | copy-start | bytes 2162692
  77.9 0.9 %copy-start.13 = (f32[16,16,256]{2,1,0:T(8,128)S(1)}, f32[16,16,256]{2,1,0:T(8,128)}, u32[]{:S(2)}) copy-start(f32[16,16,256]{2,1,0:T(8,128)} %copy-done.12) | copy-start | bytes 786436
where the time goes:
time: 87.1 us; the launch traced here: 86.7 us
  waiting for transfers between devices  30.5 us (35%)
  Pallas kernels  26.7 us (31%)
  starting transfers between devices  17.5 us (20%)
  local copies, waits for them, and re-layouts  11.3 us (13%)
    ppermute x4, waiting for transfers between devices, swap(): return lax.ppermute(values, axis, pairs)  30.5 us
    unnamed x36, local copies, waits for them, and re-layouts  10.5 us
    ppermute x4, starting transfers between devices, swap(): return lax.ppermute(values, axis, pairs)  10.4 us
    pallas_call x1, Pallas kernels, per_device(): call(functools.partial(solid_kernel, n_axial), 6, [(SA, SZ, NR)] + [solid...  8.19 us
    pallas_call x1, Pallas kernels, per_device(): call(functools.partial(deposit_kernel, n_axial), 11, [(SA, SZ, NR)], [VME...  7.78 us
    pallas_call x1, Pallas kernels, per_device(): call(functools.partial(fluid_kernel, n_azim, n_axial), 10, [(Q, CA, CZ, N...  7.4 us
    all_to_all x1, starting transfers between devices, per_device(): lax.all_to_all(message, ('azim', 'axial'), split_axis=0, concat_axis=0, t...  7.06 us
    pallas_call x1, Pallas kernels, per_device(): call(first_kernel, 5, [(Q, CA, CZ, NR), azim_msg, azim_msg, axial_msg, ax...  3.08 us
  transfers between devices with their start and end apart: 5, of which 3 were waited for; matrix products, arithmetic and copies ran while one was open for 0% of the time, Pallas kernels for 9%

commit v1 on v0

v1 whole, which is shorter than its diff:
```python
import functools

import jax
import jax.numpy as jnp
from jax import lax
from jax.experimental import pallas as pl
from jax.experimental.pallas import tpu as pltpu
from jax.sharding import PartitionSpec as P

CAP = 8
STEP_A = [0, 1, -1, 0, 0, 0, 0, 1, -1, 1, -1, 1, -1, 1, -1, 0, 0, 0, 0]
STEP_Z = [0, 0, 0, 1, -1, 0, 0, 1, -1, -1, 1, 0, 0, 0, 0, 1, -1, 1, -1]
STEP_R = [0, 0, 0, 0, 0, 1, -1, 0, 0, 0, 0, 1, -1, -1, 1, 1, -1, -1, 1]
OPPOSITE = [0, 2, 1, 4, 3, 6, 5, 8, 7, 10, 9, 12, 11, 14, 13, 16, 15, 18, 17]
AZIM_UP = [i for i in range(19) if STEP_A[i] == 1]
AZIM_DOWN = [i for i in range(19) if STEP_A[i] == -1]
AXIAL_UP = [i for i in range(19) if STEP_Z[i] == 1]
AXIAL_DOWN = [i for i in range(19) if STEP_Z[i] == -1]
RELAXATION = 1.25
SPEED_REF = 0.05
HEAT_CAPACITY = 6.5

Q = 19
CA, CZ, NR = 8, 16, 256
SA, SZ = 16, 16
HALVES = (0, 1)
ROWS = 32

PER_PLACE = 26
TEMP_ROW = 208
COND_ROW = 256
TAIL_ROW = 304
AXIAL_ROWS = 312
STREAMED_ROW = 100
SUMS_ROW = 190
FLAG_ROW = 244
SOLID_ROW = 264
SOLID_SKIP = (0, 20, 38, 54)
CELL_ROW = 376
AZIM_ROWS = 392

VMEM = pltpu.VMEM
f32 = jnp.float32
bf16 = jnp.bfloat16


def lanes(half):
    return pl.ds(128 * half, 128)


def moments(f):
    rho = f[0]
    for i in range(1, Q):
        rho = rho + f[i]
    d = [f[i] - f[i + 1] for i in range(1, Q, 2)]
    mom_a = d[0] + d[3] + d[4] + d[5] + d[6]
    mom_z = d[1] + d[3] - d[4] + d[7] + d[8]
    mom_r = d[2] + d[5] - d[6] + d[7] - d[8]
    return rho, mom_a, mom_z, mom_r


def collide_part(sums, f, flag, which):
    rho, mom_a, mom_z, mom_r = sums
    open_cell = flag > 0
    inv = 1.0 / jnp.where(open_cell, rho, 1.0)
    omega = jnp.where(open_cell, RELAXATION, 0.0)
    keep = 1.0 - omega
    ua, uz, ur = mom_a * inv, mom_z * inv, mom_r * inv
    base = 1.0 - 1.5 * (ua * ua + uz * uz + ur * ur)
    scale = omega * rho
    face, edge = scale * (1.0 / 18.0), scale * (1.0 / 36.0)
    post = {}
    if 0 in which:
        post[0] = keep * f[0] + scale * (1.0 / 3.0) * base
    for n, proj in enumerate(
        (ua, uz, ur, ua + uz, ua - uz, ua + ur, ua - ur, uz + ur, uz - ur)
    ):
        weight = face if n < 3 else edge
        one, two = 2 * n + 1, 2 * n + 2
        if one in which or two in which:
            even = weight * (base + 4.5 * proj * proj)
            odd = weight * (3.0 * proj)
        if one in which:
            post[one] = keep * f[one] + (even + odd)
        if two in which:
            post[two] = keep * f[two] + (even - odd)
    return post


def collide(f, flag):
    return collide_part(moments(f), f, flag, range(Q))


def conductivity(material):
    return jnp.where(
        material == 0,
        1.0,
        jnp.where(material == 1, 0.55, jnp.where(material == 2, 0.2, 0.8)),
    ).astype(f32)


def by_parity(axis, body, near, far):
    odd = lax.rem(lax.axis_index(axis), 2) == 1

    @pl.when(odd)
    def _():
        body(near, far)

    @pl.when(jnp.logical_not(odd))
    def _():
        body(far, near)


def first_kernel(
    f_far,
    flags_far,
    temp_far,
    mat_far,
    cells,
    post,
    near,
    far,
    f,
    flags,
    temp,
    mat,
    low,
    high,
    layers_in,
    others_in,
):
    others = [
        pltpu.make_async_copy(source, target, others_in.at[n])
        for n, (source, target) in enumerate(
            ((flags_far, flags), (temp_far, temp), (mat_far, mat))
        )
    ]

    def layer_copy(a):
        return pltpu.make_async_copy(f_far.at[:, a], f.at[:, a], layers_in.at[a])

    others[0].start()
    for a in range(CA):
        layer_copy(a).start()
    others[1].start()
    others[2].start()
    others[0].wait()

    def layer(a, carry):
        layer_copy(a).wait()
        for half in HALVES:
            for part in (0, 1):
                rows = pl.ds(8 * part, 8)
                flag = flags[a, rows, lanes(half)].astype(f32)
                out = collide([f[i, a, rows, lanes(half)] for i in range(Q)], flag)
                for i in range(Q):
                    post[i, a, rows, lanes(half)] = out[i]
                place = a * PER_PLACE
                target, inner, edge, near_edge = (
                    (low, AXIAL_DOWN, 0, 1) if part == 0 else (high, AXIAL_UP, 7, 6)
                )

                def put(row, value, at):
                    target[half, pl.ds(place + row, 1), :] = value[at : at + 1]

                for i in range(Q):
                    put(i, out[i], edge)
                for n, i in enumerate(inner):
                    put(Q + n, out[i], near_edge)
                put(24, flag, edge)
                put(25, flag, near_edge)
        return carry

    lax.fori_loop(0, CA, layer, 0)
    others[1].wait()
    others[2].wait()

    def solid_layer(a, carry):
        for half in HALVES:
            for part, target in ((0, low), (1, high)):
                rows = pl.ds(8 * part, 8)
                t = temp[a, rows, lanes(half)]
                c = conductivity(mat[a, rows, lanes(half)])
                for depth in range(3):
                    at = depth if part == 0 else 7 - depth
                    target[half, pl.ds(TEMP_ROW + depth * SA + a, 1), :] = t[
                        at : at + 1
                    ]
                    target[half, pl.ds(COND_ROW + depth * SA + a, 1), :] = c[
                        at : at + 1
                    ]
        return carry

    lax.fori_loop(0, SA, solid_layer, 0, unroll=4)
    rc = cells[...].astype(f32)
    low[0, pl.ds(TAIL_ROW, 8), :] = rc
    high[0, pl.ds(TAIL_ROW, 8), :] = rc

    def hand_over(down, up):
        down[...] = low[...]
        up[...] = high[...]

    by_parity("axial", hand_over, near, far)


def ends(n_axial):
    z = lax.axis_index("axial")
    return (
        jnp.where(z > 0, 1.0, 0.0).astype(f32),
        jnp.where(z < n_axial - 1, 1.0, 0.0).astype(f32),
    )


def shifted(pair, step, lane):
    if step == 0:
        return pair
    turn = 1 if step == 1 else 127
    at = 0 if step == 1 else 127
    a, b = (pltpu.roll(x, turn, 1) for x in pair)
    return [jnp.where(lane == at, b, a), jnp.where(lane == at, a, b)]


def split(x):
    one = x.astype(bf16)
    return one, (x - one.astype(f32)).astype(bf16)


def stream(
    source,
    opened,
    at_a,
    flag_a,
    row,
    lane,
    which=None,
    sides=None,
    rim=None,
    beyond=False,
):
    rows = pl.ds(row, 8)
    out = [[], []]
    for i in range(Q) if which is None else which:
        own = OPPOSITE[i]
        from_rows = pl.ds(row - STEP_Z[i], 8)

        def before(half):
            if rim and i in rim:
                return sides[rim[i][0], rim[i][1], half, from_rows, :]
            if beyond:
                return source[i, at_a, half, from_rows, :]
            return source[i, at_a - STEP_A[i], half, from_rows, :]

        def back(half):
            if beyond:
                return sides[rim[own][0], rim[own][1], half, rows, :]
            return source[own, at_a, half, rows, :]

        moved = shifted([before(half) for half in HALVES], STEP_R[i], lane)
        for half in HALVES:
            if i == 0:
                out[half].append(moved[half])
                continue
            from_a = flag_a if beyond else flag_a - STEP_A[i]
            mask = opened[STEP_R[i] % 3, from_a, half, from_rows, :]
            out[half].append(jnp.where(mask > 0, moved[half], back(half)))
    return out


def rim_kernel(
    n_axial,
    post,
    flags,
    temp,
    mat,
    cells,
    near_z,
    far_z,
    ext,
    opened,
    near,
    far,
    low,
    high,
):
    lane = lax.broadcasted_iota(jnp.int32, (8, 128), 1)
    below, above = ends(n_axial)

    def own_layer(a, carry):
        for half in HALVES:
            for part in (0, 1):
                rows = pl.ds(8 * part, 8)
                to = pl.ds(8 + 8 * part, 8)
                for i in range(Q):
                    ext[i, a, half, to, :] = post[i, a, rows, lanes(half)]
                opened[0, a, half, to, :] = flags[a, rows, lanes(half)].astype(f32)
        return carry

    lax.fori_loop(0, CA, own_layer, 0)

    def axial_rim(lower, upper):
        def layer(a, carry):
            place = a * PER_PLACE
            for half in HALVES:
                for source, first, last, moving, there in (
                    (lower, 7, 6, AXIAL_UP, below),
                    (upper, 24, 25, AXIAL_DOWN, above),
                ):

                    def get(row):
                        return source[half, pl.ds(place + row, 1), :]

                    for i in range(Q):
                        ext[i, a, half, pl.ds(first, 1), :] = get(i)
                    for n, i in enumerate(moving):
                        ext[i, a, half, pl.ds(last, 1), :] = get(Q + n)
                    opened[0, a, half, pl.ds(first, 1), :] = get(24) * there
                    opened[0, a, half, pl.ds(last, 1), :] = get(25) * there
            return carry

        lax.fori_loop(0, CA, layer, 0, unroll=2)
        own = cells[...].astype(f32)
        outside = jnp.full((CAP, 128), SA * SZ * NR, f32)
        for target, first, step in ((low, 0, 1), (high, SA - 1, -1)):
            for half in HALVES:
                for n in range(3):
                    a = first + step * n
                    at = SOLID_ROW + SOLID_SKIP[n]
                    target[half, pl.ds(at + 2 - n, 16), :] = temp[a, :, lanes(half)]
                    target[half, pl.ds(at + 56 - n, 16), :] = conductivity(
                        mat[a, :, lanes(half)]
                    )
                    for depth in range(2 - n):
                        for source, row, there in (
                            (lower, at + 1 - n - depth, below),
                            (upper, at + 18 - n + depth, above),
                        ):
                            target[half, pl.ds(row, 1), :] = source[
                                half, pl.ds(TEMP_ROW + depth * SA + a, 1), :
                            ]
                            target[half, pl.ds(row + 54, 1), :] = (
                                source[half, pl.ds(COND_ROW + depth * SA + a, 1), :]
                                * there
                            )
            target[0, pl.ds(CELL_ROW, 8), :] = own
            for half, row, source, there in (
                (1, CELL_ROW, lower, below),
                (0, CELL_ROW + 8, upper, above),
            ):
                target[half, pl.ds(row, 8), :] = jnp.where(
                    there > 0, source[0, pl.ds(TAIL_ROW, 8), :], outside
                )

    by_parity("axial", axial_rim, near_z, far_z)

    def turn(a, carry):
        turn_flags(opened, a, lane)
        return carry

    lax.fori_loop(0, CA, turn, 0, unroll=2)

    for target, layer, moving, step in (
        (low, 0, AZIM_DOWN, -1),
        (high, CA - 1, AZIM_UP, 1),
    ):
        for half in HALVES:
            for n, i in enumerate(moving):
                target[half, pl.ds(20 * n, 20), :] = ext[
                    i, layer, half, pl.ds(6, 20), :
                ]
            target[half, pl.ds(FLAG_ROW, 20), :] = opened[
                0, layer, half, pl.ds(6, 20), :
            ]
        which = [i for i in range(Q) if STEP_A[i] in (0, step)]
        for row in (7, 15, 17):
            moved = stream(ext, opened, layer, layer, row, lane, which)
            for half in HALVES:
                new = dict(zip(which, moved[half]))
                at = row - 7
                for n, i in enumerate(moving):
                    target[half, pl.ds(STREAMED_ROW + 18 * n + at, 8), :] = new[i]
                still = [i for i in which if STEP_A[i] == 0]
                for n, table in enumerate(([1] * Q, STEP_Z, STEP_R)):
                    total = None
                    for i in still:
                        if table[i]:
                            term = new[i] * table[i]
                            total = term if total is None else total + term
                    target[half, pl.ds(SUMS_ROW + 18 * n + at, 8), :] = total

    def hand_over(down, up):
        down[...] = low[...]
        up[...] = high[...]

    by_parity("azim", hand_over, near, far)


def turn_flags(opened, a, lane):
    for part in range(4):
        rows = pl.ds(8 * part, 8)
        pair = [opened[0, a, half, rows, :] for half in HALVES]
        up = shifted(pair, 1, lane)
        down = shifted(pair, -1, lane)
        opened[1, a, 0, rows, :] = jnp.where(lane == 0, 0.0, up[0])
        opened[1, a, 1, rows, :] = up[1]
        opened[2, a, 0, rows, :] = down[0]
        opened[2, a, 1, rows, :] = jnp.where(lane == 127, 0.0, down[1])


def fluid_kernel(
    n_azim,
    n_axial,
    ext,
    own_opened,
    near_a,
    far_a,
    cell,
    drive,
    owner,
    slot,
    fluid_far,
    message,
    opened,
    second,
    sides,
    speeds,
    fluid_out,
    layers_out,
):
    lane = lax.broadcasted_iota(jnp.int32, (8, 128), 1)

    def own_flags(a, carry):
        for k in range(3):
            for half in HALVES:
                opened[k, a + 1, half] = own_opened[k, a, half]
        return carry

    lax.fori_loop(0, CA, own_flags, 0, unroll=2)

    def azim_rim(lower, upper):
        for side, (source, a) in enumerate(((lower, 0), (upper, CA + 1))):
            for half in HALVES:
                for n in range(5):
                    sides[side, n, half, pl.ds(6, 20), :] = source[
                        half, pl.ds(20 * n, 20), :
                    ]
                for n in range(8):
                    sides[side, 5 + n, half, pl.ds(7, 18), :] = source[
                        half, pl.ds(STREAMED_ROW + 18 * n, 18), :
                    ]
                opened[0, a, half, pl.ds(6, 20), :] = source[
                    half, pl.ds(FLAG_ROW, 20), :
                ]

    by_parity("azim", azim_rim, near_a, far_a)
    turn_flags(opened, 0, lane)
    turn_flags(opened, CA + 1, lane)

    def finish(a, row, moved):
        for half in HALVES:
            out = collide(moved[half], opened[0, a + 1, half, pl.ds(row, 8), :])
            for i in range(Q):
                second[i, a + 1, half, pl.ds(row, 8), :] = out[i]

    def first_step(a, carry):
        for row in (7, 15, 23):
            finish(a, row, stream(ext, opened, a, a + 1, row, lane))
        return carry

    lax.fori_loop(1, CA - 1, first_step, 0)
    for side, (a, inward, outward) in enumerate(
        ((0, AZIM_UP, AZIM_DOWN), (CA - 1, AZIM_DOWN, AZIM_UP))
    ):
        rim = {i: (side, n) for n, i in enumerate(inward)}
        beyond = 0 if side == 0 else CA + 1

        def edge_step(n, carry):
            row = 7 + 8 * n
            finish(a, row, stream(ext, opened, a, a + 1, row, lane, None, sides, rim))
            far_in = stream(
                ext, opened, a, a + 1, row, lane, outward, sides, rim, beyond=True
            )
            for half in HALVES:
                rows = pl.ds(row, 8)

                def at(n):
                    return sides[side, n, half, rows, :]

                new = {i: at(5 + n) for n, i in enumerate(inward)}
                new.update(zip(outward, far_in[half]))
                sums = [at(10), None, at(11), at(12)]
                for k, table in enumerate(([1] * Q, STEP_A, STEP_Z, STEP_R)):
                    for i in inward + outward:
                        if table[i]:
                            term = new[i] * table[i]
                            sums[k] = term if sums[k] is None else sums[k] + term
                out = collide_part(
                    sums, new, opened[0, beyond, half, rows, :], inward
                )
                for i in inward:
                    second[i, beyond, half, rows, :] = out[i]
            return carry

        lax.fori_loop(0, 3, edge_step, 0)

    def second_step(a, carry):
        for part in (0, 1):
            moved = stream(second, opened, a + 1, a + 1, 8 + 8 * part, lane)
            for half in HALVES:
                for i in range(Q):
                    fluid_out[i, a, pl.ds(8 * part, 8), lanes(half)] = moved[half][i]
                rho, mom_a, mom_z, mom_r = moments(moved[half])
                inv = 1.0 / rho
                ua, uz, ur = mom_a * inv, mom_z * inv, mom_r * inv
                speeds[pl.ds(a * CZ + 8 * part, 8), lanes(half)] = jnp.sqrt(
                    ua * ua + uz * uz + ur * ur + 1e-06
                )
        layer_copy(a).start()
        return carry

    def layer_copy(a):
        return pltpu.make_async_copy(
            fluid_out.at[:, a], fluid_far.at[:, a], layers_out.at[a]
        )

    lax.fori_loop(0, CA, second_step, 0)

    rows_here = cell.shape[1]
    place = cell[...]
    row_hot = (
        lax.broadcasted_iota(jnp.int32, (CA * CZ, rows_here), 0) == place // NR
    ).astype(f32).astype(bf16)
    turned = jnp.transpose(speeds[...])
    picked = jnp.zeros((NR, rows_here), f32)
    for term in split(turned):
        picked = picked + jnp.dot(term, row_hot, preferred_element_type=f32)
    column = lax.broadcasted_iota(jnp.int32, (NR, rows_here), 0) == place % NR
    speed = jnp.sum(jnp.where(column, picked, 0.0), axis=0, keepdims=True)
    flux = drive[...] * (0.2 + speed / SPEED_REF)
    devices = n_azim * n_axial
    owner_hot = (
        lax.broadcasted_iota(jnp.int32, (devices, rows_here), 0) == owner[...]
    ).astype(f32).astype(bf16)
    slotted = jnp.where(
        lax.broadcasted_iota(jnp.int32, (128, rows_here), 0) == slot[...], flux, 0.0
    )
    sent = jnp.zeros((devices, 128), f32)
    for term in split(slotted):
        sent = sent + lax.dot_general(
            owner_hot, term, (((1,), (1,)), ((), ())), preferred_element_type=f32
        )
    total = jnp.zeros((devices, 128), f32)
    for da in (-1, 0, 1):
        for dz in (-1, 0, 1):
            which = (da + 1) * 3 + dz + 1
            back = (-(da * n_axial + dz)) % devices
            moved = pltpu.roll(sent, back, 0) if back else sent
            total = total + (pltpu.roll(moved, CAP * which, 1) if which else moved)
    for o in range(devices):
        message[o, :, :] = total[o : o + 1]
    for a in range(CA):
        layer_copy(a).wait()


def link(first, second):
    joined = first + second
    good = joined > 0
    return jnp.where(
        good,
        (2.0 / HEAT_CAPACITY) * first * second / jnp.where(good, joined, 1.0),
        0.0,
    )


def sweep(source, link_a, link_z, link_r, keep, a, row, lane):
    rows = pl.ds(row, 8)
    pair = [source[a, half, rows, :] for half in HALVES]
    lr = [link_r[a, half, rows, :] for half in HALVES]
    up = shifted(pair, -1, lane)
    down = shifted([x * y for x, y in zip(pair, lr)], 1, lane)
    out = []
    for half in HALVES:
        total = keep[a, half, rows, :] * pair[half]
        total = total + link_a[a, half, rows, :] * source[a + 1, half, rows, :]
        total = total + link_a[a - 1, half, rows, :] * source[a - 1, half, rows, :]
        total = (
            total + link_z[a, half, rows, :] * source[a, half, pl.ds(row + 1, 8), :]
        )
        total = (
            total
            + link_z[a, half, pl.ds(row - 1, 8), :]
            * source[a, half, pl.ds(row - 1, 8), :]
        )
        out.append(total + lr[half] * up[half] + down[half])
    return out


def solid_kernel(
    n_axial,
    temp,
    mat,
    near_a,
    far_a,
    near_z,
    far_z,
    cells,
    swept,
    link_a,
    link_z,
    link_r,
    keep,
    all_cells,
    ext,
    cond,
    other,
):
    lane = lax.broadcasted_iota(jnp.int32, (8, 128), 1)

    def own_layer(a, carry):
        for half in HALVES:
            for part in (0, 1):
                rows = pl.ds(8 * part, 8)
                to = pl.ds(8 + 8 * part, 8)
                ext[a + 3, half, to, :] = temp[a, rows, lanes(half)]
                cond[a + 3, half, to, :] = conductivity(mat[a, rows, lanes(half)])
        return carry

    lax.fori_loop(0, SA, own_layer, 0, unroll=4)

    def azim_rim(lower, upper):
        for half in HALVES:
            for n in range(3):
                for source, a in ((lower, 2 - n), (upper, 19 + n)):
                    at = SOLID_ROW + SOLID_SKIP[n]
                    rows = pl.ds(6 + n, 20 - 2 * n)
                    ext[a, half, rows, :] = source[half, pl.ds(at, 20 - 2 * n), :]
                    cond[a, half, rows, :] = source[half, pl.ds(at + 54, 20 - 2 * n), :]
        for source, which in ((lower, 0), (upper, 6)):
            all_cells[which + 1] = source[0, pl.ds(CELL_ROW, 8), :]
            all_cells[which] = source[1, pl.ds(CELL_ROW, 8), :]
            all_cells[which + 2] = source[0, pl.ds(CELL_ROW + 8, 8), :]

    by_parity("azim", azim_rim, near_a, far_a)
    below, above = ends(n_axial)

    def axial_rim(lower, upper):
        def layer(a, carry):
            for half in HALVES:
                for depth in range(3):
                    for source, row, there in (
                        (lower, 7 - depth, below),
                        (upper, 24 + depth, above),
                    ):
                        ext[a + 3, half, pl.ds(row, 1), :] = source[
                            half, pl.ds(TEMP_ROW + depth * SA + a, 1), :
                        ]
                        cond[a + 3, half, pl.ds(row, 1), :] = (
                            source[half, pl.ds(COND_ROW + depth * SA + a, 1), :] * there
                        )
            return carry

        lax.fori_loop(0, SA, layer, 0, unroll=4)
        outside = jnp.full((CAP, 128), SA * SZ * NR, f32)
        for source, which, there in ((lower, 3, below), (upper, 5, above)):
            all_cells[which] = jnp.where(
                there > 0, source[0, pl.ds(TAIL_ROW, 8), :], outside
            )

    by_parity("axial", axial_rim, near_z, far_z)
    all_cells[4] = cells[...].astype(f32)

    def links(a, carry):
        for row in (5, 13, 21):
            rows = pl.ds(row, 8)
            pair = [cond[a, half, rows, :] for half in HALVES]
            up = shifted(pair, -1, lane)
            up = [up[0], jnp.where(lane == 127, 0.0, up[1])]
            for half in HALVES:
                link_a[a, half, rows, :] = link(pair[half], cond[a + 1, half, rows, :])
                link_z[a, half, rows, :] = link(
                    pair[half], cond[a, half, pl.ds(row + 1, 8), :]
                )
                link_r[a, half, rows, :] = link(pair[half], up[half])
        return carry

    lax.fori_loop(0, SA + 5, links, 0, unroll=3)

    def keeps(a, carry):
        for row in (6, 14, 22):
            rows = pl.ds(row, 8)
            pair = [link_r[a, half, rows, :] for half in HALVES]
            down = shifted(pair, 1, lane)
            for half in HALVES:
                keep[a, half, rows, :] = 1.0 - (
                    link_a[a, half, rows, :]
                    + link_a[a - 1, half, rows, :]
                    + link_z[a, half, rows, :]
                    + link_z[a, half, pl.ds(row - 1, 8), :]
                    + pair[half]
                    + down[half]
                )
        return carry

    lax.fori_loop(1, SA + 5, keeps, 0, unroll=4)

    def once(source, target, first, last, at):
        def layer(a, carry):
            for row in at:
                out = sweep(source, link_a, link_z, link_r, keep, a, row, lane)
                for half in HALVES:
                    target[a, half, pl.ds(row, 8), :] = out[half]
            return carry

        lax.fori_loop(first, last, layer, 0, unroll=2)

    once(ext, other, 1, SA + 5, (6, 14, 22))
    once(other, ext, 2, SA + 4, (7, 15, 23))

    def final(a, carry):
        for part in (0, 1):
            out = sweep(ext, link_a, link_z, link_r, keep, a + 3, 8 + 8 * part, lane)
            for half in HALVES:
                swept[a, pl.ds(8 * part, 8), lanes(half)] = out[half]
        return carry

    lax.fori_loop(0, SA, final, 0, unroll=4)


def deposit_kernel(
    swept_far,
    link_a_far,
    link_z_far,
    link_r_far,
    keep_far,
    arrived,
    all_cells,
    solid_out,
    heat,
    other,
    came,
    swept,
    link_a,
    link_z,
    link_r,
    keep,
    brought,
):
    copies = [
        pltpu.make_async_copy(source, target, brought.at[n])
        for n, (source, target) in enumerate(
            (
                (swept_far, swept),
                (link_a_far, link_a),
                (link_z_far, link_z),
                (link_r_far, link_r),
                (keep_far, keep),
            )
        )
    ]
    for copy in copies:
        copy.start()
    lane = lax.broadcasted_iota(jnp.int32, (8, 128), 1)
    senders = arrived.shape[0]
    for s in range(senders):
        came[pl.ds(s, 1), :] = arrived[s]

    def clear(a, carry):
        for half in HALVES:
            heat[a, half] = jnp.zeros((ROWS, 128), f32)
        return carry

    lax.fori_loop(0, SA + 6, clear, 0, unroll=2)

    values = jnp.transpose(came[...]) * (1.0 / HEAT_CAPACITY)

    def place(which, rows, row_of):
        cell = all_cells[which].astype(jnp.int32)
        value = values[CAP * which : CAP * (which + 1)]
        one, two = split(value)
        at_row = row_of(lax.broadcasted_iota(jnp.int32, (rows, senders), 0))
        at_col = lax.broadcasted_iota(jnp.int32, (NR, senders), 0)
        left, right = [[], []], []
        for c in range(CAP):
            hit = at_row == (cell[c : c + 1] // NR)
            for to, term in zip(left, (one, two)):
                to.append(
                    jnp.where(hit, term[c : c + 1].astype(f32), 0.0).astype(bf16)
                )
            right.append((at_col == cell[c : c + 1] % NR).astype(f32).astype(bf16))
        right = jnp.concatenate(right, axis=1)
        total = None
        for to in left:
            part = lax.dot_general(
                jnp.concatenate(to, axis=1),
                right,
                (((1,), (1,)), ((), ())),
                preferred_element_type=f32,
            )
            total = part if total is None else total + part
        return total

    own = place(4, SA * SZ, lambda j: j)
    for a in range(SA):
        for half in HALVES:
            heat[a + 3, half, pl.ds(8, 16), :] = own[
                16 * a : 16 * a + 16, 128 * half : 128 * half + 128
            ]
    low = place(1, 32, lambda j: j + 14 * SZ)
    high = place(7, 32, lambda j: j)
    for n in range(2):
        for half in HALVES:
            cut = slice(128 * half, 128 * half + 128)
            heat[1 + n, half, pl.ds(8, 16), :] = low[16 * n : 16 * n + 16, cut]
            heat[19 + n, half, pl.ds(8, 16), :] = high[16 * n : 16 * n + 16, cut]
    low = place(3, 32, lambda j: (j // 2) * SZ + 14 + j % 2)
    high = place(5, 32, lambda j: (j // 2) * SZ + j % 2)
    for a in range(SA):
        for half in HALVES:
            cut = slice(128 * half, 128 * half + 128)
            heat[a + 3, half, pl.ds(6, 2), :] = low[2 * a : 2 * a + 2, cut]
            heat[a + 3, half, pl.ds(24, 2), :] = high[2 * a : 2 * a + 2, cut]
    for which, cell_row, a, row in (
        (0, 255, 2, 7),
        (2, 240, 2, 24),
        (6, 15, 19, 7),
        (8, 0, 19, 24),
    ):
        one = place(which, 8, lambda j: jnp.where(j == 0, cell_row, -1))
        for half in HALVES:
            heat[a, half, pl.ds(row, 1), :] = one[0:1, 128 * half : 128 * half + 128]

    for copy in copies:
        copy.wait()

    def middle(a, carry):
        for row in (7, 15, 23):
            out = sweep(heat, link_a, link_z, link_r, keep, a, row, lane)
            for half in HALVES:
                other[a, half, pl.ds(row, 8), :] = (
                    out[half] + heat[a, half, pl.ds(row, 8), :]
                )
        return carry

    lax.fori_loop(2, SA + 4, middle, 0, unroll=2)

    def final(a, carry):
        for part in (0, 1):
            rows = pl.ds(8 * part, 8)
            out = sweep(other, link_a, link_z, link_r, keep, a + 3, 8 + 8 * part, lane)
            for half in HALVES:
                solid_out[a, rows, lanes(half)] = (
                    out[half]
                    + heat[a + 3, half, pl.ds(8 + 8 * part, 8), :]
                    + swept[a, rows, lanes(half)]
                )
        return carry

    lax.fori_loop(0, SA, final, 0, unroll=4)


def call(kernel, ins, outs, scratch=(), limit=16, moved=0, far_ins=0, far_outs=0):
    here, there = (pl.BlockSpec(memory_space=m) for m in (VMEM, pltpu.HBM))
    kernel_call = pl.pallas_call(
        kernel,
        out_shape=[jax.ShapeDtypeStruct(s, f32) for s in outs],
        in_specs=[there] * far_ins + [here] * (ins - far_ins),
        out_specs=[there] * far_outs + [here] * (len(outs) - far_outs),
        scratch_shapes=list(scratch),
        compiler_params=pltpu.CompilerParams(vmem_limit_bytes=limit * 1024 * 1024),
        cost_estimate=pl.CostEstimate(
            flops=0, bytes_accessed=moved, transcendentals=0
        ),
    )

    def run(*args):
        far = [pltpu.with_memory_space_constraint(x, pltpu.HBM) for x in args[:far_ins]]
        return kernel_call(*far, *args[far_ins:])

    return run


def swap(values, axis, far):
    count = lax.axis_size(axis)
    pairs = [(i, (((i + 1) ^ 1) - 1) % count if far else i ^ 1) for i in range(count)]
    return lax.ppermute(values, axis, pairs)


def per_device(
    n_azim,
    n_axial,
    populations,
    fluid_flags,
    wall_cell,
    wall_drive,
    wall_owner,
    wall_slot,
    receive_cell,
    materials,
    solid_temp,
):
    devices = n_azim * n_axial
    cells = receive_cell.reshape(devices, CAP).T
    azim_msg = (2, AZIM_ROWS, 128)
    axial_msg = (2, AXIAL_ROWS, 128)
    fluid = (Q, CA, CZ, NR)
    solid = (SA, SZ, NR)
    fluid_ext = (Q, CA, 2, ROWS, 128)
    solid_ext = (SA + 6, 2, ROWS, 128)
    post, near_z, far_z = call(
        first_kernel,
        5,
        [fluid, axial_msg, axial_msg],
        [
            VMEM(fluid, f32),
            VMEM((CA, CZ, NR), jnp.int32),
            VMEM(solid, f32),
            VMEM(solid, jnp.int32),
            VMEM(axial_msg, f32),
            VMEM(axial_msg, f32),
            pltpu.SemaphoreType.DMA((CA,)),
            pltpu.SemaphoreType.DMA((3,)),
        ],
        moved=8 << 20,
        far_ins=4,
    )(populations, fluid_flags, solid_temp, materials, cells)
    near_z = swap(near_z, "axial", False)
    far_z = swap(far_z, "axial", True)
    ext, opened, near_a, far_a = call(
        functools.partial(rim_kernel, n_axial),
        7,
        [fluid_ext, (3, CA, 2, ROWS, 128), azim_msg, azim_msg],
        [VMEM(azim_msg, f32), VMEM(azim_msg, f32)],
        moved=8 << 20,
    )(post, fluid_flags, solid_temp, materials, cells, near_z, far_z)
    near_a = swap(near_a, "azim", False)
    far_a = swap(far_a, "azim", True)
    rows = wall_cell.shape[0]
    fluid_out, message = call(
        functools.partial(fluid_kernel, n_azim, n_axial),
        8,
        [fluid, (devices, 1, 128)],
        [
            VMEM((3, CA + 2, 2, ROWS, 128), f32),
            VMEM((Q, CA + 2, 2, ROWS, 128), f32),
            VMEM((2, 13, 2, ROWS, 128), f32),
            VMEM((CA * CZ, NR), f32),
            VMEM(fluid, f32),
            pltpu.SemaphoreType.DMA((CA,)),
        ],
        limit=28,
        moved=16 << 20,
        far_outs=1,
    )(
        ext,
        opened,
        near_a,
        far_a,
        wall_cell.reshape(1, rows),
        wall_drive.reshape(1, rows),
        wall_owner.reshape(1, rows),
        wall_slot.reshape(1, rows),
    )
    arrived = lax.all_to_all(
        message, ("azim", "axial"), split_axis=0, concat_axis=0, tiled=True
    )
    *swept, all_cells = call(
        functools.partial(solid_kernel, n_axial),
        7,
        [solid] + [solid_ext] * 4 + [(9, CAP, devices)],
        [VMEM(solid_ext, f32)] * 3,
        moved=8 << 20,
    )(solid_temp, materials, near_a, far_a, near_z, far_z, cells)
    (solid_out,) = call(
        deposit_kernel,
        7,
        [solid],
        [
            VMEM(solid_ext, f32),
            VMEM(solid_ext, f32),
            VMEM((devices, 128), f32),
            VMEM(solid, f32),
        ]
        + [VMEM(solid_ext, f32)] * 4
        + [pltpu.SemaphoreType.DMA((5,))],
        moved=8 << 20,
        far_ins=5,
    )(*swept, arrived, all_cells)
    return fluid_out, solid_out


def solution(mesh):
    both = ("azim", "axial")
    in_specs = (
        P(None, "azim", "axial", None),
        P("azim", "axial", None),
        P(both),
        P(both),
        P(both),
        P(both),
        P(both),
        P("azim", "axial", None),
        P("azim", "axial", None),
    )
    out_specs = (P(None, "azim", "axial", None), P("azim", "axial", None))
    return jax.shard_map(
        functools.partial(per_device, mesh.shape["azim"], mesh.shape["axial"]),
        mesh=mesh,
        in_specs=in_specs,
        out_specs=out_specs,
        check_vma=False,
    )
```

time: 87.1 us -> 67.6 us (0.78)
  Pallas kernels: 26.7 us -> 18.3 us
  local copies, waits for them, and re-layouts: 11.3 us -> 5.1 us
  waiting for transfers between devices: 30.5 us -> 25.6 us
    pallas_call x5, Pallas kernels: 26.7 us -> 18.3 us  [run(): return kernel_call(*far, *args[far_ins:])]
    ppermute x4, waiting for transfers between devices: 30.5 us -> 24 us  [swap(): return lax.ppermute(values, axis, pairs)]
    unnamed x36 -> x24, local copies, waits for them, and re-layouts: 10.5 us -> 4.23 us
    all_to_all x1, waiting for transfers between devices: 0.01 us -> 1.57 us  [per_device(): lax.all_to_all(message, ('azim', 'axial'), split_axis=0, concat_axis=0, t...]
  transfers between devices with their start and end apart: 5 -> 5, of which waited for: 3 -> 4; matrix products, arithmetic and copies ran while one was open for 0% -> 0% of each run, Pallas kernels for 9% -> 6%
where the time goes in v1:
time: 67.6 us; the launch traced here: 67.4 us
  waiting for transfers between devices  25.6 us (38%)
  Pallas kernels  18.3 us (27%)
  starting transfers between devices  17.7 us (26%)
  local copies, waits for them, and re-layouts  5.1 us (8%)
  between operations  0.76 us (1%)
    ppermute x4, waiting for transfers between devices, swap(): return lax.ppermute(values, axis, pairs)  24 us
    pallas_call x5, Pallas kernels, run(): return kernel_call(*far, *args[far_ins:])  18.3 us
    ppermute x4, starting transfers between devices, swap(): return lax.ppermute(values, axis, pairs)  10.4 us
    all_to_all x1, starting transfers between devices, per_device(): lax.all_to_all(message, ('azim', 'axial'), split_axis=0, concat_axis=0, t...  7.34 us
    unnamed x24, local copies, waits for them, and re-layouts  4.23 us
    all_to_all x1, waiting for transfers between devices, per_device(): lax.all_to_all(message, ('azim', 'axial'), split_axis=0, concat_axis=0, t...  1.57 us
  transfers between devices with their start and end apart: 5, of which 4 were waited for; matrix products, arithmetic and copies ran while one was open for 0% of the time, Pallas kernels for 6%

profile of v1, /device:TPU:1, one launch (start us, length us, event | category | flops | bytes accessed | tf_op | source)
XLA Modules:
  0.0 67.4 jit_solution(18191668684330088076)
XLA Ops:
  0.6 0.0 copy-start
  0.6 0.0 copy-start.1
  0.7 0.0 copy-start.6
  0.7 0.8 %reshape.19 = s32[128,8]{1,0:T(8,128)S(1)} reshape(s32[1024]{0:T(1024)} %param.15) | data formatting | bytes 8192 | tf_op jit(solution)/shard_map/reshape | solution.py:901
  1.5 2.7 %shard_map.104 = (f32[19,8,16,256]{3,2,1,0:T(8,128)S(1)}, f32[2,312,128]{2,1,0:T(8,128)S(1)}, f32[2,312,128]{2,1,0:T(8,128)S(1)}) custom-call(f32[19,8,16,256]{3,2,1,0:T(8,128)} %f_far.1, s32[8,16,256]{2,1,0:T(8,128)} %flags.1, f32[16,16,256]{2,1,0:T(8,128)} %temp.3, s32[16,16,256]{2,1,0:T(8,128)} %mat.3, s32[8,128]{1,0:T(8,128)S(1)} %bitcast.5), custom_call_target="tpu_custom_call" | custom-call | bytes 8388608 | tf_op jit(solution)/shard_map/pallas_call | solution.py:876
  4.3 0.0 copy-start.8
  4.3 0.0 copy-start.9
  4.3 0.0 copy-start.10
  4.3 0.0 copy-start.11
  4.3 2.2 %collective-permute-start = (f32[2,312,128]{2,1,0:T(8,128)S(1)}, f32[2,312,128]{2,1,0:T(8,128)S(1)}, u32[]{:S(2)}, u32[]{:S(2)}) collective-permute-start(f32[2,312,128]{2,1,0:T(8,128)S(1)} %get-tuple-element.18), channel_id=1, source_target_pairs={{0,1},{1,0},{2,3},{3,2},{4,5},{5,4},{6,7},{7,6},{8,9},{9,8},{10,11... | collective-permute-start | bytes 958472 | tf_op jit(solution)/shard_map/ppermute | solution.py:884
  6.5 3.6 %collective-permute-start.1 = (f32[2,312,128]{2,1,0:T(8,128)S(1)}, f32[2,312,128]{2,1,0:T(8,128)S(1)}, u32[]{:S(2)}, u32[]{:S(2)}) collective-permute-start(f32[2,312,128]{2,1,0:T(8,128)S(1)} %get-tuple-element.19), channel_id=1, source_target_pairs={{0,7},{1,2},{2,1},{3,4},{4,3},{5,6},{6,5},{7,0},{8,15},{9,10},{10,... | collective-permute-start | bytes 958472 | tf_op jit(solution)/shard_map/ppermute | solution.py:884
  10.1 3.2 %collective-permute-done.near_z = f32[2,312,128]{2,1,0:T(8,128)S(1)} collective-permute-done((f32[2,312,128]{2,1,0:T(8,128)S(1)}, f32[2,312,128]{2,1,0:T(8,128)S(1)}, u32[]{:S(2)}, u32[]{:S(2)}) %collective-permute-start) | collective-permute-done | bytes 319520 | tf_op jit(solution)/shard_map/ppermute | solution.py:884
  13.4 10.6 %collective-permute-done.1.far_z = f32[2,312,128]{2,1,0:T(8,128)S(1)} collective-permute-done((f32[2,312,128]{2,1,0:T(8,128)S(1)}, f32[2,312,128]{2,1,0:T(8,128)S(1)}, u32[]{:S(2)}, u32[]{:S(2)}) %collective-permute-start.1) | collective-permute-done | bytes 319520 | tf_op jit(solution)/shard_map/ppermute | solution.py:884
  23.9 0.0 copy-done
  23.9 0.0 copy-done.1
  23.9 0.0 copy-done.6
  23.9 1.4 %shard_map.105 = (f32[19,8,2,32,128]{4,3,2,1,0:T(8,128)S(1)}, f32[3,8,2,32,128]{4,3,2,1,0:T(8,128)S(1)}, f32[2,392,128]{2,1,0:T(8,128)S(1)}, f32[2,392,128]{2,1,0:T(8,128)S(1)}) custom-call(f32[19,8,16,256]{3,2,1,0:T(8,128)S(1)} %get-tuple-element.17.post, s32[8,16,256]{2,1,0:T(8,128)S(1)} %copy-done.6, f32[16,16,256]{2,1,0:T(8,128)S(1)} %copy-done, ...), custom_call_target="tpu_custom_call" | custom-call | bytes 8388608 | tf_op jit(solution)/shard_map/pallas_call | solution.py:876
  25.3 1.6 %collective-permute-start.2 = (f32[2,392,128]{2,1,0:T(8,128)S(1)}, f32[2,392,128]{2,1,0:T(8,128)S(1)}, u32[]{:S(2)}, u32[]{:S(2)}) collective-permute-start(f32[2,392,128]{2,1,0:T(8,128)S(1)} %get-tuple-element.22), channel_id=1, source_target_pairs={{0,8},{8,0},{16,24},{24,16},{32,40},{40,32},{48,56},{56,48},{64,72... | collective-permute-start | bytes 1204232 | tf_op jit(solution)/shard_map/ppermute | solution.py:884
  26.9 2.9 %collective-permute-start.3 = (f32[2,392,128]{2,1,0:T(8,128)S(1)}, f32[2,392,128]{2,1,0:T(8,128)S(1)}, u32[]{:S(2)}, u32[]{:S(2)}) collective-permute-start(f32[2,392,128]{2,1,0:T(8,128)S(1)} %get-tuple-element.23), channel_id=1, source_target_pairs={{0,120},{8,16},{16,8},{24,32},{32,24},{40,48},{48,40},{56,64},{64,... | collective-permute-start | bytes 1204232 | tf_op jit(solution)/shard_map/ppermute | solution.py:884
  29.8 0.0 collective-permute-done.2.near_a
  29.8 10.2 %collective-permute-done.3.far_a = f32[2,392,128]{2,1,0:T(8,128)S(1)} collective-permute-done((f32[2,392,128]{2,1,0:T(8,128)S(1)}, f32[2,392,128]{2,1,0:T(8,128)S(1)}, u32[]{:S(2)}, u32[]{:S(2)}) %collective-permute-start.3) | collective-permute-done | bytes 401440 | tf_op jit(solution)/shard_map/ppermute | solution.py:884
  40.0 0.0 copy-done.11
  40.0 5.5 %shard_map.106 = (f32[19,8,16,256]{3,2,1,0:T(8,128)}, f32[128,1,128]{2,1,0:T(1,128)}) custom-call(f32[19,8,2,32,128]{4,3,2,1,0:T(8,128)S(1)} %get-tuple-element.20.ext, f32[3,8,2,32,128]{4,3,2,1,0:T(8,128)S(1)} %get-tuple-element.21.own_opened, f32[2,392,128]{2,1,0:T(8,128)S(1)} %collective-permute-done.2.near_a, ...), custom_call_target="tpu_custom_call" | custom-call | bytes 16777216 | tf_op jit(solution)/shard_map/pallas_call | solution.py:876
  45.5 7.3 %all-to-all-start = ((f32[128,1,128]{2,1,0:T(1,128)}), f32[128,1,128]{2,1,0:T(1,128)S(1)}, u32[]{:S(2)}, u32[]{:S(2)}) async-start(f32[128,1,128]{2,1,0:T(1,128)} %get-tuple-element.30), calls=%async_computation | async-start | bytes 131072 | tf_op jit(solution)/shard_map/all_to_all | solution.py:962
  52.9 3.9 %shard_map.107 = (f32[16,16,256]{2,1,0:T(8,128)S(1)}, f32[22,2,32,128]{3,2,1,0:T(8,128)S(1)}, f32[22,2,32,128]{3,2,1,0:T(8,128)S(1)}, f32[22,2,32,128]{3,2,1,0:T...) custom-call(f32[16,16,256]{2,1,0:T(8,128)S(1)} %copy-done, s32[16,16,256]{2,1,0:T(8,128)S(1)} %copy-done.1, ...), custom_call_target="tpu_custom_call" | custom-call | bytes 8388608 | tf_op jit(solution)/shard_map/pallas_call | solution.py:876
  56.7 0.9 %copy-done.2 = f32[22,2,32,128]{3,2,1,0:T(8,128)} copy-done((f32[22,2,32,128]{3,2,1,0:T(8,128)}, f32[22,2,32,128]{3,2,1,0:T(8,128)S(1)}, u32[]{:S(2)}) %copy-start.2) | copy-done | bytes 720920
  57.6 0.9 %copy-done.3 = f32[22,2,32,128]{3,2,1,0:T(8,128)} copy-done((f32[22,2,32,128]{3,2,1,0:T(8,128)}, f32[22,2,32,128]{3,2,1,0:T(8,128)S(1)}, u32[]{:S(2)}) %copy-start.3) | copy-done | bytes 720920
  58.5 0.9 %copy-done.4 = f32[22,2,32,128]{3,2,1,0:T(8,128)} copy-done((f32[22,2,32,128]{3,2,1,0:T(8,128)}, f32[22,2,32,128]{3,2,1,0:T(8,128)S(1)}, u32[]{:S(2)}) %copy-start.4) | copy-done | bytes 720920
  59.4 0.9 %copy-done.5 = f32[22,2,32,128]{3,2,1,0:T(8,128)} copy-done((f32[22,2,32,128]{3,2,1,0:T(8,128)}, f32[22,2,32,128]{3,2,1,0:T(8,128)S(1)}, u32[]{:S(2)}) %copy-start.5) | copy-done | bytes 720920
  60.2 0.7 %copy-done.7 = f32[16,16,256]{2,1,0:T(8,128)} copy-done((f32[16,16,256]{2,1,0:T(8,128)}, f32[16,16,256]{2,1,0:T(8,128)S(1)}, u32[]{:S(2)}) %copy-start.7) | copy-done | bytes 262168
  60.9 1.6 %all-to-all-done.arrived = f32[128,1,128]{2,1,0:T(1,128)S(1)} async-done(((f32[128,1,128]{2,1,0:T(1,128)}), f32[128,1,128]{2,1,0:T(1,128)S(1)}, u32[]{:S(2)}, u32[]{:S(2)}) %all-to-all-start) | async-done | bytes 65568 | tf_op jit(solution)/shard_map/all_to_all | solution.py:962
  62.5 4.9 %shard_map.108 = f32[16,16,256]{2,1,0:T(8,128)} custom-call(f32[16,16,256]{2,1,0:T(8,128)} %copy-done.7, f32[22,2,32,128]{3,2,1,0:T(8,128)} %copy-done.2, f32[22,2,32,128]{3,2,1,0:T(8,128)} %copy-done.3, f32[22,2,32,128]{3,2,1,0:T(8,128)} %copy-done.4, f32[22,2,32,128]{3,2,1,0:T(8,128)} %copy-done.5, f32[128,1,128]{2,1,0:T(1,128)S(1)} %all-to-all-done.arrived, ...), custom_call_target="tpu_custom_call" | custom-call | bytes 8388608 | tf_op jit(solution)/shard_map/pallas_call | solution.py:876
  (9 shorter events, 0.1 us)
Async XLA Ops:
  0.6 23.3 %copy-start = (f32[16,16,256]{2,1,0:T(8,128)S(1)}, f32[16,16,256]{2,1,0:T(8,128)}, u32[]{:S(2)}) copy-start(f32[16,16,256]{2,1,0:T(8,128)} %temp.3) | copy-start | bytes 786436
  0.6 23.3 %copy-start.1 = (s32[16,16,256]{2,1,0:T(8,128)S(1)}, s32[16,16,256]{2,1,0:T(8,128)}, u32[]{:S(2)}) copy-start(s32[16,16,256]{2,1,0:T(8,128)} %mat.3) | copy-start | bytes 786436
  0.7 23.3 %copy-start.6 = (s32[8,16,256]{2,1,0:T(8,128)S(1)}, s32[8,16,256]{2,1,0:T(8,128)}, u32[]{:S(2)}) copy-start(s32[8,16,256]{2,1,0:T(8,128)} %flags.1) | copy-start | bytes 393220
  4.3 35.8 %copy-start.8 = (s32[512]{0:T(512)S(1)}, s32[512]{0:T(512)}, u32[]{:S(2)}) copy-start(s32[512]{0:T(512)} %param.11) | copy-start | bytes 6148
  4.3 35.8 %copy-start.9 = (f32[512]{0:T(512)S(1)}, f32[512]{0:T(512)}, u32[]{:S(2)}) copy-start(f32[512]{0:T(512)} %param.12) | copy-start | bytes 6148
  4.3 35.8 %copy-start.10 = (s32[512]{0:T(512)S(1)}, s32[512]{0:T(512)}, u32[]{:S(2)}) copy-start(s32[512]{0:T(512)} %param.13) | copy-start | bytes 6148
  4.3 35.8 %copy-start.11 = (s32[512]{0:T(512)S(1)}, s32[512]{0:T(512)}, u32[]{:S(2)}) copy-start(s32[512]{0:T(512)} %param.14) | copy-start | bytes 6148
  4.3 9.1 %collective-permute-start = (f32[2,312,128]{2,1,0:T(8,128)S(1)}, f32[2,312,128]{2,1,0:T(8,128)S(1)}, u32[]{:S(2)}, u32[]{:S(2)}) collective-permute-start(f32[2,312,128]{2,1,0:T(8,128)S(1)} %get-tuple-element.18), channel_id=1, source_target_pairs={{0,1},{1,0},{2,3},{3,2},{4,5},{5,4},{6,7},{7,6},{8,9},{9,8},{10,11... | collective-permute-start | bytes 958472 | tf_op jit(solution)/shard_map/ppermute | solution.py:884
  6.5 17.4 %collective-permute-start.1 = (f32[2,312,128]{2,1,0:T(8,128)S(1)}, f32[2,312,128]{2,1,0:T(8,128)S(1)}, u32[]{:S(2)}, u32[]{:S(2)}) collective-permute-start(f32[2,312,128]{2,1,0:T(8,128)S(1)} %get-tuple-element.19), channel_id=1, source_target_pairs={{0,7},{1,2},{2,1},{3,4},{4,3},{5,6},{6,5},{7,0},{8,15},{9,10},{10,... | collective-permute-start | bytes 958472 | tf_op jit(solution)/shard_map/ppermute | solution.py:884
  25.3 4.5 %collective-permute-start.2 = (f32[2,392,128]{2,1,0:T(8,128)S(1)}, f32[2,392,128]{2,1,0:T(8,128)S(1)}, u32[]{:S(2)}, u32[]{:S(2)}) collective-permute-start(f32[2,392,128]{2,1,0:T(8,128)S(1)} %get-tuple-element.22), channel_id=1, source_target_pairs={{0,8},{8,0},{16,24},{24,16},{32,40},{40,32},{48,56},{56,48},{64,72... | collective-permute-start | bytes 1204232 | tf_op jit(solution)/shard_map/ppermute | solution.py:884
  26.9 13.1 %collective-permute-start.3 = (f32[2,392,128]{2,1,0:T(8,128)S(1)}, f32[2,392,128]{2,1,0:T(8,128)S(1)}, u32[]{:S(2)}, u32[]{:S(2)}) collective-permute-start(f32[2,392,128]{2,1,0:T(8,128)S(1)} %get-tuple-element.23), channel_id=1, source_target_pairs={{0,120},{8,16},{16,8},{24,32},{32,24},{40,48},{48,40},{56,64},{64,... | collective-permute-start | bytes 1204232 | tf_op jit(solution)/shard_map/ppermute | solution.py:884
  45.5 17.0 %all-to-all-start = ((f32[128,1,128]{2,1,0:T(1,128)}), f32[128,1,128]{2,1,0:T(1,128)S(1)}, u32[]{:S(2)}, u32[]{:S(2)}) async-start(f32[128,1,128]{2,1,0:T(1,128)} %get-tuple-element.30), calls=%async_computation | async-start | bytes 131072 | tf_op jit(solution)/shard_map/all_to_all | solution.py:962
  56.7 0.9 %copy-start.2 = (f32[22,2,32,128]{3,2,1,0:T(8,128)}, f32[22,2,32,128]{3,2,1,0:T(8,128)S(1)}, u32[]{:S(2)}) copy-start(f32[22,2,32,128]{3,2,1,0:T(8,128)S(1)} %get-tuple-element.26.link_a_far) | copy-start | bytes 2162692
  57.6 0.9 %copy-start.3 = (f32[22,2,32,128]{3,2,1,0:T(8,128)}, f32[22,2,32,128]{3,2,1,0:T(8,128)S(1)}, u32[]{:S(2)}) copy-start(f32[22,2,32,128]{3,2,1,0:T(8,128)S(1)} %get-tuple-element.27.link_z_far) | copy-start | bytes 2162692
  58.5 0.9 %copy-start.4 = (f32[22,2,32,128]{3,2,1,0:T(8,128)}, f32[22,2,32,128]{3,2,1,0:T(8,128)S(1)}, u32[]{:S(2)}) copy-start(f32[22,2,32,128]{3,2,1,0:T(8,128)S(1)} %get-tuple-element.28.link_r_far) | copy-start | bytes 2162692
  59.4 0.9 %copy-start.5 = (f32[22,2,32,128]{3,2,1,0:T(8,128)}, f32[22,2,32,128]{3,2,1,0:T(8,128)S(1)}, u32[]{:S(2)}) copy-start(f32[22,2,32,128]{3,2,1,0:T(8,128)S(1)} %get-tuple-element.29.keep_far) | copy-start | bytes 2162692
  60.2 0.7 %copy-start.7 = (f32[16,16,256]{2,1,0:T(8,128)}, f32[16,16,256]{2,1,0:T(8,128)S(1)}, u32[]{:S(2)}) copy-start(f32[16,16,256]{2,1,0:T(8,128)S(1)} %get-tuple-element.25.swept_far) | copy-start | bytes 786436

commit v2 on v1

--- a/solution.py
+++ b/solution.py
@@ -27,17 +27,18 @@
 ROWS = 32
 
 PER_PLACE = 26
-TEMP_ROW = 208
-COND_ROW = 256
-TAIL_ROW = 304
-AXIAL_ROWS = 312
+AXIAL_ROWS = CA * PER_PLACE
 STREAMED_ROW = 100
 SUMS_ROW = 190
 FLAG_ROW = 244
-SOLID_ROW = 264
-SOLID_SKIP = (0, 20, 38, 54)
-CELL_ROW = 376
-AZIM_ROWS = 392
+AZIM_ROWS = 264
+SOLID_COND = 48
+SOLID_CELLS = 96
+SOLID_ROWS = 104
+SKIP = (0, 20, 38)
+END_COND = 54
+END_CELLS = 112
+END_ROWS = 128
 
 VMEM = pltpu.VMEM
 f32 = jnp.float32
@@ -111,40 +112,17 @@
         body(far, near)
 
 
-def first_kernel(
-    f_far,
-    flags_far,
-    temp_far,
-    mat_far,
-    cells,
-    post,
-    near,
-    far,
-    f,
-    flags,
-    temp,
-    mat,
-    low,
-    high,
-    layers_in,
-    others_in,
-):
-    others = [
-        pltpu.make_async_copy(source, target, others_in.at[n])
-        for n, (source, target) in enumerate(
-            ((flags_far, flags), (temp_far, temp), (mat_far, mat))
-        )
-    ]
+def first_kernel(f_far, flags_far, post, near, far, token, f, flags, low, high, come):
+    flags_copy = pltpu.make_async_copy(flags_far, flags, come.at[CA])
 
     def layer_copy(a):
-        return pltpu.make_async_copy(f_far.at[:, a], f.at[:, a], layers_in.at[a])
-
-    others[0].start()
+        return pltpu.make_async_copy(f_far.at[:, a], f.at[:, a], come.at[a])
+
+    flags_copy.start()
     for a in range(CA):
         layer_copy(a).start()
-    others[1].start()
-    others[2].start()
-    others[0].wait()
+    token[...] = jnp.zeros((8, 128), f32)
+    flags_copy.wait()
 
     def layer(a, carry):
         layer_copy(a).wait()
@@ -172,10 +150,85 @@
         return carry
 
     lax.fori_loop(0, CA, layer, 0)
-    others[1].wait()
-    others[2].wait()
-
-    def solid_layer(a, carry):
+
+    def hand_over(down, up):
+        down[...] = low[...]
+        up[...] = high[...]
+
+    by_parity("axial", hand_over, near, far)
+
+
+def solid_azim_kernel(temp_far, mat_far, cells, token, near, far, temp, mat, come):
+    copies = []
+    for n, layers in enumerate((pl.ds(0, 3), pl.ds(SA - 3, 3))):
+        for k, (source, target) in enumerate(((temp_far, temp), (mat_far, mat))):
+            copy = pltpu.make_async_copy(
+                source.at[layers], target.at[n], come.at[2 * n + k]
+            )
+            copy.start()
+            copies.append(copy)
+    for copy in copies:
+        copy.wait()
+
+    def fill(down, up):
+        for side, target in enumerate((down, up)):
+            for half in HALVES:
+                for n in range(3):
+                    a = n if side == 0 else 2 - n
+                    target[half, pl.ds(16 * n, 16), :] = temp[side, a, :, lanes(half)]
+                    target[half, pl.ds(SOLID_COND + 16 * n, 16), :] = conductivity(
+                        mat[side, a, :, lanes(half)]
+                    )
+            target[0, pl.ds(SOLID_CELLS, 8), :] = cells[...].astype(f32)
+
+    by_parity("azim", fill, near, far)
+
+
+def solid_axial_kernel(
+    temp_far,
+    mat_far,
+    cells,
+    near_s,
+    far_s,
+    token,
+    near,
+    far,
+    temp,
+    mat,
+    low,
+    high,
+    come,
+):
+    copies = [
+        pltpu.make_async_copy(source, target, come.at[n])
+        for n, (source, target) in enumerate(((temp_far, temp), (mat_far, mat)))
+    ]
+    for copy in copies:
+        copy.start()
+
+    def azim_ends(lower, upper):
+        for target, edge, step in ((low, 0, 1), (high, SZ - 1, -1)):
+            for half in HALVES:
+                for depth in range(2):
+                    z = edge + step * depth
+                    for n in range(2 - depth):
+                        for source, at in (
+                            (lower, 1 - depth - n),
+                            (upper, 18 - depth + n),
+                        ):
+                            for kind, here in ((0, 0), (END_COND, SOLID_COND)):
+                                target[half, pl.ds(kind + SKIP[depth] + at, 1), :] = (
+                                    source[half, pl.ds(here + 16 * n + z, 1), :]
+                                )
+            target[0, pl.ds(END_CELLS, 8), :] = cells[...].astype(f32)
+            target[1, pl.ds(END_CELLS, 8), :] = lower[0, pl.ds(SOLID_CELLS, 8), :]
+            target[0, pl.ds(END_CELLS + 8, 8), :] = upper[0, pl.ds(SOLID_CELLS, 8), :]
+
+    by_parity("azim", azim_ends, near_s, far_s)
+    for copy in copies:
+        copy.wait()
+
+    def layer(a, carry):
         for half in HALVES:
             for part, target in ((0, low), (1, high)):
                 rows = pl.ds(8 * part, 8)
@@ -183,18 +236,12 @@
                 c = conductivity(mat[a, rows, lanes(half)])
                 for depth in range(3):
                     at = depth if part == 0 else 7 - depth
-                    target[half, pl.ds(TEMP_ROW + depth * SA + a, 1), :] = t[
-                        at : at + 1
-                    ]
-                    target[half, pl.ds(COND_ROW + depth * SA + a, 1), :] = c[
-                        at : at + 1
-                    ]
-        return carry
-
-    lax.fori_loop(0, SA, solid_layer, 0, unroll=4)
-    rc = cells[...].astype(f32)
-    low[0, pl.ds(TAIL_ROW, 8), :] = rc
-    high[0, pl.ds(TAIL_ROW, 8), :] = rc
+                    row = SKIP[depth] + 2 - depth + a
+                    target[half, pl.ds(row, 1), :] = t[at : at + 1]
+                    target[half, pl.ds(END_COND + row, 1), :] = c[at : at + 1]
+        return carry
+
+    lax.fori_loop(0, SA, layer, 0, unroll=4)
 
     def hand_over(down, up):
         down[...] = low[...]
@@ -270,18 +317,17 @@
     n_axial,
     post,
     flags,
-    temp,
-    mat,
-    cells,
     near_z,
     far_z,
     ext,
     opened,
     near,
     far,
+    token,
     low,
     high,
 ):
+    token[...] = jnp.zeros((8, 128), f32)
     lane = lax.broadcasted_iota(jnp.int32, (8, 128), 1)
     below, above = ends(n_axial)
 
@@ -318,38 +364,6 @@
             return carry
 
         lax.fori_loop(0, CA, layer, 0, unroll=2)
-        own = cells[...].astype(f32)
-        outside = jnp.full((CAP, 128), SA * SZ * NR, f32)
-        for target, first, step in ((low, 0, 1), (high, SA - 1, -1)):
-            for half in HALVES:
-                for n in range(3):
-                    a = first + step * n
-                    at = SOLID_ROW + SOLID_SKIP[n]
-                    target[half, pl.ds(at + 2 - n, 16), :] = temp[a, :, lanes(half)]
-                    target[half, pl.ds(at + 56 - n, 16), :] = conductivity(
-                        mat[a, :, lanes(half)]
-                    )
-                    for depth in range(2 - n):
-                        for source, row, there in (
-                            (lower, at + 1 - n - depth, below),
-                            (upper, at + 18 - n + depth, above),
-                        ):
-                            target[half, pl.ds(row, 1), :] = source[
-                                half, pl.ds(TEMP_ROW + depth * SA + a, 1), :
-                            ]
-                            target[half, pl.ds(row + 54, 1), :] = (
-                                source[half, pl.ds(COND_ROW + depth * SA + a, 1), :]
-                                * there
-                            )
-            target[0, pl.ds(CELL_ROW, 8), :] = own
-            for half, row, source, there in (
-                (1, CELL_ROW, lower, below),
-                (0, CELL_ROW + 8, upper, above),
-            ):
-                target[half, pl.ds(row, 8), :] = jnp.where(
-                    there > 0, source[0, pl.ds(TAIL_ROW, 8), :], outside
-                )
-
     by_parity("axial", axial_rim, near_z, far_z)
 
     def turn(a, carry):
@@ -598,10 +612,10 @@
     n_axial,
     temp,
     mat,
-    near_a,
-    far_a,
-    near_z,
-    far_z,
+    near_s,
+    far_s,
+    near_e,
+    far_e,
     cells,
     swept,
     link_a,
@@ -630,42 +644,38 @@
         for half in HALVES:
             for n in range(3):
                 for source, a in ((lower, 2 - n), (upper, 19 + n)):
-                    at = SOLID_ROW + SOLID_SKIP[n]
-                    rows = pl.ds(6 + n, 20 - 2 * n)
-                    ext[a, half, rows, :] = source[half, pl.ds(at, 20 - 2 * n), :]
-                    cond[a, half, rows, :] = source[half, pl.ds(at + 54, 20 - 2 * n), :]
-        for source, which in ((lower, 0), (upper, 6)):
-            all_cells[which + 1] = source[0, pl.ds(CELL_ROW, 8), :]
-            all_cells[which] = source[1, pl.ds(CELL_ROW, 8), :]
-            all_cells[which + 2] = source[0, pl.ds(CELL_ROW + 8, 8), :]
-
-    by_parity("azim", azim_rim, near_a, far_a)
+                    ext[a, half, pl.ds(8, 16), :] = source[half, pl.ds(16 * n, 16), :]
+                    cond[a, half, pl.ds(8, 16), :] = source[
+                        half, pl.ds(SOLID_COND + 16 * n, 16), :
+                    ]
+        all_cells[1] = lower[0, pl.ds(SOLID_CELLS, 8), :]
+        all_cells[7] = upper[0, pl.ds(SOLID_CELLS, 8), :]
+
+    by_parity("azim", azim_rim, near_s, far_s)
     below, above = ends(n_axial)
 
     def axial_rim(lower, upper):
-        def layer(a, carry):
-            for half in HALVES:
-                for depth in range(3):
+        for half in HALVES:
+            for depth in range(3):
+                for n in range(20 - 2 * depth):
+                    a = 1 + depth + n
+                    at = SKIP[depth] + n
                     for source, row, there in (
                         (lower, 7 - depth, below),
                         (upper, 24 + depth, above),
                     ):
-                        ext[a + 3, half, pl.ds(row, 1), :] = source[
-                            half, pl.ds(TEMP_ROW + depth * SA + a, 1), :
-                        ]
-                        cond[a + 3, half, pl.ds(row, 1), :] = (
-                            source[half, pl.ds(COND_ROW + depth * SA + a, 1), :] * there
+                        ext[a, half, pl.ds(row, 1), :] = source[half, pl.ds(at, 1), :]
+                        cond[a, half, pl.ds(row, 1), :] = (
+                            source[half, pl.ds(END_COND + at, 1), :] * there
                         )
-            return carry
-
-        lax.fori_loop(0, SA, layer, 0, unroll=4)
         outside = jnp.full((CAP, 128), SA * SZ * NR, f32)
-        for source, which, there in ((lower, 3, below), (upper, 5, above)):
-            all_cells[which] = jnp.where(
-                there > 0, source[0, pl.ds(TAIL_ROW, 8), :], outside
-            )
-
-    by_parity("axial", axial_rim, near_z, far_z)
+        for source, dz, there in ((lower, 0, below), (upper, 2, above)):
+            for which, half, row in ((0, 1, 0), (3, 0, 0), (6, 0, 8)):
+                all_cells[which + dz] = jnp.where(
+                    there > 0, source[half, pl.ds(END_CELLS + row, 8), :], outside
+                )
+
+    by_parity("axial", axial_rim, near_e, far_e)
     all_cells[4] = cells[...].astype(f32)
 
     def links(a, carry):
@@ -786,17 +796,13 @@
                     jnp.where(hit, term[c : c + 1].astype(f32), 0.0).astype(bf16)
                 )
             right.append((at_col == cell[c : c + 1] % NR).astype(f32).astype(bf16))
-        right = jnp.concatenate(right, axis=1)
-        total = None
-        for to in left:
-            part = lax.dot_general(
-                jnp.concatenate(to, axis=1),
-                right,
-                (((1,), (1,)), ((), ())),
-                preferred_element_type=f32,
-            )
-            total = part if total is None else total + part
-        return total
+        both = lax.dot_general(
+            jnp.concatenate([jnp.concatenate(to, axis=1) for to in left], axis=0),
+            jnp.concatenate(right, axis=1),
+            (((1,), (1,)), ((), ())),
+            preferred_element_type=f32,
+        )
+        return both[:rows] + both[rows:]
 
     own = place(4, SA * SZ, lambda j: j)
     for a in range(SA):
@@ -857,11 +863,16 @@
     lax.fori_loop(0, SA, final, 0, unroll=4)
 
 
-def call(kernel, ins, outs, scratch=(), limit=16, moved=0, far_ins=0, far_outs=0):
+def call(
+    kernel, ins, outs, scratch=(), limit=16, moved=0, far_ins=0, far_outs=0, held=()
+):
     here, there = (pl.BlockSpec(memory_space=m) for m in (VMEM, pltpu.HBM))
     kernel_call = pl.pallas_call(
         kernel,
-        out_shape=[jax.ShapeDtypeStruct(s, f32) for s in outs],
+        out_shape=[
+            VMEM(s, f32) if n in held else jax.ShapeDtypeStruct(s, f32)
+            for n, s in enumerate(outs)
+        ],
         in_specs=[there] * far_ins + [here] * (ins - far_ins),
         out_specs=[there] * far_outs + [here] * (len(outs) - far_outs),
         scratch_shapes=list(scratch),
@@ -901,38 +912,71 @@
     cells = receive_cell.reshape(devices, CAP).T
     azim_msg = (2, AZIM_ROWS, 128)
     axial_msg = (2, AXIAL_ROWS, 128)
+    solid_msg = (2, SOLID_ROWS, 128)
+    end_msg = (2, END_ROWS, 128)
     fluid = (Q, CA, CZ, NR)
     solid = (SA, SZ, NR)
     fluid_ext = (Q, CA, 2, ROWS, 128)
     solid_ext = (SA + 6, 2, ROWS, 128)
-    post, near_z, far_z = call(
+    post, near_z, far_z, token = call(
         first_kernel,
-        5,
-        [fluid, axial_msg, axial_msg],
+        2,
+        [fluid, axial_msg, axial_msg, (8, 128)],
         [
             VMEM(fluid, f32),
             VMEM((CA, CZ, NR), jnp.int32),
+            VMEM(axial_msg, f32),
+            VMEM(axial_msg, f32),
+            pltpu.SemaphoreType.DMA((CA + 1,)),
+        ],
+        moved=8 << 20,
+        far_ins=2,
+    )(populations, fluid_flags)
+    near_z = swap(near_z, "axial", False)
+    far_z = swap(far_z, "axial", True)
+    near_s, far_s = call(
+        solid_azim_kernel,
+        4,
+        [solid_msg, solid_msg],
+        [
+            VMEM((2, 3, SZ, NR), f32),
+            VMEM((2, 3, SZ, NR), jnp.int32),
+            pltpu.SemaphoreType.DMA((4,)),
+        ],
+        moved=2 << 20,
+        far_ins=2,
+    )(solid_temp, materials, cells, token)
+    near_s = swap(near_s, "azim", False)
+    far_s = swap(far_s, "azim", True)
+    near_z, far_z, near_s, far_s = lax.optimization_barrier(
+        (near_z, far_z, near_s, far_s)
+    )
+    ext, opened, near_a, far_a, token = call(
+        functools.partial(rim_kernel, n_axial),
+        4,
+        [fluid_ext, (3, CA, 2, ROWS, 128), azim_msg, azim_msg, (8, 128)],
+        [VMEM(azim_msg, f32), VMEM(azim_msg, f32)],
+        moved=8 << 20,
+        held=(0, 1),
+    )(post, fluid_flags, near_z, far_z)
+    near_a = swap(near_a, "azim", False)
+    far_a = swap(far_a, "azim", True)
+    near_e, far_e = call(
+        solid_axial_kernel,
+        6,
+        [end_msg, end_msg],
+        [
             VMEM(solid, f32),
             VMEM(solid, jnp.int32),
-            VMEM(axial_msg, f32),
-            VMEM(axial_msg, f32),
-            pltpu.SemaphoreType.DMA((CA,)),
-            pltpu.SemaphoreType.DMA((3,)),
+            VMEM(end_msg, f32),
+            VMEM(end_msg, f32),
+            pltpu.SemaphoreType.DMA((2,)),
         ],
-        moved=8 << 20,
-        far_ins=4,
-    )(populations, fluid_flags, solid_temp, materials, cells)
-    near_z = swap(near_z, "axial", False)
-    far_z = swap(far_z, "axial", True)
-    ext, opened, near_a, far_a = call(
-        functools.partial(rim_kernel, n_axial),
-        7,
-        [fluid_ext, (3, CA, 2, ROWS, 128), azim_msg, azim_msg],
-        [VMEM(azim_msg, f32), VMEM(azim_msg, f32)],
-        moved=8 << 20,
-    )(post, fluid_flags, solid_temp, materials, cells, near_z, far_z)
-    near_a = swap(near_a, "azim", False)
-    far_a = swap(far_a, "azim", True)
+        moved=2 << 20,
+        far_ins=2,
+    )(solid_temp, materials, cells, near_s, far_s, token)
+    near_e = swap(near_e, "axial", False)
+    far_e = swap(far_e, "axial", True)
     rows = wall_cell.shape[0]
     fluid_out, message = call(
         functools.partial(fluid_kernel, n_azim, n_axial),
@@ -950,8 +994,8 @@
         moved=16 << 20,
         far_outs=1,
     )(
-        ext,
-        opened,
+        pltpu.with_memory_space_constraint(ext, VMEM),
+        pltpu.with_memory_space_constraint(opened, VMEM),
         near_a,
         far_a,
         wall_cell.reshape(1, rows),
@@ -968,7 +1012,7 @@
         [solid] + [solid_ext] * 4 + [(9, CAP, devices)],
         [VMEM(solid_ext, f32)] * 3,
         moved=8 << 20,
-    )(solid_temp, materials, near_a, far_a, near_z, far_z, cells)
+    )(solid_temp, materials, near_s, far_s, near_e, far_e, cells)
     (solid_out,) = call(
         deposit_kernel,
         7,

time: 67.6 us -> 62.3 us (0.922)
  waiting for transfers between devices: 25.6 us -> 14 us
  starting transfers between devices: 17.7 us -> 23.3 us
  Pallas kernels: 18.3 us -> 19.5 us
  local copies, waits for them, and re-layouts: 5.1 us -> 4.37 us
    ppermute x4 -> x8, waiting for transfers between devices: 24 us -> 12.5 us  [swap(): return lax.ppermute(values, axis, pairs)]
    ppermute x4 -> x8, starting transfers between devices: 10.4 us -> 15.9 us  [swap(): return lax.ppermute(values, axis, pairs)]
    pallas_call x5 -> x7, Pallas kernels: 18.3 us -> 19.5 us  [run(): return kernel_call(*far, *args[far_ins:])]
    reshape x2, local copies, waits for them, and re-layouts: 0.87 us -> 0.13 us  [per_device(): cells = receive_cell.reshape(devices, CAP).T]
    unnamed x24 -> x26, local copies, waits for them, and re-layouts: 4.23 us -> 4.24 us
  transfers between devices with their start and end apart: 5 -> 9, of which waited for: 4 -> 3; matrix products, arithmetic and copies ran while one was open for 0% -> 0% of each run, Pallas kernels for 6% -> 18%
where the time goes in v2:
time: 62.3 us; the launch traced here: 62 us
  starting transfers between devices  23.3 us (37%)
  Pallas kernels  19.5 us (31%)
  waiting for transfers between devices  14 us (22%)
  local copies, waits for them, and re-layouts  4.37 us (7%)
  between operations  0.83 us (1%)
    pallas_call x7, Pallas kernels, run(): return kernel_call(*far, *args[far_ins:])  19.5 us
    ppermute x8, starting transfers between devices, swap(): return lax.ppermute(values, axis, pairs)  15.9 us
    ppermute x8, waiting for transfers between devices, swap(): return lax.ppermute(values, axis, pairs)  12.5 us
    all_to_all x1, starting transfers between devices, per_device(): lax.all_to_all(message, ('azim', 'axial'), split_axis=0, concat_axis=0, t...  7.42 us
    unnamed x26, local copies, waits for them, and re-layouts  4.24 us
    all_to_all x1, waiting for transfers between devices, per_device(): lax.all_to_all(message, ('azim', 'axial'), split_axis=0, concat_axis=0, t...  1.53 us
  transfers between devices with their start and end apart: 9, of which 3 were waited for; matrix products, arithmetic and copies ran while one was open for 0% of the time, Pallas kernels for 18%

profile of v2, /device:TPU:1, one launch (start us, length us, event | category | flops | bytes accessed | tf_op | source)
XLA Modules:
  0.0 62.0 jit_solution(3546606380015721126)
XLA Ops:
  0.6 2.9 %shard_map.104 = (f32[19,8,16,256]{3,2,1,0:T(8,128)S(1)}, f32[2,208,128]{2,1,0:T(8,128)}, f32[2,208,128]{2,1,0:T(8,128)S(1)}, f32[8,128]{1,0:T(8,128)S(1)}) custom-call(f32[19,8,16,256]{3,2,1,0:T(8,128)} %f_far.1, s32[8,16,256]{2,1,0:T(8,128)} %flags.1), custom_call_target="tpu_custom_call" | custom-call | bytes 8388608 | tf_op jit(solution)/shard_map/pallas_call | solution.py:887
  3.5 0.0 copy-start.8
  3.5 0.0 copy-start.9
  3.6 0.0 copy-start.10
  3.6 0.0 copy-start.11
  3.6 2.2 %collective-permute-start = (f32[2,208,128]{2,1,0:T(8,128)}, f32[2,208,128]{2,1,0:T(8,128)S(1)}, u32[]{:S(2)}, u32[]{:S(2)}) collective-permute-start(f32[2,208,128]{2,1,0:T(8,128)} %get-tuple-element.28), channel_id=1, source_target_pairs={{0,1},{1,0},{2,3},{3,2},{4,5},{5,4},{6,7},{7,6},{8,9},{9,8},{10,11... | collective-permute-start | bytes 638984 | tf_op jit(solution)/shard_map/ppermute | solution.py:895
  5.8 3.6 %collective-permute-start.1 = (f32[2,208,128]{2,1,0:T(8,128)S(1)}, f32[2,208,128]{2,1,0:T(8,128)S(1)}, u32[]{:S(2)}, u32[]{:S(2)}) collective-permute-start(f32[2,208,128]{2,1,0:T(8,128)S(1)} %get-tuple-element.29), channel_id=1, source_target_pairs={{0,7},{1,2},{2,1},{3,4},{4,3},{5,6},{6,5},{7,0},{8,15},{9,10},{10,... | collective-permute-start | bytes 638984 | tf_op jit(solution)/shard_map/ppermute | solution.py:895
  9.4 0.1 reshape.19
  9.6 1.0 %shard_map.105 = (f32[2,104,128]{2,1,0:T(8,128)S(1)}, f32[2,104,128]{2,1,0:T(8,128)S(1)}) custom-call(f32[16,16,256]{2,1,0:T(8,128)} %temp.1, s32[16,16,256]{2,1,0:T(8,128)} %mat.1, s32[8,128]{1,0:T(8,128)S(1)} %bitcast.5, f32[8,128]{1,0:T(8,128)S(1)} %get-tuple-element.30.token), custom_call_target="tpu_custom_call" | custom-call | bytes 2097152 | tf_op jit(solution)/shard_map/pallas_call | solution.py:887
  10.5 1.3 %collective-permute-start.2 = (f32[2,104,128]{2,1,0:T(8,128)S(1)}, f32[2,104,128]{2,1,0:T(8,128)S(1)}, u32[]{:S(2)}, u32[]{:S(2)}) collective-permute-start(f32[2,104,128]{2,1,0:T(8,128)S(1)} %get-tuple-element.31), channel_id=1, source_target_pairs={{0,8},{8,0},{16,24},{24,16},{32,40},{40,32},{48,56},{56,48},{64,72... | collective-permute-start | bytes 319496 | tf_op jit(solution)/shard_map/ppermute | solution.py:895
  11.8 2.9 %collective-permute-start.3 = (f32[2,104,128]{2,1,0:T(8,128)S(1)}, f32[2,104,128]{2,1,0:T(8,128)S(1)}, u32[]{:S(2)}, u32[]{:S(2)}) collective-permute-start(f32[2,104,128]{2,1,0:T(8,128)S(1)} %get-tuple-element.32), channel_id=1, source_target_pairs={{0,120},{8,16},{16,8},{24,32},{32,24},{40,48},{48,40},{56,64},{64,... | collective-permute-start | bytes 319496 | tf_op jit(solution)/shard_map/ppermute | solution.py:895
  14.7 0.0 collective-permute-done.2.near_s
  14.7 6.5 %collective-permute-done.3.far_s = f32[2,104,128]{2,1,0:T(8,128)S(1)} collective-permute-done((f32[2,104,128]{2,1,0:T(8,128)S(1)}, f32[2,104,128]{2,1,0:T(8,128)S(1)}, u32[]{:S(2)}, u32[]{:S(2)}) %collective-permute-start.3) | collective-permute-done | bytes 106528 | tf_op jit(solution)/shard_map/ppermute | solution.py:895
  21.3 1.3 %shard_map.106 = (f32[19,8,2,32,128]{4,3,2,1,0:T(8,128)S(1)}, f32[3,8,2,32,128]{4,3,2,1,0:T(8,128)S(1)}, f32[2,264,128]{2,1,0:T(8,128)S(1)}, f32[2,264,128]{2,1,0:T(8,128)S(1)}, f32[8,128]{1,0:T(8,128)S(1)}) custom-call(f32[19,8,16,256]{3,2,1,0:T(8,128)S(1)} %get-tuple-element.27.post, s32[8,16,256]{2,1,0:T(8,128)S(1)} %copy-done.6, ...), custom_call_target="tpu_custom_call" | custom-call | bytes 8388608 | tf_op jit(solution)/shard_map/pallas_call | solution.py:887
  22.6 1.5 %collective-permute-start.4 = (f32[2,264,128]{2,1,0:T(8,128)S(1)}, f32[2,264,128]{2,1,0:T(8,128)S(1)}, u32[]{:S(2)}, u32[]{:S(2)}) collective-permute-start(f32[2,264,128]{2,1,0:T(8,128)S(1)} %get-tuple-element.37), channel_id=1, source_target_pairs={{0,8},{8,0},{16,24},{24,16},{32,40},{40,32},{48,56},{56,48},{64,72... | collective-permute-start | bytes 811016 | tf_op jit(solution)/shard_map/ppermute | solution.py:895
  24.1 1.8 %collective-permute-start.5 = (f32[2,264,128]{2,1,0:T(8,128)S(1)}, f32[2,264,128]{2,1,0:T(8,128)S(1)}, u32[]{:S(2)}, u32[]{:S(2)}) collective-permute-start(f32[2,264,128]{2,1,0:T(8,128)S(1)} %get-tuple-element.38), channel_id=1, source_target_pairs={{0,120},{8,16},{16,8},{24,32},{32,24},{40,48},{48,40},{56,64},{64,... | collective-permute-start | bytes 811016 | tf_op jit(solution)/shard_map/ppermute | solution.py:895
  25.8 1.2 %shard_map.108 = (f32[2,128,128]{2,1,0:T(8,128)S(1)}, f32[2,128,128]{2,1,0:T(8,128)S(1)}) custom-call(f32[16,16,256]{2,1,0:T(8,128)} %temp.1, s32[16,16,256]{2,1,0:T(8,128)} %mat.1, s32[8,128]{1,0:T(8,128)S(1)} %bitcast.6, f32[2,104,128]{2,1,0:T(8,128)S(1)} %collective-permute-done.2.near_s, f32[2,104,128]{2,1,0:T(8,128)S(1)} %collective-permute-done.3.far_s, ...), custom_call_target="tpu_custom_call" | custom-call | bytes 2097152 | tf_op jit(solution)/shard_map/pallas_call | solution.py:887
  27.0 0.1 collective-permute-start.6
  27.1 2.5 %collective-permute-start.7 = (f32[2,128,128]{2,1,0:T(8,128)S(1)}, f32[2,128,128]{2,1,0:T(8,128)S(1)}, u32[]{:S(2)}, u32[]{:S(2)}) collective-permute-start(f32[2,128,128]{2,1,0:T(8,128)S(1)} %get-tuple-element.44), channel_id=1, source_target_pairs={{0,7},{1,2},{2,1},{3,4},{4,3},{5,6},{6,5},{7,0},{8,15},{9,10},{10,... | collective-permute-start | bytes 393224 | tf_op jit(solution)/shard_map/ppermute | solution.py:895
  29.6 6.0 %collective-permute-done.5.far_a = f32[2,264,128]{2,1,0:T(8,128)S(1)} collective-permute-done((f32[2,264,128]{2,1,0:T(8,128)S(1)}, f32[2,264,128]{2,1,0:T(8,128)S(1)}, u32[]{:S(2)}, u32[]{:S(2)}) %collective-permute-start.5) | collective-permute-done | bytes 270368 | tf_op jit(solution)/shard_map/ppermute | solution.py:895
  35.6 0.0 copy-start
  35.6 0.0 copy-start.1
  35.6 5.5 %shard_map.107 = (f32[19,8,16,256]{3,2,1,0:T(8,128)}, f32[128,1,128]{2,1,0:T(1,128)}) custom-call(f32[19,8,2,32,128]{4,3,2,1,0:T(8,128)S(1)} %get-tuple-element.35.ext, f32[3,8,2,32,128]{4,3,2,1,0:T(8,128)S(1)} %get-tuple-element.36.own_opened, f32[2,264,128]{2,1,0:T(8,128)S(1)} %collective-permute-done.4.near_a, ...), custom_call_target="tpu_custom_call" | custom-call | bytes 16777216 | tf_op jit(solution)/shard_map/pallas_call | solution.py:887
  41.1 7.4 %all-to-all-start = ((f32[128,1,128]{2,1,0:T(1,128)}), f32[128,1,128]{2,1,0:T(1,128)S(1)}, u32[]{:S(2)}, u32[]{:S(2)}) async-start(f32[128,1,128]{2,1,0:T(1,128)} %get-tuple-element.50), calls=%async_computation | async-start | bytes 131072 | tf_op jit(solution)/shard_map/all_to_all | solution.py:1006
  48.5 3.8 %shard_map.109 = (f32[16,16,256]{2,1,0:T(8,128)S(1)}, f32[22,2,32,128]{3,2,1,0:T(8,128)S(1)}, f32[22,2,32,128]{3,2,1,0:T(8,128)S(1)}, f32[22,2,32,128]{3,2,1,0:T...) custom-call(f32[16,16,256]{2,1,0:T(8,128)S(1)} %copy-done, s32[16,16,256]{2,1,0:T(8,128)S(1)} %copy-done.1, ...), custom_call_target="tpu_custom_call" | custom-call | bytes 8388608 | tf_op jit(solution)/shard_map/pallas_call | solution.py:887
  52.4 0.9 %copy-done.2 = f32[22,2,32,128]{3,2,1,0:T(8,128)} copy-done((f32[22,2,32,128]{3,2,1,0:T(8,128)}, f32[22,2,32,128]{3,2,1,0:T(8,128)S(1)}, u32[]{:S(2)}) %copy-start.2) | copy-done | bytes 720920
  53.3 0.9 %copy-done.3 = f32[22,2,32,128]{3,2,1,0:T(8,128)} copy-done((f32[22,2,32,128]{3,2,1,0:T(8,128)}, f32[22,2,32,128]{3,2,1,0:T(8,128)S(1)}, u32[]{:S(2)}) %copy-start.3) | copy-done | bytes 720920
  54.2 0.9 %copy-done.4 = f32[22,2,32,128]{3,2,1,0:T(8,128)} copy-done((f32[22,2,32,128]{3,2,1,0:T(8,128)}, f32[22,2,32,128]{3,2,1,0:T(8,128)S(1)}, u32[]{:S(2)}) %copy-start.4) | copy-done | bytes 720920
  55.0 0.9 %copy-done.5 = f32[22,2,32,128]{3,2,1,0:T(8,128)} copy-done((f32[22,2,32,128]{3,2,1,0:T(8,128)}, f32[22,2,32,128]{3,2,1,0:T(8,128)S(1)}, u32[]{:S(2)}) %copy-start.5) | copy-done | bytes 720920
  55.9 0.7 %copy-done.7 = f32[16,16,256]{2,1,0:T(8,128)} copy-done((f32[16,16,256]{2,1,0:T(8,128)}, f32[16,16,256]{2,1,0:T(8,128)S(1)}, u32[]{:S(2)}) %copy-start.7) | copy-done | bytes 262168
  56.6 1.5 %all-to-all-done.arrived = f32[128,1,128]{2,1,0:T(1,128)S(1)} async-done(((f32[128,1,128]{2,1,0:T(1,128)}), f32[128,1,128]{2,1,0:T(1,128)S(1)}, u32[]{:S(2)}, u32[]{:S(2)}) %all-to-all-start) | async-done | bytes 65568 | tf_op jit(solution)/shard_map/all_to_all | solution.py:1006
  58.1 3.9 %shard_map.110 = f32[16,16,256]{2,1,0:T(8,128)} custom-call(f32[16,16,256]{2,1,0:T(8,128)} %copy-done.7, f32[22,2,32,128]{3,2,1,0:T(8,128)} %copy-done.2, f32[22,2,32,128]{3,2,1,0:T(8,128)} %copy-done.3, f32[22,2,32,128]{3,2,1,0:T(8,128)} %copy-done.4, f32[22,2,32,128]{3,2,1,0:T(8,128)} %copy-done.5, f32[128,1,128]{2,1,0:T(1,128)S(1)} %all-to-all-done.arrived, ...), custom_call_target="tpu_custom_call" | custom-call | bytes 8388608 | tf_op jit(solution)/shard_map/pallas_call | solution.py:887
  (21 shorter events, 0.1 us)
Async XLA Ops:
  0.6 20.6 %copy-start.6 = (s32[8,16,256]{2,1,0:T(8,128)S(1)}, s32[8,16,256]{2,1,0:T(8,128)}, u32[]{:S(2)}) copy-start(s32[8,16,256]{2,1,0:T(8,128)} %flags.1) | copy-start | bytes 393220
  0.6 8.8 %copy-start.12 = (s32[1024]{0:T(1024)S(1)}, s32[1024]{0:T(1024)}, u32[]{:S(2)}) copy-start(s32[1024]{0:T(1024)} %param.15) | copy-start | bytes 12292
  3.5 32.0 %copy-start.8 = (s32[512]{0:T(512)S(1)}, s32[512]{0:T(512)}, u32[]{:S(2)}) copy-start(s32[512]{0:T(512)} %param.11) | copy-start | bytes 6148
  3.5 32.0 %copy-start.9 = (f32[512]{0:T(512)S(1)}, f32[512]{0:T(512)}, u32[]{:S(2)}) copy-start(f32[512]{0:T(512)} %param.12) | copy-start | bytes 6148
  3.6 32.0 %copy-start.10 = (s32[512]{0:T(512)S(1)}, s32[512]{0:T(512)}, u32[]{:S(2)}) copy-start(s32[512]{0:T(512)} %param.13) | copy-start | bytes 6148
  3.6 32.0 %copy-start.11 = (s32[512]{0:T(512)S(1)}, s32[512]{0:T(512)}, u32[]{:S(2)}) copy-start(s32[512]{0:T(512)} %param.14) | copy-start | bytes 6148
  3.6 17.7 %collective-permute-start = (f32[2,208,128]{2,1,0:T(8,128)}, f32[2,208,128]{2,1,0:T(8,128)S(1)}, u32[]{:S(2)}, u32[]{:S(2)}) collective-permute-start(f32[2,208,128]{2,1,0:T(8,128)} %get-tuple-element.28), channel_id=1, source_target_pairs={{0,1},{1,0},{2,3},{3,2},{4,5},{5,4},{6,7},{7,6},{8,9},{9,8},{10,11... | collective-permute-start | bytes 638984 | tf_op jit(solution)/shard_map/ppermute | solution.py:895
  5.8 15.5 %collective-permute-start.1 = (f32[2,208,128]{2,1,0:T(8,128)S(1)}, f32[2,208,128]{2,1,0:T(8,128)S(1)}, u32[]{:S(2)}, u32[]{:S(2)}) collective-permute-start(f32[2,208,128]{2,1,0:T(8,128)S(1)} %get-tuple-element.29), channel_id=1, source_target_pairs={{0,7},{1,2},{2,1},{3,4},{4,3},{5,6},{6,5},{7,0},{8,15},{9,10},{10,... | collective-permute-start | bytes 638984 | tf_op jit(solution)/shard_map/ppermute | solution.py:895
  10.5 4.2 %collective-permute-start.2 = (f32[2,104,128]{2,1,0:T(8,128)S(1)}, f32[2,104,128]{2,1,0:T(8,128)S(1)}, u32[]{:S(2)}, u32[]{:S(2)}) collective-permute-start(f32[2,104,128]{2,1,0:T(8,128)S(1)} %get-tuple-element.31), channel_id=1, source_target_pairs={{0,8},{8,0},{16,24},{24,16},{32,40},{40,32},{48,56},{56,48},{64,72... | collective-permute-start | bytes 319496 | tf_op jit(solution)/shard_map/ppermute | solution.py:895
  11.8 9.4 %collective-permute-start.3 = (f32[2,104,128]{2,1,0:T(8,128)S(1)}, f32[2,104,128]{2,1,0:T(8,128)S(1)}, u32[]{:S(2)}, u32[]{:S(2)}) collective-permute-start(f32[2,104,128]{2,1,0:T(8,128)S(1)} %get-tuple-element.32), channel_id=1, source_target_pairs={{0,120},{8,16},{16,8},{24,32},{32,24},{40,48},{48,40},{56,64},{64,... | collective-permute-start | bytes 319496 | tf_op jit(solution)/shard_map/ppermute | solution.py:895
  22.6 7.0 %collective-permute-start.4 = (f32[2,264,128]{2,1,0:T(8,128)S(1)}, f32[2,264,128]{2,1,0:T(8,128)S(1)}, u32[]{:S(2)}, u32[]{:S(2)}) collective-permute-start(f32[2,264,128]{2,1,0:T(8,128)S(1)} %get-tuple-element.37), channel_id=1, source_target_pairs={{0,8},{8,0},{16,24},{24,16},{32,40},{40,32},{48,56},{56,48},{64,72... | collective-permute-start | bytes 811016 | tf_op jit(solution)/shard_map/ppermute | solution.py:895
  24.1 11.5 %collective-permute-start.5 = (f32[2,264,128]{2,1,0:T(8,128)S(1)}, f32[2,264,128]{2,1,0:T(8,128)S(1)}, u32[]{:S(2)}, u32[]{:S(2)}) collective-permute-start(f32[2,264,128]{2,1,0:T(8,128)S(1)} %get-tuple-element.38), channel_id=1, source_target_pairs={{0,120},{8,16},{16,8},{24,32},{32,24},{40,48},{48,40},{56,64},{64,... | collective-permute-start | bytes 811016 | tf_op jit(solution)/shard_map/ppermute | solution.py:895
  27.0 21.5 %collective-permute-start.6 = (f32[2,128,128]{2,1,0:T(8,128)S(1)}, f32[2,128,128]{2,1,0:T(8,128)S(1)}, u32[]{:S(2)}, u32[]{:S(2)}) collective-permute-start(f32[2,128,128]{2,1,0:T(8,128)S(1)} %get-tuple-element.43), channel_id=1, source_target_pairs={{0,1},{1,0},{2,3},{3,2},{4,5},{5,4},{6,7},{7,6},{8,9},{9,8},{10,11... | collective-permute-start | bytes 393224 | tf_op jit(solution)/shard_map/ppermute | solution.py:895
  27.1 21.4 %collective-permute-start.7 = (f32[2,128,128]{2,1,0:T(8,128)S(1)}, f32[2,128,128]{2,1,0:T(8,128)S(1)}, u32[]{:S(2)}, u32[]{:S(2)}) collective-permute-start(f32[2,128,128]{2,1,0:T(8,128)S(1)} %get-tuple-element.44), channel_id=1, source_target_pairs={{0,7},{1,2},{2,1},{3,4},{4,3},{5,6},{6,5},{7,0},{8,15},{9,10},{10,... | collective-permute-start | bytes 393224 | tf_op jit(solution)/shard_map/ppermute | solution.py:895
  35.6 12.9 %copy-start = (f32[16,16,256]{2,1,0:T(8,128)S(1)}, f32[16,16,256]{2,1,0:T(8,128)}, u32[]{:S(2)}) copy-start(f32[16,16,256]{2,1,0:T(8,128)} %temp.1) | copy-start | bytes 786436
  35.6 12.9 %copy-start.1 = (s32[16,16,256]{2,1,0:T(8,128)S(1)}, s32[16,16,256]{2,1,0:T(8,128)}, u32[]{:S(2)}) copy-start(s32[16,16,256]{2,1,0:T(8,128)} %mat.1) | copy-start | bytes 786436
  41.1 17.1 %all-to-all-start = ((f32[128,1,128]{2,1,0:T(1,128)}), f32[128,1,128]{2,1,0:T(1,128)S(1)}, u32[]{:S(2)}, u32[]{:S(2)}) async-start(f32[128,1,128]{2,1,0:T(1,128)} %get-tuple-element.50), calls=%async_computation | async-start | bytes 131072 | tf_op jit(solution)/shard_map/all_to_all | solution.py:1006
  52.4 0.9 %copy-start.2 = (f32[22,2,32,128]{3,2,1,0:T(8,128)}, f32[22,2,32,128]{3,2,1,0:T(8,128)S(1)}, u32[]{:S(2)}) copy-start(f32[22,2,32,128]{3,2,1,0:T(8,128)S(1)} %get-tuple-element.46.link_a_far) | copy-start | bytes 2162692
  53.3 0.9 %copy-start.3 = (f32[22,2,32,128]{3,2,1,0:T(8,128)}, f32[22,2,32,128]{3,2,1,0:T(8,128)S(1)}, u32[]{:S(2)}) copy-start(f32[22,2,32,128]{3,2,1,0:T(8,128)S(1)} %get-tuple-element.47.link_z_far) | copy-start | bytes 2162692
  54.2 0.9 %copy-start.4 = (f32[22,2,32,128]{3,2,1,0:T(8,128)}, f32[22,2,32,128]{3,2,1,0:T(8,128)S(1)}, u32[]{:S(2)}) copy-start(f32[22,2,32,128]{3,2,1,0:T(8,128)S(1)} %get-tuple-element.48.link_r_far) | copy-start | bytes 2162692
  55.0 0.9 %copy-start.5 = (f32[22,2,32,128]{3,2,1,0:T(8,128)}, f32[22,2,32,128]{3,2,1,0:T(8,128)S(1)}, u32[]{:S(2)}) copy-start(f32[22,2,32,128]{3,2,1,0:T(8,128)S(1)} %get-tuple-element.49.keep_far) | copy-start | bytes 2162692
  55.9 0.7 %copy-start.7 = (f32[16,16,256]{2,1,0:T(8,128)}, f32[16,16,256]{2,1,0:T(8,128)S(1)}, u32[]{:S(2)}) copy-start(f32[16,16,256]{2,1,0:T(8,128)S(1)} %get-tuple-element.45.swept_far) | copy-start | bytes 786436

commit v3 on v2

--- a/solution.py
+++ b/solution.py
@@ -39,6 +39,8 @@
 END_COND = 54
 END_CELLS = 112
 END_ROWS = 128
+
+GROUP = 5
 
 VMEM = pltpu.VMEM
 f32 = jnp.float32
@@ -112,7 +114,9 @@
         body(far, near)
 
 
-def first_kernel(f_far, flags_far, post, near, far, token, f, flags, low, high, come):
+def first_kernel(
+    f_far, flags_far, post, air, near, far, token, f, flags, low, high, come
+):
     flags_copy = pltpu.make_async_copy(flags_far, flags, come.at[CA])
 
     def layer_copy(a):
@@ -132,7 +136,8 @@
                 flag = flags[a, rows, lanes(half)].astype(f32)
                 out = collide([f[i, a, rows, lanes(half)] for i in range(Q)], flag)
                 for i in range(Q):
-                    post[i, a, rows, lanes(half)] = out[i]
+                    post[i, a, half, rows, :] = out[i]
+                air[a, half, rows, :] = flag
                 place = a * PER_PLACE
                 target, inner, edge, near_edge = (
                     (low, AXIAL_DOWN, 0, 1) if part == 0 else (high, AXIAL_UP, 7, 6)
@@ -158,7 +163,10 @@
     by_parity("axial", hand_over, near, far)
 
 
-def solid_azim_kernel(temp_far, mat_far, cells, token, near, far, temp, mat, come):
+def solid_azim_kernel(
+    temp_far, mat_far, cells, token, near, far, packed, temp, mat, come
+):
+    packed[...] = jnp.zeros((8, 128), f32)
     copies = []
     for n, layers in enumerate((pl.ds(0, 3), pl.ds(SA - 3, 3))):
         for k, (source, target) in enumerate(((temp_far, temp), (mat_far, mat))):
@@ -316,29 +324,26 @@
 def rim_kernel(
     n_axial,
     post,
-    flags,
+    air,
     near_z,
     far_z,
+    packed,
     ext,
     opened,
     near,
     far,
-    token,
     low,
     high,
 ):
-    token[...] = jnp.zeros((8, 128), f32)
     lane = lax.broadcasted_iota(jnp.int32, (8, 128), 1)
     below, above = ends(n_axial)
 
     def own_layer(a, carry):
-        for half in HALVES:
-            for part in (0, 1):
-                rows = pl.ds(8 * part, 8)
-                to = pl.ds(8 + 8 * part, 8)
-                for i in range(Q):
-                    ext[i, a, half, to, :] = post[i, a, rows, lanes(half)]
-                opened[0, a, half, to, :] = flags[a, rows, lanes(half)].astype(f32)
+        to = pl.ds(8, 16)
+        for half in HALVES:
+            for i in range(Q):
+                ext[i, a, half, to, :] = post[i, a, half]
+            opened[0, a, half, to, :] = air[a, half]
         return carry
 
     lax.fori_loop(0, CA, own_layer, 0)
@@ -420,9 +425,58 @@
         opened[2, a, 1, rows, :] = jnp.where(lane == 127, 0.0, down[1])
 
 
-def fluid_kernel(
+def step_two(second, opened, a, flag_a, lane, speeds, target, at):
+    for part in (0, 1):
+        moved = stream(second, opened, a + 1, flag_a, 8 + 8 * part, lane)
+        for half in HALVES:
+            for i in range(Q):
+                target[i, at, pl.ds(8 * part, 8), lanes(half)] = moved[half][i]
+            rho, mom_a, mom_z, mom_r = moments(moved[half])
+            inv = 1.0 / rho
+            ua, uz, ur = mom_a * inv, mom_z * inv, mom_r * inv
+            speeds[pl.ds(a * CZ + 8 * part, 8), lanes(half)] = jnp.sqrt(
+                ua * ua + uz * uz + ur * ur + 1e-06
+            )
+
+
+def inner_kernel(
+    ext, opened, fluid_far, second, speeds, token, fluid_out, layers_out
+):
+    token[...] = jnp.zeros((8, 128), f32)
+    lane = lax.broadcasted_iota(jnp.int32, (8, 128), 1)
+
+    def first_step(a, carry):
+        for row in (7, 15, 17):
+            moved = stream(ext, opened, a, a, row, lane)
+            for half in HALVES:
+                out = collide(moved[half], opened[0, a, half, pl.ds(row, 8), :])
+                for i in range(Q):
+                    second[i, a + 1, half, pl.ds(row, 8), :] = out[i]
+        return carry
+
+    lax.fori_loop(1, CA - 1, first_step, 0)
+
+    def layer_copy(n):
+        return pltpu.make_async_copy(
+            fluid_out.at[:, n], fluid_far.at[:, n + 2], layers_out.at[n]
+        )
+
+    def second_step(n, carry):
+        step_two(second, opened, n + 2, n + 2, lane, speeds, fluid_out, n)
+        layer_copy(n).start()
+        return carry
+
+    lax.fori_loop(0, CA - 4, second_step, 0)
+    for n in range(CA - 4):
+        layer_copy(n).wait()
+
+
+def outer_kernel(
     n_azim,
     n_axial,
+    fluid_so_far,
+    second_so_far,
+    inner_speeds,
     ext,
     own_opened,
     near_a,
@@ -432,15 +486,17 @@
     owner,
     slot,
     fluid_far,
+    second,
     message,
     opened,
-    second,
     sides,
     speeds,
     fluid_out,
     layers_out,
 ):
     lane = lax.broadcasted_iota(jnp.int32, (8, 128), 1)
+    inside = pl.ds(2 * CZ, (CA - 4) * CZ)
+    speeds[inside, :] = inner_speeds[inside, :]
 
     def own_flags(a, carry):
         for k in range(3):
@@ -475,12 +531,11 @@
             for i in range(Q):
                 second[i, a + 1, half, pl.ds(row, 8), :] = out[i]
 
-    def first_step(a, carry):
-        for row in (7, 15, 23):
-            finish(a, row, stream(ext, opened, a, a + 1, row, lane))
-        return carry
-
-    lax.fori_loop(1, CA - 1, first_step, 0)
+    def layer_copy(n, a):
+        return pltpu.make_async_copy(
+            fluid_out.at[:, n], fluid_far.at[:, a], layers_out.at[n]
+        )
+
     for side, (a, inward, outward) in enumerate(
         ((0, AZIM_UP, AZIM_DOWN), (CA - 1, AZIM_DOWN, AZIM_UP))
     ):
@@ -516,27 +571,15 @@
 
         lax.fori_loop(0, 3, edge_step, 0)
 
-    def second_step(a, carry):
-        for part in (0, 1):
-            moved = stream(second, opened, a + 1, a + 1, 8 + 8 * part, lane)
-            for half in HALVES:
-                for i in range(Q):
-                    fluid_out[i, a, pl.ds(8 * part, 8), lanes(half)] = moved[half][i]
-                rho, mom_a, mom_z, mom_r = moments(moved[half])
-                inv = 1.0 / rho
-                ua, uz, ur = mom_a * inv, mom_z * inv, mom_r * inv
-                speeds[pl.ds(a * CZ + 8 * part, 8), lanes(half)] = jnp.sqrt(
-                    ua * ua + uz * uz + ur * ur + 1e-06
-                )
-        layer_copy(a).start()
-        return carry
-
-    def layer_copy(a):
-        return pltpu.make_async_copy(
-            fluid_out.at[:, a], fluid_far.at[:, a], layers_out.at[a]
-        )
-
-    lax.fori_loop(0, CA, second_step, 0)
+        def second_step(n, carry):
+            layer = n + side * (CA - 2)
+            at = n + 2 * side
+            step_two(second, opened, layer, layer + 1, lane, speeds, fluid_out, at)
+            layer_copy(at, layer).start()
+            return carry
+
+        lax.fori_loop(0, 2, second_step, 0)
+
 
     rows_here = cell.shape[1]
     place = cell[...]
@@ -571,8 +614,8 @@
             total = total + (pltpu.roll(moved, CAP * which, 1) if which else moved)
     for o in range(devices):
         message[o, :, :] = total[o : o + 1]
-    for a in range(CA):
-        layer_copy(a).wait()
+    for n, a in enumerate((0, 1, CA - 2, CA - 1)):
+        layer_copy(n, a).wait()
 
 
 def link(first, second):
@@ -610,23 +653,35 @@
 
 def solid_kernel(
     n_axial,
-    temp,
-    mat,
+    temp_far,
+    mat_far,
     near_s,
     far_s,
     near_e,
     far_e,
     cells,
     swept,
+    links_out,
+    all_cells,
     link_a,
     link_z,
     link_r,
     keep,
-    all_cells,
     ext,
     cond,
     other,
+    temp,
+    mat,
+    come,
 ):
+    copies = [
+        pltpu.make_async_copy(source, target, come.at[n])
+        for n, (source, target) in enumerate(((temp_far, temp), (mat_far, mat)))
+    ]
+    for copy in copies:
+        copy.start()
+    for copy in copies:
+        copy.wait()
     lane = lax.broadcasted_iota(jnp.int32, (8, 128), 1)
 
     def own_layer(a, carry):
@@ -712,6 +767,14 @@
 
     lax.fori_loop(1, SA + 5, keeps, 0, unroll=4)
 
+    def trim(a, carry):
+        for half in HALVES:
+            for n, kind in enumerate((link_a, link_z, link_r)):
+                links_out[n, a, half] = kind[a + 1, half, pl.ds(6, 24), :]
+        return carry
+
+    lax.fori_loop(0, SA + 4, trim, 0, unroll=2)
+
     def once(source, target, first, last, at):
         def layer(a, carry):
             for row in at:
@@ -737,10 +800,7 @@
 
 def deposit_kernel(
     swept_far,
-    link_a_far,
-    link_z_far,
-    link_r_far,
-    keep_far,
+    links_far,
     arrived,
     all_cells,
     solid_out,
@@ -748,26 +808,21 @@
     other,
     came,
     swept,
-    link_a,
-    link_z,
-    link_r,
-    keep,
+    links,
     brought,
 ):
-    copies = [
-        pltpu.make_async_copy(source, target, brought.at[n])
-        for n, (source, target) in enumerate(
-            (
-                (swept_far, swept),
-                (link_a_far, link_a),
-                (link_z_far, link_z),
-                (link_r_far, link_r),
-                (keep_far, keep),
-            )
+    groups = [
+        pltpu.make_async_copy(
+            links_far.at[:, pl.ds(GROUP * n, GROUP)],
+            links.at[:, pl.ds(GROUP * n, GROUP)],
+            brought.at[n],
         )
+        for n in range((SA + 4) // GROUP)
     ]
-    for copy in copies:
+    swept_copy = pltpu.make_async_copy(swept_far, swept, brought.at[len(groups)])
+    for copy in groups:
         copy.start()
+    swept_copy.start()
     lane = lax.broadcasted_iota(jnp.int32, (8, 128), 1)
     senders = arrived.shape[0]
     for s in range(senders):
@@ -775,11 +830,10 @@
 
     def clear(a, carry):
         for half in HALVES:
-            heat[a, half] = jnp.zeros((ROWS, 128), f32)
-        return carry
-
-    lax.fori_loop(0, SA + 6, clear, 0, unroll=2)
-
+            heat[a, half] = jnp.zeros((24, 128), f32)
+        return carry
+
+    lax.fori_loop(0, SA + 4, clear, 0, unroll=2)
     values = jnp.transpose(came[...]) * (1.0 / HEAT_CAPACITY)
 
     def place(which, rows, row_of):
@@ -807,7 +861,7 @@
     own = place(4, SA * SZ, lambda j: j)
     for a in range(SA):
         for half in HALVES:
-            heat[a + 3, half, pl.ds(8, 16), :] = own[
+            heat[a + 2, half, pl.ds(2, 16), :] = own[
                 16 * a : 16 * a + 16, 128 * half : 128 * half + 128
             ]
     low = place(1, 32, lambda j: j + 14 * SZ)
@@ -815,48 +869,66 @@
     for n in range(2):
         for half in HALVES:
             cut = slice(128 * half, 128 * half + 128)
-            heat[1 + n, half, pl.ds(8, 16), :] = low[16 * n : 16 * n + 16, cut]
-            heat[19 + n, half, pl.ds(8, 16), :] = high[16 * n : 16 * n + 16, cut]
+            heat[n, half, pl.ds(2, 16), :] = low[16 * n : 16 * n + 16, cut]
+            heat[18 + n, half, pl.ds(2, 16), :] = high[16 * n : 16 * n + 16, cut]
     low = place(3, 32, lambda j: (j // 2) * SZ + 14 + j % 2)
     high = place(5, 32, lambda j: (j // 2) * SZ + j % 2)
     for a in range(SA):
         for half in HALVES:
             cut = slice(128 * half, 128 * half + 128)
-            heat[a + 3, half, pl.ds(6, 2), :] = low[2 * a : 2 * a + 2, cut]
-            heat[a + 3, half, pl.ds(24, 2), :] = high[2 * a : 2 * a + 2, cut]
+            heat[a + 2, half, pl.ds(0, 2), :] = low[2 * a : 2 * a + 2, cut]
+            heat[a + 2, half, pl.ds(18, 2), :] = high[2 * a : 2 * a + 2, cut]
     for which, cell_row, a, row in (
-        (0, 255, 2, 7),
-        (2, 240, 2, 24),
-        (6, 15, 19, 7),
-        (8, 0, 19, 24),
+        (0, 255, 1, 1),
+        (2, 240, 1, 18),
+        (6, 15, 18, 1),
+        (8, 0, 18, 18),
     ):
         one = place(which, 8, lambda j: jnp.where(j == 0, cell_row, -1))
         for half in HALVES:
             heat[a, half, pl.ds(row, 1), :] = one[0:1, 128 * half : 128 * half + 128]
 
-    for copy in copies:
+    def spread(source, a, row):
+        rows, before, after = (pl.ds(row + n, 8) for n in (0, -1, 1))
+        pair = [source[a, half, rows, :] for half in HALVES]
+        up = shifted(pair, -1, lane)
+        flow = [links[2, a, half, rows, :] * (up[half] - pair[half]) for half in HALVES]
+        back = shifted(flow, 1, lane)
+        out = []
+        for half in HALVES:
+            here = pair[half]
+            out.append(
+                here
+                + links[0, a, half, rows, :] * (source[a + 1, half, rows, :] - here)
+                + links[0, a - 1, half, rows, :] * (source[a - 1, half, rows, :] - here)
+                + links[1, a, half, rows, :] * (source[a, half, after, :] - here)
+                + links[1, a, half, before, :] * (source[a, half, before, :] - here)
+                + (flow[half] - back[half])
+                + heat[a, half, rows, :]
+            )
+        return out
+
+    def middle(a, carry):
+        for row in (1, 9, 11):
+            out = spread(heat, a, row)
+            for half in HALVES:
+                other[a, half, pl.ds(row, 8), :] = out[half]
+        return carry
+
+    for n, copy in enumerate(groups):
         copy.wait()
-
-    def middle(a, carry):
-        for row in (7, 15, 23):
-            out = sweep(heat, link_a, link_z, link_r, keep, a, row, lane)
-            for half in HALVES:
-                other[a, half, pl.ds(row, 8), :] = (
-                    out[half] + heat[a, half, pl.ds(row, 8), :]
-                )
-        return carry
-
-    lax.fori_loop(2, SA + 4, middle, 0, unroll=2)
+        first = max(GROUP * n, 1)
+        last = min(GROUP * (n + 1), SA + 3)
+        lax.fori_loop(first, last, middle, 0, unroll=last - first)
+    swept_copy.wait()
 
     def final(a, carry):
         for part in (0, 1):
             rows = pl.ds(8 * part, 8)
-            out = sweep(other, link_a, link_z, link_r, keep, a + 3, 8 + 8 * part, lane)
+            out = spread(other, a + 2, 2 + 8 * part)
             for half in HALVES:
                 solid_out[a, rows, lanes(half)] = (
-                    out[half]
-                    + heat[a + 3, half, pl.ds(8 + 8 * part, 8), :]
-                    + swept[a, rows, lanes(half)]
+                    out[half] + swept[a, rows, lanes(half)]
                 )
         return carry
 
@@ -864,7 +936,7 @@
 
 
 def call(
-    kernel, ins, outs, scratch=(), limit=16, moved=0, far_ins=0, far_outs=0, held=()
+    kernel, ins, outs, scratch=(), limit=16, moved=0, far_ins=0, far_outs=0, held=(), aliases={}
 ):
     here, there = (pl.BlockSpec(memory_space=m) for m in (VMEM, pltpu.HBM))
     kernel_call = pl.pallas_call(
@@ -876,6 +948,7 @@
         in_specs=[there] * far_ins + [here] * (ins - far_ins),
         out_specs=[there] * far_outs + [here] * (len(outs) - far_outs),
         scratch_shapes=list(scratch),
+        input_output_aliases=aliases,
         compiler_params=pltpu.CompilerParams(vmem_limit_bytes=limit * 1024 * 1024),
         cost_estimate=pl.CostEstimate(
             flops=0, bytes_accessed=moved, transcendentals=0
@@ -918,10 +991,11 @@
     solid = (SA, SZ, NR)
     fluid_ext = (Q, CA, 2, ROWS, 128)
     solid_ext = (SA + 6, 2, ROWS, 128)
-    post, near_z, far_z, token = call(
+    opened_ext = (3, CA, 2, ROWS, 128)
+    post, air, near_z, far_z, token = call(
         first_kernel,
         2,
-        [fluid, axial_msg, axial_msg, (8, 128)],
+        [(Q, CA, 2, CZ, 128), (CA, 2, CZ, 128), axial_msg, axial_msg, (8, 128)],
         [
             VMEM(fluid, f32),
             VMEM((CA, CZ, NR), jnp.int32),
@@ -931,13 +1005,14 @@
         ],
         moved=8 << 20,
         far_ins=2,
+        held=(0, 1, 2, 3),
     )(populations, fluid_flags)
     near_z = swap(near_z, "axial", False)
     far_z = swap(far_z, "axial", True)
-    near_s, far_s = call(
+    near_s, far_s, packed = call(
         solid_azim_kernel,
         4,
-        [solid_msg, solid_msg],
+        [solid_msg, solid_msg, (8, 128)],
         [
             VMEM((2, 3, SZ, NR), f32),
             VMEM((2, 3, SZ, NR), jnp.int32),
@@ -951,16 +1026,27 @@
     near_z, far_z, near_s, far_s = lax.optimization_barrier(
         (near_z, far_z, near_s, far_s)
     )
-    ext, opened, near_a, far_a, token = call(
+    ext, opened, near_a, far_a = call(
         functools.partial(rim_kernel, n_axial),
-        4,
-        [fluid_ext, (3, CA, 2, ROWS, 128), azim_msg, azim_msg, (8, 128)],
+        5,
+        [fluid_ext, opened_ext, azim_msg, azim_msg],
         [VMEM(azim_msg, f32), VMEM(azim_msg, f32)],
         moved=8 << 20,
         held=(0, 1),
-    )(post, fluid_flags, near_z, far_z)
+    )(post, air, near_z, far_z, packed)
     near_a = swap(near_a, "azim", False)
     far_a = swap(far_a, "azim", True)
+    rows = wall_cell.shape[0]
+    ext, opened = (pltpu.with_memory_space_constraint(x, VMEM) for x in (ext, opened))
+    fluid_out, second, speeds, token = call(
+        inner_kernel,
+        2,
+        [fluid, (Q, CA + 2, 2, ROWS, 128), (CA * CZ, NR), (8, 128)],
+        [VMEM((Q, CA - 4, CZ, NR), f32), pltpu.SemaphoreType.DMA((CA - 4,))],
+        moved=12 << 20,
+        far_outs=1,
+        held=(1, 2),
+    )(ext, opened)
     near_e, far_e = call(
         solid_axial_kernel,
         6,
@@ -977,25 +1063,28 @@
     )(solid_temp, materials, cells, near_s, far_s, token)
     near_e = swap(near_e, "axial", False)
     far_e = swap(far_e, "axial", True)
-    rows = wall_cell.shape[0]
-    fluid_out, message = call(
-        functools.partial(fluid_kernel, n_azim, n_axial),
-        8,
-        [fluid, (devices, 1, 128)],
+    fluid_out, _, message = call(
+        functools.partial(outer_kernel, n_azim, n_axial),
+        11,
+        [fluid, (Q, CA + 2, 2, ROWS, 128), (devices, 1, 128)],
         [
             VMEM((3, CA + 2, 2, ROWS, 128), f32),
-            VMEM((Q, CA + 2, 2, ROWS, 128), f32),
             VMEM((2, 13, 2, ROWS, 128), f32),
             VMEM((CA * CZ, NR), f32),
-            VMEM(fluid, f32),
-            pltpu.SemaphoreType.DMA((CA,)),
+            VMEM((Q, 4, CZ, NR), f32),
+            pltpu.SemaphoreType.DMA((4,)),
         ],
-        limit=28,
-        moved=16 << 20,
+        moved=8 << 20,
+        far_ins=1,
         far_outs=1,
+        held=(1,),
+        aliases={0: 0, 1: 1},
     )(
-        pltpu.with_memory_space_constraint(ext, VMEM),
-        pltpu.with_memory_space_constraint(opened, VMEM),
+        fluid_out,
+        pltpu.with_memory_space_constraint(second, VMEM),
+        pltpu.with_memory_space_constraint(speeds, VMEM),
+        ext,
+        opened,
         near_a,
         far_a,
         wall_cell.reshape(1, rows),
@@ -1006,28 +1095,35 @@
     arrived = lax.all_to_all(
         message, ("azim", "axial"), split_axis=0, concat_axis=0, tiled=True
     )
-    *swept, all_cells = call(
+    link_shape = (3, SA + 4, 2, 24, 128)
+    swept, links, all_cells = call(
         functools.partial(solid_kernel, n_axial),
         7,
-        [solid] + [solid_ext] * 4 + [(9, CAP, devices)],
-        [VMEM(solid_ext, f32)] * 3,
+        [solid, link_shape, (9, CAP, devices)],
+        [VMEM(solid_ext, f32)] * 7
+        + [
+            VMEM(solid, f32),
+            VMEM(solid, jnp.int32),
+            pltpu.SemaphoreType.DMA((2,)),
+        ],
         moved=8 << 20,
+        far_ins=2,
     )(solid_temp, materials, near_s, far_s, near_e, far_e, cells)
     (solid_out,) = call(
         deposit_kernel,
-        7,
+        4,
         [solid],
         [
-            VMEM(solid_ext, f32),
-            VMEM(solid_ext, f32),
+            VMEM(link_shape[1:], f32),
+            VMEM(link_shape[1:], f32),
             VMEM((devices, 128), f32),
             VMEM(solid, f32),
-        ]
-        + [VMEM(solid_ext, f32)] * 4
-        + [pltpu.SemaphoreType.DMA((5,))],
+            VMEM(link_shape, f32),
+            pltpu.SemaphoreType.DMA((5,)),
+        ],
         moved=8 << 20,
-        far_ins=5,
-    )(*swept, arrived, all_cells)
+        far_ins=2,
+    )(swept, links, arrived, all_cells)
     return fluid_out, solid_out
 
 

time: 62.3 us -> 58.3 us (0.936)
  local copies, waits for them, and re-layouts: 4.37 us -> 1.98 us
  Pallas kernels: 19.5 us -> 21.1 us
  waiting for transfers between devices: 14 us -> 12.4 us
  starting transfers between devices: 23.3 us -> 21.8 us
    ppermute x8, waiting for transfers between devices: 12.5 us -> 9.52 us  [swap(): return lax.ppermute(values, axis, pairs)]
    unnamed x26 -> x14, local copies, waits for them, and re-layouts: 4.24 us -> 1.85 us
    pallas_call x7 -> x8, Pallas kernels: 19.5 us -> 21.1 us  [run(): return kernel_call(*far, *args[far_ins:])]
    all_to_all x1, starting transfers between devices: 7.42 us -> 5.98 us  [per_device(): lax.all_to_all(message, ('azim', 'axial'), split_axis=0, concat_axis=0, t...]
    all_to_all x1, waiting for transfers between devices: 1.53 us -> 2.9 us  [per_device(): lax.all_to_all(message, ('azim', 'axial'), split_axis=0, concat_axis=0, t...]
  transfers between devices with their start and end apart: 9 -> 9, of which waited for: 3 -> 3; matrix products, arithmetic and copies ran while one was open for 0% -> 0% of each run, Pallas kernels for 18% -> 23%
where the time goes in v3:
time: 58.3 us; the launch traced here: 58.1 us
  starting transfers between devices  21.8 us (37%)
  Pallas kernels  21.1 us (36%)
  waiting for transfers between devices  12.4 us (21%)
  local copies, waits for them, and re-layouts  1.98 us (3%)
  between operations  0.77 us (1%)
    pallas_call x8, Pallas kernels, run(): return kernel_call(*far, *args[far_ins:])  21.1 us
    ppermute x8, starting transfers between devices, swap(): return lax.ppermute(values, axis, pairs)  15.9 us
    ppermute x8, waiting for transfers between devices, swap(): return lax.ppermute(values, axis, pairs)  9.52 us
    all_to_all x1, starting transfers between devices, per_device(): lax.all_to_all(message, ('azim', 'axial'), split_axis=0, concat_axis=0, t...  5.98 us
    all_to_all x1, waiting for transfers between devices, per_device(): lax.all_to_all(message, ('azim', 'axial'), split_axis=0, concat_axis=0, t...  2.9 us
    unnamed x14, local copies, waits for them, and re-layouts  1.85 us
  transfers between devices with their start and end apart: 9, of which 3 were waited for; matrix products, arithmetic and copies ran while one was open for 0% of the time, Pallas kernels for 23%

profile of v3, /device:TPU:1, one launch (start us, length us, event | category | flops | bytes accessed | tf_op | source)
XLA Modules:
  0.0 58.1 jit_solution(18343755555120047380)
XLA Ops:
  0.6 0.0 copy-start.6
  0.6 2.8 %shard_map.104 = (f32[19,8,2,16,128]{4,3,2,1,0:T(8,128)S(1)}, f32[8,2,16,128]{3,2,1,0:T(8,128)S(1)}, f32[2,208,128]{2,1,0:T(8,128)}, f32[2,208,128]{2,1,0:T(8,128)S(1)}, f32[8,128]{1,0:T(8,128)S(1)}) custom-call(f32[19,8,16,256]{3,2,1,0:T(8,128)} %f_far.1, s32[8,16,256]{2,1,0:T(8,128)} %flags_far.1), custom_call_target="tpu_custom_call" | custom-call | bytes 8388608 | tf_op jit(solution)/shard_map/pallas_call | solution.py:960
  3.5 2.2 %collective-permute-start = (f32[2,208,128]{2,1,0:T(8,128)}, f32[2,208,128]{2,1,0:T(8,128)S(1)}, u32[]{:S(2)}, u32[]{:S(2)}) collective-permute-start(f32[2,208,128]{2,1,0:T(8,128)} %get-tuple-element.31), channel_id=1, source_target_pairs={{0,1},{1,0},{2,3},{3,2},{4,5},{5,4},{6,7},{7,6},{8,9},{9,8},{10,11... | collective-permute-start | bytes 638984 | tf_op jit(solution)/shard_map/ppermute | solution.py:968
  5.7 3.6 %collective-permute-start.1 = (f32[2,208,128]{2,1,0:T(8,128)S(1)}, f32[2,208,128]{2,1,0:T(8,128)S(1)}, u32[]{:S(2)}, u32[]{:S(2)}) collective-permute-start(f32[2,208,128]{2,1,0:T(8,128)S(1)} %get-tuple-element.32), channel_id=1, source_target_pairs={{0,7},{1,2},{2,1},{3,4},{4,3},{5,6},{6,5},{7,0},{8,15},{9,10},{10,... | collective-permute-start | bytes 638984 | tf_op jit(solution)/shard_map/ppermute | solution.py:968
  9.3 0.0 copy-done.6
  9.3 0.1 reshape.19
  9.5 1.0 %shard_map.105 = (f32[2,104,128]{2,1,0:T(8,128)S(1)}, f32[2,104,128]{2,1,0:T(8,128)S(1)}, f32[8,128]{1,0:T(8,128)S(1)}) custom-call(f32[16,16,256]{2,1,0:T(8,128)} %temp_far.5, s32[16,16,256]{2,1,0:T(8,128)} %mat_far.5, s32[8,128]{1,0:T(8,128)S(1)} %bitcast.5, f32[8,128]{1,0:T(8,128)S(1)} %get-tuple-element.33.token), custom_call_target="tpu_custom_call" | custom-call | bytes 2097152 | tf_op jit(solution)/shard_map/pallas_call | solution.py:960
  10.4 1.3 %collective-permute-start.2 = (f32[2,104,128]{2,1,0:T(8,128)S(1)}, f32[2,104,128]{2,1,0:T(8,128)S(1)}, u32[]{:S(2)}, u32[]{:S(2)}) collective-permute-start(f32[2,104,128]{2,1,0:T(8,128)S(1)} %get-tuple-element.34), channel_id=1, source_target_pairs={{0,8},{8,0},{16,24},{24,16},{32,40},{40,32},{48,56},{56,48},{64,72... | collective-permute-start | bytes 319496 | tf_op jit(solution)/shard_map/ppermute | solution.py:968
  11.8 2.9 %collective-permute-start.3 = (f32[2,104,128]{2,1,0:T(8,128)S(1)}, f32[2,104,128]{2,1,0:T(8,128)S(1)}, u32[]{:S(2)}, u32[]{:S(2)}) collective-permute-start(f32[2,104,128]{2,1,0:T(8,128)S(1)} %get-tuple-element.35), channel_id=1, source_target_pairs={{0,120},{8,16},{16,8},{24,32},{32,24},{40,48},{48,40},{56,64},{64,... | collective-permute-start | bytes 319496 | tf_op jit(solution)/shard_map/ppermute | solution.py:968
  14.7 0.0 collective-permute-done.2.near_s
  14.7 6.5 %collective-permute-done.3.far_s = f32[2,104,128]{2,1,0:T(8,128)S(1)} collective-permute-done((f32[2,104,128]{2,1,0:T(8,128)S(1)}, f32[2,104,128]{2,1,0:T(8,128)S(1)}, u32[]{:S(2)}, u32[]{:S(2)}) %collective-permute-start.3) | collective-permute-done | bytes 106528 | tf_op jit(solution)/shard_map/ppermute | solution.py:968
  21.2 0.0 collective-permute-done.near_z
  21.2 0.0 collective-permute-done.1.far_z
  21.2 1.3 %shard_map.106 = (f32[19,8,2,32,128]{4,3,2,1,0:T(8,128)S(1)}, f32[3,8,2,32,128]{4,3,2,1,0:T(8,128)S(1)}, f32[2,264,128]{2,1,0:T(8,128)S(1)}, f32[2,264,128]{2,1,0:T(8,128)S(1)}) custom-call(f32[19,8,2,16,128]{4,3,2,1,0:T(8,128)S(1)} %get-tuple-element.29.post, f32[8,2,16,128]{3,2,1,0:T(8,128)S(1)} %get-tuple-element.30.air, ...), custom_call_target="tpu_custom_call" | custom-call | bytes 8388608 | tf_op jit(solution)/shard_map/pallas_call | solution.py:960
  22.5 1.5 %collective-permute-start.4 = (f32[2,264,128]{2,1,0:T(8,128)S(1)}, f32[2,264,128]{2,1,0:T(8,128)S(1)}, u32[]{:S(2)}, u32[]{:S(2)}) collective-permute-start(f32[2,264,128]{2,1,0:T(8,128)S(1)} %get-tuple-element.44), channel_id=1, source_target_pairs={{0,8},{8,0},{16,24},{24,16},{32,40},{40,32},{48,56},{56,48},{64,72... | collective-permute-start | bytes 811016 | tf_op jit(solution)/shard_map/ppermute | solution.py:968
  24.0 1.8 %collective-permute-start.5 = (f32[2,264,128]{2,1,0:T(8,128)S(1)}, f32[2,264,128]{2,1,0:T(8,128)S(1)}, u32[]{:S(2)}, u32[]{:S(2)}) collective-permute-start(f32[2,264,128]{2,1,0:T(8,128)S(1)} %get-tuple-element.45), channel_id=1, source_target_pairs={{0,120},{8,16},{16,8},{24,32},{32,24},{40,48},{48,40},{56,64},{64,... | collective-permute-start | bytes 811016 | tf_op jit(solution)/shard_map/ppermute | solution.py:968
  25.7 2.9 %shard_map.107 = (f32[19,8,16,256]{3,2,1,0:T(8,128)}, f32[19,10,2,32,128]{4,3,2,1,0:T(8,128)S(1)}, f32[128,256]{1,0:T(8,128)S(1)}, f32[8,128]{1,0:T(8,128)S(1)}) custom-call(f32[19,8,2,32,128]{4,3,2,1,0:T(8,128)S(1)} %get-tuple-element.39.ext, f32[3,8,2,32,128]{4,3,2,1,0:T(8,128)S(1)} %get-tuple-element.40.opened.own_opened), custom_call_target="tpu_custom_call" | custom-call | bytes 12582912 | tf_op jit(solution)/shard_map/pallas_call | solution.py:960
  28.6 1.2 %shard_map.109 = (f32[2,128,128]{2,1,0:T(8,128)S(1)}, f32[2,128,128]{2,1,0:T(8,128)S(1)}) custom-call(f32[16,16,256]{2,1,0:T(8,128)} %temp_far.5, s32[16,16,256]{2,1,0:T(8,128)} %mat_far.5, s32[8,128]{1,0:T(8,128)S(1)} %bitcast.6, f32[2,104,128]{2,1,0:T(8,128)S(1)} %collective-permute-done.2.near_s, f32[2,104,128]{2,1,0:T(8,128)S(1)} %collective-permute-done.3.far_s, ...), custom_call_target="tpu_custom_call" | custom-call | bytes 2097152 | tf_op jit(solution)/shard_map/pallas_call | solution.py:960
  29.9 0.1 collective-permute-start.6
  30.0 2.5 %collective-permute-start.7 = (f32[2,128,128]{2,1,0:T(8,128)S(1)}, f32[2,128,128]{2,1,0:T(8,128)S(1)}, u32[]{:S(2)}, u32[]{:S(2)}) collective-permute-start(f32[2,128,128]{2,1,0:T(8,128)S(1)} %get-tuple-element.51), channel_id=1, source_target_pairs={{0,7},{1,2},{2,1},{3,4},{4,3},{5,6},{6,5},{7,0},{8,15},{9,10},{10,... | collective-permute-start | bytes 393224 | tf_op jit(solution)/shard_map/ppermute | solution.py:968
  32.4 0.0 collective-permute-done.4.near_a
  32.4 3.0 %collective-permute-done.5.far_a = f32[2,264,128]{2,1,0:T(8,128)S(1)} collective-permute-done((f32[2,264,128]{2,1,0:T(8,128)S(1)}, f32[2,264,128]{2,1,0:T(8,128)S(1)}, u32[]{:S(2)}, u32[]{:S(2)}) %collective-permute-start.5) | collective-permute-done | bytes 270368 | tf_op jit(solution)/shard_map/ppermute | solution.py:968
  35.4 0.0 copy-done.5
  35.4 3.3 %shard_map.108 = (f32[19,8,16,256]{3,2,1,0:T(8,128)}, f32[19,10,2,32,128]{4,3,2,1,0:T(8,128)S(1)}, f32[128,1,128]{2,1,0:T(1,128)}) custom-call(f32[19,8,16,256]{3,2,1,0:T(8,128)} %get-tuple-element.41.fluid_so_far, f32[19,10,2,32,128]{4,3,2,1,0:T(8,128)S(1)} %get-tuple-element.42.second_so_far, ...), custom_call_target="tpu_custom_call", output_to_operand_aliasing={{0}: (0, {}), {1}: (1, {})} | custom-call | bytes 8388608 | tf_op jit(solution)/shard_map/pallas_call | solution.py:960
  38.7 6.0 %all-to-all-start = ((f32[128,1,128]{2,1,0:T(1,128)}), f32[128,1,128]{2,1,0:T(1,128)S(1)}, u32[]{:S(2)}, u32[]{:S(2)}) async-start(f32[128,1,128]{2,1,0:T(1,128)} %get-tuple-element.54), calls=%async_computation | async-start | bytes 131072 | tf_op jit(solution)/shard_map/all_to_all | solution.py:1095
  44.7 0.0 collective-permute-done.6.near_e
  44.7 0.0 collective-permute-done.7.far_e
  44.7 4.9 %shard_map.110 = (f32[16,16,256]{2,1,0:T(8,128)S(1)}, f32[3,20,2,24,128]{4,3,2,1,0:T(8,128)S(1)}, f32[9,8,128]{2,1,0:T(8,128)S(1)}) custom-call(f32[16,16,256]{2,1,0:T(8,128)} %temp_far.5, s32[16,16,256]{2,1,0:T(8,128)} %mat_far.5, f32[2,104,128]{2,1,0:T(8,128)S(1)} %collective-permute-done.2.near_s, f32[2,104,128]{2,1,0:T(8,128)S(1)} %collective-permute-done.3.far_s, ...), custom_call_target="tpu_custom_call" | custom-call | bytes 8388608 | tf_op jit(solution)/shard_map/pallas_call | solution.py:960
  49.6 1.1 %copy-done = f32[3,20,2,24,128]{4,3,2,1,0:T(8,128)} copy-done((f32[3,20,2,24,128]{4,3,2,1,0:T(8,128)}, f32[3,20,2,24,128]{4,3,2,1,0:T(8,128)S(1)}, u32[]{:S(2)}) %copy-start) | copy-done | bytes 1474584
  50.7 0.7 %copy-done.1 = f32[16,16,256]{2,1,0:T(8,128)} copy-done((f32[16,16,256]{2,1,0:T(8,128)}, f32[16,16,256]{2,1,0:T(8,128)S(1)}, u32[]{:S(2)}) %copy-start.1) | copy-done | bytes 262168
  51.4 2.9 %all-to-all-done.arrived = f32[128,1,128]{2,1,0:T(1,128)S(1)} async-done(((f32[128,1,128]{2,1,0:T(1,128)}), f32[128,1,128]{2,1,0:T(1,128)S(1)}, u32[]{:S(2)}, u32[]{:S(2)}) %all-to-all-start) | async-done | bytes 65568 | tf_op jit(solution)/shard_map/all_to_all | solution.py:1095
  54.3 3.7 %shard_map.111 = f32[16,16,256]{2,1,0:T(8,128)} custom-call(f32[16,16,256]{2,1,0:T(8,128)} %copy-done.1, f32[3,20,2,24,128]{4,3,2,1,0:T(8,128)} %copy-done, f32[128,1,128]{2,1,0:T(1,128)S(1)} %all-to-all-done.arrived, f32[9,8,128]{2,1,0:T(8,128)S(1)} %get-tuple-element.55.all_cells), custom_call_target="tpu_custom_call" | custom-call | bytes 8388608 | tf_op jit(solution)/shard_map/pallas_call | solution.py:960
  (10 shorter events, 0.1 us)
Async XLA Ops:
  0.6 8.7 %copy-start.6 = (s32[1024]{0:T(1024)S(1)}, s32[1024]{0:T(1024)}, u32[]{:S(2)}) copy-start(s32[1024]{0:T(1024)} %param.15) | copy-start | bytes 12292
  3.5 17.7 %collective-permute-start = (f32[2,208,128]{2,1,0:T(8,128)}, f32[2,208,128]{2,1,0:T(8,128)S(1)}, u32[]{:S(2)}, u32[]{:S(2)}) collective-permute-start(f32[2,208,128]{2,1,0:T(8,128)} %get-tuple-element.31), channel_id=1, source_target_pairs={{0,1},{1,0},{2,3},{3,2},{4,5},{5,4},{6,7},{7,6},{8,9},{9,8},{10,11... | collective-permute-start | bytes 638984 | tf_op jit(solution)/shard_map/ppermute | solution.py:968
  5.7 15.5 %collective-permute-start.1 = (f32[2,208,128]{2,1,0:T(8,128)S(1)}, f32[2,208,128]{2,1,0:T(8,128)S(1)}, u32[]{:S(2)}, u32[]{:S(2)}) collective-permute-start(f32[2,208,128]{2,1,0:T(8,128)S(1)} %get-tuple-element.32), channel_id=1, source_target_pairs={{0,7},{1,2},{2,1},{3,4},{4,3},{5,6},{6,5},{7,0},{8,15},{9,10},{10,... | collective-permute-start | bytes 638984 | tf_op jit(solution)/shard_map/ppermute | solution.py:968
  10.4 4.2 %collective-permute-start.2 = (f32[2,104,128]{2,1,0:T(8,128)S(1)}, f32[2,104,128]{2,1,0:T(8,128)S(1)}, u32[]{:S(2)}, u32[]{:S(2)}) collective-permute-start(f32[2,104,128]{2,1,0:T(8,128)S(1)} %get-tuple-element.34), channel_id=1, source_target_pairs={{0,8},{8,0},{16,24},{24,16},{32,40},{40,32},{48,56},{56,48},{64,72... | collective-permute-start | bytes 319496 | tf_op jit(solution)/shard_map/ppermute | solution.py:968
  11.8 9.4 %collective-permute-start.3 = (f32[2,104,128]{2,1,0:T(8,128)S(1)}, f32[2,104,128]{2,1,0:T(8,128)S(1)}, u32[]{:S(2)}, u32[]{:S(2)}) collective-permute-start(f32[2,104,128]{2,1,0:T(8,128)S(1)} %get-tuple-element.35), channel_id=1, source_target_pairs={{0,120},{8,16},{16,8},{24,32},{32,24},{40,48},{48,40},{56,64},{64,... | collective-permute-start | bytes 319496 | tf_op jit(solution)/shard_map/ppermute | solution.py:968
  22.5 10.0 %collective-permute-start.4 = (f32[2,264,128]{2,1,0:T(8,128)S(1)}, f32[2,264,128]{2,1,0:T(8,128)S(1)}, u32[]{:S(2)}, u32[]{:S(2)}) collective-permute-start(f32[2,264,128]{2,1,0:T(8,128)S(1)} %get-tuple-element.44), channel_id=1, source_target_pairs={{0,8},{8,0},{16,24},{24,16},{32,40},{40,32},{48,56},{56,48},{64,72... | collective-permute-start | bytes 811016 | tf_op jit(solution)/shard_map/ppermute | solution.py:968
  24.0 11.4 %collective-permute-start.5 = (f32[2,264,128]{2,1,0:T(8,128)S(1)}, f32[2,264,128]{2,1,0:T(8,128)S(1)}, u32[]{:S(2)}, u32[]{:S(2)}) collective-permute-start(f32[2,264,128]{2,1,0:T(8,128)S(1)} %get-tuple-element.45), channel_id=1, source_target_pairs={{0,120},{8,16},{16,8},{24,32},{32,24},{40,48},{48,40},{56,64},{64,... | collective-permute-start | bytes 811016 | tf_op jit(solution)/shard_map/ppermute | solution.py:968
  25.7 9.7 %copy-start.2 = (s32[512]{0:T(512)S(1)}, s32[512]{0:T(512)}, u32[]{:S(2)}) copy-start(s32[512]{0:T(512)} %param.11) | copy-start | bytes 6148
  25.7 9.7 %copy-start.3 = (f32[512]{0:T(512)S(1)}, f32[512]{0:T(512)}, u32[]{:S(2)}) copy-start(f32[512]{0:T(512)} %param.12) | copy-start | bytes 6148
  25.7 9.7 %copy-start.4 = (s32[512]{0:T(512)S(1)}, s32[512]{0:T(512)}, u32[]{:S(2)}) copy-start(s32[512]{0:T(512)} %param.13) | copy-start | bytes 6148
  25.7 9.7 %copy-start.5 = (s32[512]{0:T(512)S(1)}, s32[512]{0:T(512)}, u32[]{:S(2)}) copy-start(s32[512]{0:T(512)} %param.14) | copy-start | bytes 6148
  29.9 14.9 %collective-permute-start.6 = (f32[2,128,128]{2,1,0:T(8,128)S(1)}, f32[2,128,128]{2,1,0:T(8,128)S(1)}, u32[]{:S(2)}, u32[]{:S(2)}) collective-permute-start(f32[2,128,128]{2,1,0:T(8,128)S(1)} %get-tuple-element.50), channel_id=1, source_target_pairs={{0,1},{1,0},{2,3},{3,2},{4,5},{5,4},{6,7},{7,6},{8,9},{9,8},{10,11... | collective-permute-start | bytes 393224 | tf_op jit(solution)/shard_map/ppermute | solution.py:968
  30.0 14.8 %collective-permute-start.7 = (f32[2,128,128]{2,1,0:T(8,128)S(1)}, f32[2,128,128]{2,1,0:T(8,128)S(1)}, u32[]{:S(2)}, u32[]{:S(2)}) collective-permute-start(f32[2,128,128]{2,1,0:T(8,128)S(1)} %get-tuple-element.51), channel_id=1, source_target_pairs={{0,7},{1,2},{2,1},{3,4},{4,3},{5,6},{6,5},{7,0},{8,15},{9,10},{10,... | collective-permute-start | bytes 393224 | tf_op jit(solution)/shard_map/ppermute | solution.py:968
  38.7 15.6 %all-to-all-start = ((f32[128,1,128]{2,1,0:T(1,128)}), f32[128,1,128]{2,1,0:T(1,128)S(1)}, u32[]{:S(2)}, u32[]{:S(2)}) async-start(f32[128,1,128]{2,1,0:T(1,128)} %get-tuple-element.54), calls=%async_computation | async-start | bytes 131072 | tf_op jit(solution)/shard_map/all_to_all | solution.py:1095
  49.6 1.1 %copy-start = (f32[3,20,2,24,128]{4,3,2,1,0:T(8,128)}, f32[3,20,2,24,128]{4,3,2,1,0:T(8,128)S(1)}, u32[]{:S(2)}) copy-start(f32[3,20,2,24,128]{4,3,2,1,0:T(8,128)S(1)} %get-tuple-element.53.links_far) | copy-start | bytes 4423684
  50.7 0.7 %copy-start.1 = (f32[16,16,256]{2,1,0:T(8,128)}, f32[16,16,256]{2,1,0:T(8,128)S(1)}, u32[]{:S(2)}) copy-start(f32[16,16,256]{2,1,0:T(8,128)S(1)} %get-tuple-element.52.swept_far) | copy-start | bytes 786436

commit v4 on v3

--- a/solution.py
+++ b/solution.py
@@ -803,13 +803,15 @@
     links_far,
     arrived,
     all_cells,
-    solid_out,
+    solid_far,
     heat,
     other,
     came,
     swept,
     links,
+    solid_out,
     brought,
+    taken,
 ):
     groups = [
         pltpu.make_async_copy(
@@ -932,7 +934,16 @@
                 )
         return carry
 
-    lax.fori_loop(0, SA, final, 0, unroll=4)
+    quarters = []
+    for n in range(4):
+        at = pl.ds(4 * n, 4)
+        lax.fori_loop(4 * n, 4 * n + 4, final, 0, unroll=4)
+        quarters.append(
+            pltpu.make_async_copy(solid_out.at[at], solid_far.at[at], taken.at[n])
+        )
+        quarters[-1].start()
+    for copy in quarters:
+        copy.wait()
 
 
 def call(
@@ -965,6 +976,8 @@
 def swap(values, axis, far):
     count = lax.axis_size(axis)
     pairs = [(i, (((i + 1) ^ 1) - 1) % count if far else i ^ 1) for i in range(count)]
+    if axis == "axial" and far:
+        pairs[0], pairs[-1] = (0, 0), (count - 1, count - 1)
     return lax.ppermute(values, axis, pairs)
 
 
@@ -1119,10 +1132,13 @@
             VMEM((devices, 128), f32),
             VMEM(solid, f32),
             VMEM(link_shape, f32),
+            VMEM(solid, f32),
             pltpu.SemaphoreType.DMA((5,)),
+            pltpu.SemaphoreType.DMA((4,)),
         ],
         moved=8 << 20,
         far_ins=2,
+        far_outs=1,
     )(swept, links, arrived, all_cells)
     return fluid_out, solid_out
 

time: 58.3 us -> 58.2 us (level)
  starting transfers between devices: 21.8 us -> 26.4 us
  waiting for transfers between devices: 12.4 us -> 8.13 us
    all_to_all x1, starting transfers between devices: 5.98 us -> 12.7 us  [per_device(): lax.all_to_all(message, ('azim', 'axial'), split_axis=0, concat_axis=0, t...]
    ppermute x8, waiting for transfers between devices: 9.52 us -> 5.23 us  [swap(): return lax.ppermute(values, axis, pairs)]
    ppermute x8, starting transfers between devices: 15.9 us -> 13.6 us  [swap(): return lax.ppermute(values, axis, pairs)]
  transfers between devices with their start and end apart: 9 -> 9, of which waited for: 3 -> 2; matrix products, arithmetic and copies ran while one was open for 0% -> 0% of each run, Pallas kernels for 23% -> 23%
where the time goes in v4:
time: 58.2 us; the launch traced here: 57.9 us
  starting transfers between devices  26.4 us (45%)
  Pallas kernels  20.6 us (35%)
  waiting for transfers between devices  8.13 us (14%)
  local copies, waits for them, and re-layouts  1.98 us (3%)
  between operations  0.82 us (1%)
    pallas_call x8, Pallas kernels, run(): return kernel_call(*far, *args[far_ins:])  20.6 us
    ppermute x8, starting transfers between devices, swap(): return lax.ppermute(values, axis, pairs)  13.6 us
    all_to_all x1, starting transfers between devices, per_device(): lax.all_to_all(message, ('azim', 'axial'), split_axis=0, concat_axis=0, t...  12.7 us
    ppermute x8, waiting for transfers between devices, swap(): return lax.ppermute(values, axis, pairs)  5.23 us
    all_to_all x1, waiting for transfers between devices, per_device(): lax.all_to_all(message, ('azim', 'axial'), split_axis=0, concat_axis=0, t...  2.9 us
    unnamed x14, local copies, waits for them, and re-layouts  1.85 us
  transfers between devices with their start and end apart: 9, of which 2 were waited for; matrix products, arithmetic and copies ran while one was open for 0% of the time, Pallas kernels for 23%

profile of v4, /device:TPU:1, one launch (start us, length us, event | category | flops | bytes accessed | tf_op | source)
XLA Modules:
  0.0 57.9 jit_solution(5356226677638881100)
XLA Ops:
  0.6 0.0 copy-start.6
  0.6 2.8 %shard_map.104 = (f32[19,8,2,16,128]{4,3,2,1,0:T(8,128)S(1)}, f32[8,2,16,128]{3,2,1,0:T(8,128)S(1)}, f32[2,208,128]{2,1,0:T(8,128)}, f32[2,208,128]{2,1,0:T(8,128)S(1)}, f32[8,128]{1,0:T(8,128)S(1)}) custom-call(f32[19,8,16,256]{3,2,1,0:T(8,128)} %f_far.1, s32[8,16,256]{2,1,0:T(8,128)} %flags_far.1), custom_call_target="tpu_custom_call" | custom-call | bytes 8388608 | tf_op jit(solution)/shard_map/pallas_call | solution.py:971
  3.5 2.2 %collective-permute-start = (f32[2,208,128]{2,1,0:T(8,128)}, f32[2,208,128]{2,1,0:T(8,128)S(1)}, u32[]{:S(2)}, u32[]{:S(2)}) collective-permute-start(f32[2,208,128]{2,1,0:T(8,128)} %get-tuple-element.31), channel_id=1, source_target_pairs={{0,1},{1,0},{2,3},{3,2},{4,5},{5,4},{6,7},{7,6},{8,9},{9,8},{10,11... | collective-permute-start | bytes 638984 | tf_op jit(solution)/shard_map/ppermute | solution.py:981
  5.7 0.7 %collective-permute-start.1 = (f32[2,208,128]{2,1,0:T(8,128)S(1)}, f32[2,208,128]{2,1,0:T(8,128)S(1)}, u32[]{:S(2)}, u32[]{:S(2)}) collective-permute-start(f32[2,208,128]{2,1,0:T(8,128)S(1)} %get-tuple-element.32), channel_id=1, source_target_pairs={{0,0},{1,2},{2,1},{3,4},{4,3},{5,6},{6,5},{7,7},{8,8},{9,10},{10,9... | collective-permute-start | bytes 638984 | tf_op jit(solution)/shard_map/ppermute | solution.py:981
  6.4 0.0 copy-done.6
  6.4 0.1 reshape.19
  6.5 1.0 %shard_map.105 = (f32[2,104,128]{2,1,0:T(8,128)S(1)}, f32[2,104,128]{2,1,0:T(8,128)S(1)}, f32[8,128]{1,0:T(8,128)S(1)}) custom-call(f32[16,16,256]{2,1,0:T(8,128)} %temp_far.5, s32[16,16,256]{2,1,0:T(8,128)} %mat_far.5, s32[8,128]{1,0:T(8,128)S(1)} %bitcast.5, f32[8,128]{1,0:T(8,128)S(1)} %get-tuple-element.33.token), custom_call_target="tpu_custom_call" | custom-call | bytes 2097152 | tf_op jit(solution)/shard_map/pallas_call | solution.py:971
  7.5 1.0 %collective-permute-start.2 = (f32[2,104,128]{2,1,0:T(8,128)S(1)}, f32[2,104,128]{2,1,0:T(8,128)S(1)}, u32[]{:S(2)}, u32[]{:S(2)}) collective-permute-start(f32[2,104,128]{2,1,0:T(8,128)S(1)} %get-tuple-element.34), channel_id=1, source_target_pairs={{0,8},{8,0},{16,24},{24,16},{32,40},{40,32},{48,56},{56,48},{64,72... | collective-permute-start | bytes 319496 | tf_op jit(solution)/shard_map/ppermute | solution.py:981
  8.5 2.6 %collective-permute-start.3 = (f32[2,104,128]{2,1,0:T(8,128)S(1)}, f32[2,104,128]{2,1,0:T(8,128)S(1)}, u32[]{:S(2)}, u32[]{:S(2)}) collective-permute-start(f32[2,104,128]{2,1,0:T(8,128)S(1)} %get-tuple-element.35), channel_id=1, source_target_pairs={{0,120},{8,16},{16,8},{24,32},{32,24},{40,48},{48,40},{56,64},{64,... | collective-permute-start | bytes 319496 | tf_op jit(solution)/shard_map/ppermute | solution.py:981
  11.1 0.0 collective-permute-done.2.near_s
  11.1 5.2 %collective-permute-done.3.far_s = f32[2,104,128]{2,1,0:T(8,128)S(1)} collective-permute-done((f32[2,104,128]{2,1,0:T(8,128)S(1)}, f32[2,104,128]{2,1,0:T(8,128)S(1)}, u32[]{:S(2)}, u32[]{:S(2)}) %collective-permute-start.3) | collective-permute-done | bytes 106528 | tf_op jit(solution)/shard_map/ppermute | solution.py:981
  16.3 0.0 collective-permute-done.near_z
  16.3 0.0 collective-permute-done.1.far_z
  16.3 1.3 %shard_map.106 = (f32[19,8,2,32,128]{4,3,2,1,0:T(8,128)S(1)}, f32[3,8,2,32,128]{4,3,2,1,0:T(8,128)S(1)}, f32[2,264,128]{2,1,0:T(8,128)S(1)}, f32[2,264,128]{2,1,0:T(8,128)S(1)}) custom-call(f32[19,8,2,16,128]{4,3,2,1,0:T(8,128)S(1)} %get-tuple-element.29.post, f32[8,2,16,128]{3,2,1,0:T(8,128)S(1)} %get-tuple-element.30.air, ...), custom_call_target="tpu_custom_call" | custom-call | bytes 8388608 | tf_op jit(solution)/shard_map/pallas_call | solution.py:971
  17.6 0.2 collective-permute-start.4
  17.8 1.6 %collective-permute-start.5 = (f32[2,264,128]{2,1,0:T(8,128)S(1)}, f32[2,264,128]{2,1,0:T(8,128)S(1)}, u32[]{:S(2)}, u32[]{:S(2)}) collective-permute-start(f32[2,264,128]{2,1,0:T(8,128)S(1)} %get-tuple-element.45), channel_id=1, source_target_pairs={{0,120},{8,16},{16,8},{24,32},{32,24},{40,48},{48,40},{56,64},{64,... | collective-permute-start | bytes 811016 | tf_op jit(solution)/shard_map/ppermute | solution.py:981
  19.5 2.9 %shard_map.107 = (f32[19,8,16,256]{3,2,1,0:T(8,128)}, f32[19,10,2,32,128]{4,3,2,1,0:T(8,128)S(1)}, f32[128,256]{1,0:T(8,128)S(1)}, f32[8,128]{1,0:T(8,128)S(1)}) custom-call(f32[19,8,2,32,128]{4,3,2,1,0:T(8,128)S(1)} %get-tuple-element.39.ext, f32[3,8,2,32,128]{4,3,2,1,0:T(8,128)S(1)} %get-tuple-element.40.opened.own_opened), custom_call_target="tpu_custom_call" | custom-call | bytes 12582912 | tf_op jit(solution)/shard_map/pallas_call | solution.py:971
  22.4 1.2 %shard_map.109 = (f32[2,128,128]{2,1,0:T(8,128)S(1)}, f32[2,128,128]{2,1,0:T(8,128)S(1)}) custom-call(f32[16,16,256]{2,1,0:T(8,128)} %temp_far.5, s32[16,16,256]{2,1,0:T(8,128)} %mat_far.5, s32[8,128]{1,0:T(8,128)S(1)} %bitcast.6, f32[2,104,128]{2,1,0:T(8,128)S(1)} %collective-permute-done.2.near_s, f32[2,104,128]{2,1,0:T(8,128)S(1)} %collective-permute-done.3.far_s, ...), custom_call_target="tpu_custom_call" | custom-call | bytes 2097152 | tf_op jit(solution)/shard_map/pallas_call | solution.py:971
  23.6 4.6 %collective-permute-start.6 = (f32[2,128,128]{2,1,0:T(8,128)S(1)}, f32[2,128,128]{2,1,0:T(8,128)S(1)}, u32[]{:S(2)}, u32[]{:S(2)}) collective-permute-start(f32[2,128,128]{2,1,0:T(8,128)S(1)} %get-tuple-element.50), channel_id=1, source_target_pairs={{0,1},{1,0},{2,3},{3,2},{4,5},{5,4},{6,7},{7,6},{8,9},{9,8},{10,11... | collective-permute-start | bytes 393224 | tf_op jit(solution)/shard_map/ppermute | solution.py:981
  28.2 0.7 %collective-permute-start.7 = (f32[2,128,128]{2,1,0:T(8,128)S(1)}, f32[2,128,128]{2,1,0:T(8,128)S(1)}, u32[]{:S(2)}, u32[]{:S(2)}) collective-permute-start(f32[2,128,128]{2,1,0:T(8,128)S(1)} %get-tuple-element.51), channel_id=1, source_target_pairs={{0,0},{1,2},{2,1},{3,4},{4,3},{5,6},{6,5},{7,7},{8,8},{9,10},{10,9... | collective-permute-start | bytes 393224 | tf_op jit(solution)/shard_map/ppermute | solution.py:981
  28.9 0.0 collective-permute-done.4.near_a
  28.9 0.0 collective-permute-done.5.far_a
  28.9 0.0 copy-done.2
  28.9 3.3 %shard_map.108 = (f32[19,8,16,256]{3,2,1,0:T(8,128)}, f32[19,10,2,32,128]{4,3,2,1,0:T(8,128)S(1)}, f32[128,1,128]{2,1,0:T(1,128)}) custom-call(f32[19,8,16,256]{3,2,1,0:T(8,128)} %get-tuple-element.41.fluid_so_far, f32[19,10,2,32,128]{4,3,2,1,0:T(8,128)S(1)} %get-tuple-element.42.second_so_far, ...), custom_call_target="tpu_custom_call", output_to_operand_aliasing={{0}: (0, {}), {1}: (1, {})} | custom-call | bytes 8388608 | tf_op jit(solution)/shard_map/pallas_call | solution.py:971
  32.2 12.7 %all-to-all-start = ((f32[128,1,128]{2,1,0:T(1,128)}), f32[128,1,128]{2,1,0:T(1,128)S(1)}, u32[]{:S(2)}, u32[]{:S(2)}) async-start(f32[128,1,128]{2,1,0:T(1,128)} %get-tuple-element.54), calls=%async_computation | async-start | bytes 131072 | tf_op jit(solution)/shard_map/all_to_all | solution.py:1108
  45.0 0.0 collective-permute-done.6.near_e
  45.0 0.0 collective-permute-done.7.far_e
  45.0 4.9 %shard_map.110 = (f32[16,16,256]{2,1,0:T(8,128)S(1)}, f32[3,20,2,24,128]{4,3,2,1,0:T(8,128)S(1)}, f32[9,8,128]{2,1,0:T(8,128)S(1)}) custom-call(f32[16,16,256]{2,1,0:T(8,128)} %temp_far.5, s32[16,16,256]{2,1,0:T(8,128)} %mat_far.5, f32[2,104,128]{2,1,0:T(8,128)S(1)} %collective-permute-done.2.near_s, f32[2,104,128]{2,1,0:T(8,128)S(1)} %collective-permute-done.3.far_s, ...), custom_call_target="tpu_custom_call" | custom-call | bytes 8388608 | tf_op jit(solution)/shard_map/pallas_call | solution.py:971
  49.9 1.1 %copy-done = f32[3,20,2,24,128]{4,3,2,1,0:T(8,128)} copy-done((f32[3,20,2,24,128]{4,3,2,1,0:T(8,128)}, f32[3,20,2,24,128]{4,3,2,1,0:T(8,128)S(1)}, u32[]{:S(2)}) %copy-start) | copy-done | bytes 1474584
  51.0 0.7 %copy-done.1 = f32[16,16,256]{2,1,0:T(8,128)} copy-done((f32[16,16,256]{2,1,0:T(8,128)}, f32[16,16,256]{2,1,0:T(8,128)S(1)}, u32[]{:S(2)}) %copy-start.1) | copy-done | bytes 262168
  51.7 2.9 %all-to-all-done.arrived = f32[128,1,128]{2,1,0:T(1,128)S(1)} async-done(((f32[128,1,128]{2,1,0:T(1,128)}), f32[128,1,128]{2,1,0:T(1,128)S(1)}, u32[]{:S(2)}, u32[]{:S(2)}) %all-to-all-start) | async-done | bytes 65568 | tf_op jit(solution)/shard_map/all_to_all | solution.py:1108
  54.6 3.3 %shard_map.111 = f32[16,16,256]{2,1,0:T(8,128)} custom-call(f32[16,16,256]{2,1,0:T(8,128)} %copy-done.1, f32[3,20,2,24,128]{4,3,2,1,0:T(8,128)} %copy-done, f32[128,1,128]{2,1,0:T(1,128)S(1)} %all-to-all-done.arrived, f32[9,8,128]{2,1,0:T(8,128)S(1)} %get-tuple-element.55.all_cells), custom_call_target="tpu_custom_call" | custom-call | bytes 8388608 | tf_op jit(solution)/shard_map/pallas_call | solution.py:971
  (10 shorter events, 0.1 us)
Async XLA Ops:
  0.6 5.7 %copy-start.6 = (s32[1024]{0:T(1024)S(1)}, s32[1024]{0:T(1024)}, u32[]{:S(2)}) copy-start(s32[1024]{0:T(1024)} %param.15) | copy-start | bytes 12292
  3.5 12.8 %collective-permute-start = (f32[2,208,128]{2,1,0:T(8,128)}, f32[2,208,128]{2,1,0:T(8,128)S(1)}, u32[]{:S(2)}, u32[]{:S(2)}) collective-permute-start(f32[2,208,128]{2,1,0:T(8,128)} %get-tuple-element.31), channel_id=1, source_target_pairs={{0,1},{1,0},{2,3},{3,2},{4,5},{5,4},{6,7},{7,6},{8,9},{9,8},{10,11... | collective-permute-start | bytes 638984 | tf_op jit(solution)/shard_map/ppermute | solution.py:981
  5.7 10.6 %collective-permute-start.1 = (f32[2,208,128]{2,1,0:T(8,128)S(1)}, f32[2,208,128]{2,1,0:T(8,128)S(1)}, u32[]{:S(2)}, u32[]{:S(2)}) collective-permute-start(f32[2,208,128]{2,1,0:T(8,128)S(1)} %get-tuple-element.32), channel_id=1, source_target_pairs={{0,0},{1,2},{2,1},{3,4},{4,3},{5,6},{6,5},{7,7},{8,8},{9,10},{10,9... | collective-permute-start | bytes 638984 | tf_op jit(solution)/shard_map/ppermute | solution.py:981
  7.5 3.6 %collective-permute-start.2 = (f32[2,104,128]{2,1,0:T(8,128)S(1)}, f32[2,104,128]{2,1,0:T(8,128)S(1)}, u32[]{:S(2)}, u32[]{:S(2)}) collective-permute-start(f32[2,104,128]{2,1,0:T(8,128)S(1)} %get-tuple-element.34), channel_id=1, source_target_pairs={{0,8},{8,0},{16,24},{24,16},{32,40},{40,32},{48,56},{56,48},{64,72... | collective-permute-start | bytes 319496 | tf_op jit(solution)/shard_map/ppermute | solution.py:981
  8.5 7.8 %collective-permute-start.3 = (f32[2,104,128]{2,1,0:T(8,128)S(1)}, f32[2,104,128]{2,1,0:T(8,128)S(1)}, u32[]{:S(2)}, u32[]{:S(2)}) collective-permute-start(f32[2,104,128]{2,1,0:T(8,128)S(1)} %get-tuple-element.35), channel_id=1, source_target_pairs={{0,120},{8,16},{16,8},{24,32},{32,24},{40,48},{48,40},{56,64},{64,... | collective-permute-start | bytes 319496 | tf_op jit(solution)/shard_map/ppermute | solution.py:981
  17.6 11.3 %collective-permute-start.4 = (f32[2,264,128]{2,1,0:T(8,128)S(1)}, f32[2,264,128]{2,1,0:T(8,128)S(1)}, u32[]{:S(2)}, u32[]{:S(2)}) collective-permute-start(f32[2,264,128]{2,1,0:T(8,128)S(1)} %get-tuple-element.44), channel_id=1, source_target_pairs={{0,8},{8,0},{16,24},{24,16},{32,40},{40,32},{48,56},{56,48},{64,72... | collective-permute-start | bytes 811016 | tf_op jit(solution)/shard_map/ppermute | solution.py:981
  17.8 11.1 %collective-permute-start.5 = (f32[2,264,128]{2,1,0:T(8,128)S(1)}, f32[2,264,128]{2,1,0:T(8,128)S(1)}, u32[]{:S(2)}, u32[]{:S(2)}) collective-permute-start(f32[2,264,128]{2,1,0:T(8,128)S(1)} %get-tuple-element.45), channel_id=1, source_target_pairs={{0,120},{8,16},{16,8},{24,32},{32,24},{40,48},{48,40},{56,64},{64,... | collective-permute-start | bytes 811016 | tf_op jit(solution)/shard_map/ppermute | solution.py:981
  19.4 9.5 %copy-start.2 = (s32[512]{0:T(512)S(1)}, s32[512]{0:T(512)}, u32[]{:S(2)}) copy-start(s32[512]{0:T(512)} %param.11) | copy-start | bytes 6148
  19.4 9.5 %copy-start.3 = (f32[512]{0:T(512)S(1)}, f32[512]{0:T(512)}, u32[]{:S(2)}) copy-start(f32[512]{0:T(512)} %param.12) | copy-start | bytes 6148
  19.4 9.5 %copy-start.4 = (s32[512]{0:T(512)S(1)}, s32[512]{0:T(512)}, u32[]{:S(2)}) copy-start(s32[512]{0:T(512)} %param.13) | copy-start | bytes 6148
  19.4 9.5 %copy-start.5 = (s32[512]{0:T(512)S(1)}, s32[512]{0:T(512)}, u32[]{:S(2)}) copy-start(s32[512]{0:T(512)} %param.14) | copy-start | bytes 6148
  23.6 21.4 %collective-permute-start.6 = (f32[2,128,128]{2,1,0:T(8,128)S(1)}, f32[2,128,128]{2,1,0:T(8,128)S(1)}, u32[]{:S(2)}, u32[]{:S(2)}) collective-permute-start(f32[2,128,128]{2,1,0:T(8,128)S(1)} %get-tuple-element.50), channel_id=1, source_target_pairs={{0,1},{1,0},{2,3},{3,2},{4,5},{5,4},{6,7},{7,6},{8,9},{9,8},{10,11... | collective-permute-start | bytes 393224 | tf_op jit(solution)/shard_map/ppermute | solution.py:981
  28.2 16.8 %collective-permute-start.7 = (f32[2,128,128]{2,1,0:T(8,128)S(1)}, f32[2,128,128]{2,1,0:T(8,128)S(1)}, u32[]{:S(2)}, u32[]{:S(2)}) collective-permute-start(f32[2,128,128]{2,1,0:T(8,128)S(1)} %get-tuple-element.51), channel_id=1, source_target_pairs={{0,0},{1,2},{2,1},{3,4},{4,3},{5,6},{6,5},{7,7},{8,8},{9,10},{10,9... | collective-permute-start | bytes 393224 | tf_op jit(solution)/shard_map/ppermute | solution.py:981
  32.2 22.4 %all-to-all-start = ((f32[128,1,128]{2,1,0:T(1,128)}), f32[128,1,128]{2,1,0:T(1,128)S(1)}, u32[]{:S(2)}, u32[]{:S(2)}) async-start(f32[128,1,128]{2,1,0:T(1,128)} %get-tuple-element.54), calls=%async_computation | async-start | bytes 131072 | tf_op jit(solution)/shard_map/all_to_all | solution.py:1108
  49.9 1.1 %copy-start = (f32[3,20,2,24,128]{4,3,2,1,0:T(8,128)}, f32[3,20,2,24,128]{4,3,2,1,0:T(8,128)S(1)}, u32[]{:S(2)}) copy-start(f32[3,20,2,24,128]{4,3,2,1,0:T(8,128)S(1)} %get-tuple-element.53.links_far) | copy-start | bytes 4423684
  51.0 0.7 %copy-start.1 = (f32[16,16,256]{2,1,0:T(8,128)}, f32[16,16,256]{2,1,0:T(8,128)S(1)}, u32[]{:S(2)}) copy-start(f32[16,16,256]{2,1,0:T(8,128)S(1)} %get-tuple-element.52.swept_far) | copy-start | bytes 786436

commit v5 on v4

--- a/solution.py
+++ b/solution.py
@@ -346,7 +346,7 @@
             opened[0, a, half, to, :] = air[a, half]
         return carry
 
-    lax.fori_loop(0, CA, own_layer, 0)
+    lax.fori_loop(0, CA, own_layer, 0, unroll=4)
 
     def axial_rim(lower, upper):
         def layer(a, carry):
@@ -368,14 +368,14 @@
                     opened[0, a, half, pl.ds(last, 1), :] = get(25) * there
             return carry
 
-        lax.fori_loop(0, CA, layer, 0, unroll=2)
+        lax.fori_loop(0, CA, layer, 0, unroll=4)
     by_parity("axial", axial_rim, near_z, far_z)
 
     def turn(a, carry):
         turn_flags(opened, a, lane)
         return carry
 
-    lax.fori_loop(0, CA, turn, 0, unroll=2)
+    lax.fori_loop(0, CA, turn, 0, unroll=8)
 
     for target, layer, moving, step in (
         (low, 0, AZIM_DOWN, -1),
@@ -504,7 +504,7 @@
                 opened[k, a + 1, half] = own_opened[k, a, half]
         return carry
 
-    lax.fori_loop(0, CA, own_flags, 0, unroll=2)
+    lax.fori_loop(0, CA, own_flags, 0, unroll=8)
 
     def azim_rim(lower, upper):
         for side, (source, a) in enumerate(((lower, 0), (upper, CA + 1))):
@@ -578,7 +578,7 @@
             layer_copy(at, layer).start()
             return carry
 
-        lax.fori_loop(0, 2, second_step, 0)
+        lax.fori_loop(0, 2, second_step, 0, unroll=2)
 
 
     rows_here = cell.shape[1]

time: 58.2 us -> 57.8 us (level)
  no operation moved by 1% of the time
where the time goes in v5:
time: 57.8 us; the launch traced here: 57.6 us
  starting transfers between devices  26.4 us (46%)
  Pallas kernels  20.3 us (35%)
  waiting for transfers between devices  8.13 us (14%)
  local copies, waits for them, and re-layouts  1.98 us (3%)
  between operations  0.82 us (1%)
    pallas_call x8, Pallas kernels, run(): return kernel_call(*far, *args[far_ins:])  20.3 us
    ppermute x8, starting transfers between devices, swap(): return lax.ppermute(values, axis, pairs)  13.6 us
    all_to_all x1, starting transfers between devices, per_device(): lax.all_to_all(message, ('azim', 'axial'), split_axis=0, concat_axis=0, t...  12.8 us
    ppermute x8, waiting for transfers between devices, swap(): return lax.ppermute(values, axis, pairs)  5.23 us
    all_to_all x1, waiting for transfers between devices, per_device(): lax.all_to_all(message, ('azim', 'axial'), split_axis=0, concat_axis=0, t...  2.9 us
    unnamed x14, local copies, waits for them, and re-layouts  1.85 us
  transfers between devices with their start and end apart: 9, of which 2 were waited for; matrix products, arithmetic and copies ran while one was open for 0% of the time, Pallas kernels for 23%

profile of v5, /device:TPU:1, one launch (start us, length us, event | category | flops | bytes accessed | tf_op | source)
XLA Modules:
  0.0 57.6 jit_solution(12947677798645288658)
XLA Ops:
  0.6 0.0 copy-start.6
  0.6 2.8 %shard_map.104 = (f32[19,8,2,16,128]{4,3,2,1,0:T(8,128)S(1)}, f32[8,2,16,128]{3,2,1,0:T(8,128)S(1)}, f32[2,208,128]{2,1,0:T(8,128)}, f32[2,208,128]{2,1,0:T(8,128)S(1)}, f32[8,128]{1,0:T(8,128)S(1)}) custom-call(f32[19,8,16,256]{3,2,1,0:T(8,128)} %f_far.1, s32[8,16,256]{2,1,0:T(8,128)} %flags_far.1), custom_call_target="tpu_custom_call" | custom-call | bytes 8388608 | tf_op jit(solution)/shard_map/pallas_call | solution.py:971
  3.5 2.2 %collective-permute-start = (f32[2,208,128]{2,1,0:T(8,128)}, f32[2,208,128]{2,1,0:T(8,128)S(1)}, u32[]{:S(2)}, u32[]{:S(2)}) collective-permute-start(f32[2,208,128]{2,1,0:T(8,128)} %get-tuple-element.31), channel_id=1, source_target_pairs={{0,1},{1,0},{2,3},{3,2},{4,5},{5,4},{6,7},{7,6},{8,9},{9,8},{10,11... | collective-permute-start | bytes 638984 | tf_op jit(solution)/shard_map/ppermute | solution.py:981
  5.7 0.7 %collective-permute-start.1 = (f32[2,208,128]{2,1,0:T(8,128)S(1)}, f32[2,208,128]{2,1,0:T(8,128)S(1)}, u32[]{:S(2)}, u32[]{:S(2)}) collective-permute-start(f32[2,208,128]{2,1,0:T(8,128)S(1)} %get-tuple-element.32), channel_id=1, source_target_pairs={{0,0},{1,2},{2,1},{3,4},{4,3},{5,6},{6,5},{7,7},{8,8},{9,10},{10,9... | collective-permute-start | bytes 638984 | tf_op jit(solution)/shard_map/ppermute | solution.py:981
  6.4 0.0 copy-done.6
  6.4 0.1 reshape.19
  6.5 1.0 %shard_map.105 = (f32[2,104,128]{2,1,0:T(8,128)S(1)}, f32[2,104,128]{2,1,0:T(8,128)S(1)}, f32[8,128]{1,0:T(8,128)S(1)}) custom-call(f32[16,16,256]{2,1,0:T(8,128)} %temp_far.5, s32[16,16,256]{2,1,0:T(8,128)} %mat_far.5, s32[8,128]{1,0:T(8,128)S(1)} %bitcast.5, f32[8,128]{1,0:T(8,128)S(1)} %get-tuple-element.33.token), custom_call_target="tpu_custom_call" | custom-call | bytes 2097152 | tf_op jit(solution)/shard_map/pallas_call | solution.py:971
  7.5 1.0 %collective-permute-start.2 = (f32[2,104,128]{2,1,0:T(8,128)S(1)}, f32[2,104,128]{2,1,0:T(8,128)S(1)}, u32[]{:S(2)}, u32[]{:S(2)}) collective-permute-start(f32[2,104,128]{2,1,0:T(8,128)S(1)} %get-tuple-element.34), channel_id=1, source_target_pairs={{0,8},{8,0},{16,24},{24,16},{32,40},{40,32},{48,56},{56,48},{64,72... | collective-permute-start | bytes 319496 | tf_op jit(solution)/shard_map/ppermute | solution.py:981
  8.5 2.6 %collective-permute-start.3 = (f32[2,104,128]{2,1,0:T(8,128)S(1)}, f32[2,104,128]{2,1,0:T(8,128)S(1)}, u32[]{:S(2)}, u32[]{:S(2)}) collective-permute-start(f32[2,104,128]{2,1,0:T(8,128)S(1)} %get-tuple-element.35), channel_id=1, source_target_pairs={{0,120},{8,16},{16,8},{24,32},{32,24},{40,48},{48,40},{56,64},{64,... | collective-permute-start | bytes 319496 | tf_op jit(solution)/shard_map/ppermute | solution.py:981
  11.1 0.0 collective-permute-done.2.near_s
  11.1 5.2 %collective-permute-done.3.far_s = f32[2,104,128]{2,1,0:T(8,128)S(1)} collective-permute-done((f32[2,104,128]{2,1,0:T(8,128)S(1)}, f32[2,104,128]{2,1,0:T(8,128)S(1)}, u32[]{:S(2)}, u32[]{:S(2)}) %collective-permute-start.3) | collective-permute-done | bytes 106528 | tf_op jit(solution)/shard_map/ppermute | solution.py:981
  16.3 0.0 collective-permute-done.near_z
  16.3 0.0 collective-permute-done.1.far_z
  16.3 1.0 %shard_map.106 = (f32[19,8,2,32,128]{4,3,2,1,0:T(8,128)S(1)}, f32[3,8,2,32,128]{4,3,2,1,0:T(8,128)S(1)}, f32[2,264,128]{2,1,0:T(8,128)S(1)}, f32[2,264,128]{2,1,0:T(8,128)S(1)}) custom-call(f32[19,8,2,16,128]{4,3,2,1,0:T(8,128)S(1)} %get-tuple-element.29.post, f32[8,2,16,128]{3,2,1,0:T(8,128)S(1)} %get-tuple-element.30.air, ...), custom_call_target="tpu_custom_call" | custom-call | bytes 8388608 | tf_op jit(solution)/shard_map/pallas_call | solution.py:971
  17.4 0.2 collective-permute-start.4
  17.6 1.6 %collective-permute-start.5 = (f32[2,264,128]{2,1,0:T(8,128)S(1)}, f32[2,264,128]{2,1,0:T(8,128)S(1)}, u32[]{:S(2)}, u32[]{:S(2)}) collective-permute-start(f32[2,264,128]{2,1,0:T(8,128)S(1)} %get-tuple-element.45), channel_id=1, source_target_pairs={{0,120},{8,16},{16,8},{24,32},{32,24},{40,48},{48,40},{56,64},{64,... | collective-permute-start | bytes 811016 | tf_op jit(solution)/shard_map/ppermute | solution.py:981
  19.2 2.9 %shard_map.107 = (f32[19,8,16,256]{3,2,1,0:T(8,128)}, f32[19,10,2,32,128]{4,3,2,1,0:T(8,128)S(1)}, f32[128,256]{1,0:T(8,128)S(1)}, f32[8,128]{1,0:T(8,128)S(1)}) custom-call(f32[19,8,2,32,128]{4,3,2,1,0:T(8,128)S(1)} %get-tuple-element.39.ext, f32[3,8,2,32,128]{4,3,2,1,0:T(8,128)S(1)} %get-tuple-element.40.opened.own_opened), custom_call_target="tpu_custom_call" | custom-call | bytes 12582912 | tf_op jit(solution)/shard_map/pallas_call | solution.py:971
  22.1 1.2 %shard_map.109 = (f32[2,128,128]{2,1,0:T(8,128)S(1)}, f32[2,128,128]{2,1,0:T(8,128)S(1)}) custom-call(f32[16,16,256]{2,1,0:T(8,128)} %temp_far.5, s32[16,16,256]{2,1,0:T(8,128)} %mat_far.5, s32[8,128]{1,0:T(8,128)S(1)} %bitcast.6, f32[2,104,128]{2,1,0:T(8,128)S(1)} %collective-permute-done.2.near_s, f32[2,104,128]{2,1,0:T(8,128)S(1)} %collective-permute-done.3.far_s, ...), custom_call_target="tpu_custom_call" | custom-call | bytes 2097152 | tf_op jit(solution)/shard_map/pallas_call | solution.py:971
  23.3 4.6 %collective-permute-start.6 = (f32[2,128,128]{2,1,0:T(8,128)S(1)}, f32[2,128,128]{2,1,0:T(8,128)S(1)}, u32[]{:S(2)}, u32[]{:S(2)}) collective-permute-start(f32[2,128,128]{2,1,0:T(8,128)S(1)} %get-tuple-element.50), channel_id=1, source_target_pairs={{0,1},{1,0},{2,3},{3,2},{4,5},{5,4},{6,7},{7,6},{8,9},{9,8},{10,11... | collective-permute-start | bytes 393224 | tf_op jit(solution)/shard_map/ppermute | solution.py:981
  28.0 0.7 %collective-permute-start.7 = (f32[2,128,128]{2,1,0:T(8,128)S(1)}, f32[2,128,128]{2,1,0:T(8,128)S(1)}, u32[]{:S(2)}, u32[]{:S(2)}) collective-permute-start(f32[2,128,128]{2,1,0:T(8,128)S(1)} %get-tuple-element.51), channel_id=1, source_target_pairs={{0,0},{1,2},{2,1},{3,4},{4,3},{5,6},{6,5},{7,7},{8,8},{9,10},{10,9... | collective-permute-start | bytes 393224 | tf_op jit(solution)/shard_map/ppermute | solution.py:981
  28.6 0.0 collective-permute-done.4.near_a
  28.7 0.0 collective-permute-done.5.far_a
  28.7 3.1 %shard_map.108 = (f32[19,8,16,256]{3,2,1,0:T(8,128)}, f32[19,10,2,32,128]{4,3,2,1,0:T(8,128)S(1)}, f32[128,1,128]{2,1,0:T(1,128)}) custom-call(f32[19,8,16,256]{3,2,1,0:T(8,128)} %get-tuple-element.41.fluid_so_far, f32[19,10,2,32,128]{4,3,2,1,0:T(8,128)S(1)} %get-tuple-element.42.second_so_far, ...), custom_call_target="tpu_custom_call", output_to_operand_aliasing={{0}: (0, {}), {1}: (1, {})} | custom-call | bytes 8388608 | tf_op jit(solution)/shard_map/pallas_call | solution.py:971
  31.9 12.8 %all-to-all-start = ((f32[128,1,128]{2,1,0:T(1,128)}), f32[128,1,128]{2,1,0:T(1,128)S(1)}, u32[]{:S(2)}, u32[]{:S(2)}) async-start(f32[128,1,128]{2,1,0:T(1,128)} %get-tuple-element.54), calls=%async_computation | async-start | bytes 131072 | tf_op jit(solution)/shard_map/all_to_all | solution.py:1108
  44.6 0.0 collective-permute-done.6.near_e
  44.6 0.0 collective-permute-done.7.far_e
  44.6 4.9 %shard_map.110 = (f32[16,16,256]{2,1,0:T(8,128)S(1)}, f32[3,20,2,24,128]{4,3,2,1,0:T(8,128)S(1)}, f32[9,8,128]{2,1,0:T(8,128)S(1)}) custom-call(f32[16,16,256]{2,1,0:T(8,128)} %temp_far.5, s32[16,16,256]{2,1,0:T(8,128)} %mat_far.5, f32[2,104,128]{2,1,0:T(8,128)S(1)} %collective-permute-done.2.near_s, f32[2,104,128]{2,1,0:T(8,128)S(1)} %collective-permute-done.3.far_s, ...), custom_call_target="tpu_custom_call" | custom-call | bytes 8388608 | tf_op jit(solution)/shard_map/pallas_call | solution.py:971
  49.5 0.0 copy-start
  49.5 1.1 %copy-done = f32[3,20,2,24,128]{4,3,2,1,0:T(8,128)} copy-done((f32[3,20,2,24,128]{4,3,2,1,0:T(8,128)}, f32[3,20,2,24,128]{4,3,2,1,0:T(8,128)S(1)}, u32[]{:S(2)}) %copy-start) | copy-done | bytes 1474584
  50.6 0.7 %copy-done.1 = f32[16,16,256]{2,1,0:T(8,128)} copy-done((f32[16,16,256]{2,1,0:T(8,128)}, f32[16,16,256]{2,1,0:T(8,128)S(1)}, u32[]{:S(2)}) %copy-start.1) | copy-done | bytes 262168
  51.3 2.9 %all-to-all-done.arrived = f32[128,1,128]{2,1,0:T(1,128)S(1)} async-done(((f32[128,1,128]{2,1,0:T(1,128)}), f32[128,1,128]{2,1,0:T(1,128)S(1)}, u32[]{:S(2)}, u32[]{:S(2)}) %all-to-all-start) | async-done | bytes 65568 | tf_op jit(solution)/shard_map/all_to_all | solution.py:1108
  54.2 3.3 %shard_map.111 = f32[16,16,256]{2,1,0:T(8,128)} custom-call(f32[16,16,256]{2,1,0:T(8,128)} %copy-done.1, f32[3,20,2,24,128]{4,3,2,1,0:T(8,128)} %copy-done, f32[128,1,128]{2,1,0:T(1,128)S(1)} %all-to-all-done.arrived, f32[9,8,128]{2,1,0:T(8,128)S(1)} %get-tuple-element.55.all_cells), custom_call_target="tpu_custom_call" | custom-call | bytes 8388608 | tf_op jit(solution)/shard_map/pallas_call | solution.py:971
  (10 shorter events, 0.1 us)
Async XLA Ops:
  0.6 5.7 %copy-start.6 = (s32[1024]{0:T(1024)S(1)}, s32[1024]{0:T(1024)}, u32[]{:S(2)}) copy-start(s32[1024]{0:T(1024)} %param.15) | copy-start | bytes 12292
  3.5 12.8 %collective-permute-start = (f32[2,208,128]{2,1,0:T(8,128)}, f32[2,208,128]{2,1,0:T(8,128)S(1)}, u32[]{:S(2)}, u32[]{:S(2)}) collective-permute-start(f32[2,208,128]{2,1,0:T(8,128)} %get-tuple-element.31), channel_id=1, source_target_pairs={{0,1},{1,0},{2,3},{3,2},{4,5},{5,4},{6,7},{7,6},{8,9},{9,8},{10,11... | collective-permute-start | bytes 638984 | tf_op jit(solution)/shard_map/ppermute | solution.py:981
  5.7 10.6 %collective-permute-start.1 = (f32[2,208,128]{2,1,0:T(8,128)S(1)}, f32[2,208,128]{2,1,0:T(8,128)S(1)}, u32[]{:S(2)}, u32[]{:S(2)}) collective-permute-start(f32[2,208,128]{2,1,0:T(8,128)S(1)} %get-tuple-element.32), channel_id=1, source_target_pairs={{0,0},{1,2},{2,1},{3,4},{4,3},{5,6},{6,5},{7,7},{8,8},{9,10},{10,9... | collective-permute-start | bytes 638984 | tf_op jit(solution)/shard_map/ppermute | solution.py:981
  7.5 3.6 %collective-permute-start.2 = (f32[2,104,128]{2,1,0:T(8,128)S(1)}, f32[2,104,128]{2,1,0:T(8,128)S(1)}, u32[]{:S(2)}, u32[]{:S(2)}) collective-permute-start(f32[2,104,128]{2,1,0:T(8,128)S(1)} %get-tuple-element.34), channel_id=1, source_target_pairs={{0,8},{8,0},{16,24},{24,16},{32,40},{40,32},{48,56},{56,48},{64,72... | collective-permute-start | bytes 319496 | tf_op jit(solution)/shard_map/ppermute | solution.py:981
  8.5 7.8 %collective-permute-start.3 = (f32[2,104,128]{2,1,0:T(8,128)S(1)}, f32[2,104,128]{2,1,0:T(8,128)S(1)}, u32[]{:S(2)}, u32[]{:S(2)}) collective-permute-start(f32[2,104,128]{2,1,0:T(8,128)S(1)} %get-tuple-element.35), channel_id=1, source_target_pairs={{0,120},{8,16},{16,8},{24,32},{32,24},{40,48},{48,40},{56,64},{64,... | collective-permute-start | bytes 319496 | tf_op jit(solution)/shard_map/ppermute | solution.py:981
  17.4 11.3 %collective-permute-start.4 = (f32[2,264,128]{2,1,0:T(8,128)S(1)}, f32[2,264,128]{2,1,0:T(8,128)S(1)}, u32[]{:S(2)}, u32[]{:S(2)}) collective-permute-start(f32[2,264,128]{2,1,0:T(8,128)S(1)} %get-tuple-element.44), channel_id=1, source_target_pairs={{0,8},{8,0},{16,24},{24,16},{32,40},{40,32},{48,56},{56,48},{64,72... | collective-permute-start | bytes 811016 | tf_op jit(solution)/shard_map/ppermute | solution.py:981
  17.6 11.1 %collective-permute-start.5 = (f32[2,264,128]{2,1,0:T(8,128)S(1)}, f32[2,264,128]{2,1,0:T(8,128)S(1)}, u32[]{:S(2)}, u32[]{:S(2)}) collective-permute-start(f32[2,264,128]{2,1,0:T(8,128)S(1)} %get-tuple-element.45), channel_id=1, source_target_pairs={{0,120},{8,16},{16,8},{24,32},{32,24},{40,48},{48,40},{56,64},{64,... | collective-permute-start | bytes 811016 | tf_op jit(solution)/shard_map/ppermute | solution.py:981
  19.2 9.5 %copy-start.2 = (s32[512]{0:T(512)S(1)}, s32[512]{0:T(512)}, u32[]{:S(2)}) copy-start(s32[512]{0:T(512)} %param.11) | copy-start | bytes 6148
  19.2 9.5 %copy-start.3 = (f32[512]{0:T(512)S(1)}, f32[512]{0:T(512)}, u32[]{:S(2)}) copy-start(f32[512]{0:T(512)} %param.12) | copy-start | bytes 6148
  19.2 9.5 %copy-start.4 = (s32[512]{0:T(512)S(1)}, s32[512]{0:T(512)}, u32[]{:S(2)}) copy-start(s32[512]{0:T(512)} %param.13) | copy-start | bytes 6148
  19.2 9.5 %copy-start.5 = (s32[512]{0:T(512)S(1)}, s32[512]{0:T(512)}, u32[]{:S(2)}) copy-start(s32[512]{0:T(512)} %param.14) | copy-start | bytes 6148
  23.3 21.3 %collective-permute-start.6 = (f32[2,128,128]{2,1,0:T(8,128)S(1)}, f32[2,128,128]{2,1,0:T(8,128)S(1)}, u32[]{:S(2)}, u32[]{:S(2)}) collective-permute-start(f32[2,128,128]{2,1,0:T(8,128)S(1)} %get-tuple-element.50), channel_id=1, source_target_pairs={{0,1},{1,0},{2,3},{3,2},{4,5},{5,4},{6,7},{7,6},{8,9},{9,8},{10,11... | collective-permute-start | bytes 393224 | tf_op jit(solution)/shard_map/ppermute | solution.py:981
  28.0 16.7 %collective-permute-start.7 = (f32[2,128,128]{2,1,0:T(8,128)S(1)}, f32[2,128,128]{2,1,0:T(8,128)S(1)}, u32[]{:S(2)}, u32[]{:S(2)}) collective-permute-start(f32[2,128,128]{2,1,0:T(8,128)S(1)} %get-tuple-element.51), channel_id=1, source_target_pairs={{0,0},{1,2},{2,1},{3,4},{4,3},{5,6},{6,5},{7,7},{8,8},{9,10},{10,9... | collective-permute-start | bytes 393224 | tf_op jit(solution)/shard_map/ppermute | solution.py:981
  31.9 22.4 %all-to-all-start = ((f32[128,1,128]{2,1,0:T(1,128)}), f32[128,1,128]{2,1,0:T(1,128)S(1)}, u32[]{:S(2)}, u32[]{:S(2)}) async-start(f32[128,1,128]{2,1,0:T(1,128)} %get-tuple-element.54), calls=%async_computation | async-start | bytes 131072 | tf_op jit(solution)/shard_map/all_to_all | solution.py:1108
  49.5 1.1 %copy-start = (f32[3,20,2,24,128]{4,3,2,1,0:T(8,128)}, f32[3,20,2,24,128]{4,3,2,1,0:T(8,128)S(1)}, u32[]{:S(2)}) copy-start(f32[3,20,2,24,128]{4,3,2,1,0:T(8,128)S(1)} %get-tuple-element.53.links_far) | copy-start | bytes 4423684
  50.6 0.7 %copy-start.1 = (f32[16,16,256]{2,1,0:T(8,128)}, f32[16,16,256]{2,1,0:T(8,128)S(1)}, u32[]{:S(2)}) copy-start(f32[16,16,256]{2,1,0:T(8,128)S(1)} %get-tuple-element.52.swept_far) | copy-start | bytes 786436
